TPU v7x, 1024 devices: a whole 4x8x16 slice. The times are simulated.
1024 devices in a mesh: row: 64 (over x, z), col: 16 (over y, core).
Axes of the slice: x: 4, y: 8, z: 16, core: 2. Of those that a mesh axis runs over, the one named last changes fastest.
Arguments:
- start: float32 [131072, 64], P(('row', 'col')), may hold values from -6 to 6
- degrees: int32 [131072], P(('row', 'col')), may hold values from 16 to 64
- blocks: float32 [64, 16, 32, 128, 128], P('row', 'col'), may hold values from -0.09375 to 0.09375
- block_rows: int32 [64, 16, 32], P('row', 'col'), may hold values from 0 to 15
- block_cols: int32 [64, 16, 32], P('row', 'col'), may hold values from 0 to 63
- block_counts: int32 [64, 16], P('row', 'col'), may hold values from 1 to 32, as said below
Outputs:
- basis: float32 [131072, 64], P(('row', 'col'))
- ritz: float32 [64, 64], replicated
Inputs may be any that keep to these rules, and one draw needn't show every extreme that they name: `block_counts`: live slots of a tile; every draw has a tile with all 32 slots live, at a drawn place.
All inputs are finite; a program needn't handle non-finite values.
Results may differ from a plain program's by a relative error of at most 0.0003.
Values sent between devices are 32-bit elements; how exact they have to be, the bound alone decides.
No kernel may reach another device: no remote copies, remote signals or barrier semaphores. Data moves between devices by JAX's collectives and lax.ppermute only.
A program may use at most 32 MiB of HBM per device.

v0:
```python
import jax
import jax.numpy as jnp
from jax import lax
from jax.sharding import PartitionSpec as P


def apply_op(piece, scale, tile_blocks, tile_rows, tile_cols, tile_count):
    block_size = tile_blocks.shape[-1]
    slots = tile_blocks.shape[0]
    width = piece.shape[1]
    scaled = piece * scale[:, None]
    gathered = lax.all_gather(scaled, "row", axis=0, tiled=True)
    column_blocks = gathered.reshape(-1, block_size, width)
    picked = column_blocks[tile_cols]
    live = (jnp.arange(slots, dtype=jnp.int32) < tile_count).astype(jnp.float32)
    prod = jnp.einsum("bik,bkf->bif", tile_blocks, picked, precision=lax.Precision.HIGHEST)
    prod = prod * live[:, None, None]
    row_blocks = lax.axis_size("col") * piece.shape[0] // block_size
    onehot = (tile_rows[:, None] == jnp.arange(row_blocks, dtype=jnp.int32)[None, :]).astype(
        jnp.float32
    )
    partial_rows = jnp.einsum("bt,bif->tif", onehot, prod, precision=lax.Precision.HIGHEST)
    partial_rows = partial_rows.reshape(row_blocks * block_size, width)
    summed = lax.psum_scatter(partial_rows, "col", scatter_dimension=0, tiled=True)
    return summed * scale[:, None]


def from_lower(lower, filtered):
    return jax.scipy.linalg.solve_triangular(lower, filtered.T, lower=True).T


def local_gram(filtered):
    return jnp.dot(filtered.T, filtered, precision=lax.Precision.HIGHEST)


def summed_gram(filtered):
    return lax.psum(local_gram(filtered), ("row", "col"))


def shards(start, degrees, blocks, block_rows, block_cols, block_counts):
    nodes_all = start.shape[0] * lax.axis_size("row") * lax.axis_size("col")
    scale = jnp.sqrt(16.0 / degrees.astype(jnp.float32))
    tile_blocks = blocks.reshape(blocks.shape[2], blocks.shape[3], blocks.shape[4])
    tile_rows = block_rows.reshape(-1)
    tile_cols = block_cols.reshape(-1)
    tile_count = block_counts.reshape(())

    def operator(vectors):
        return apply_op(vectors, scale, tile_blocks, tile_rows, tile_cols, tile_count)

    gram_matrix = summed_gram(start)
    current = from_lower(jnp.linalg.cholesky(gram_matrix / nodes_all), start)
    first = operator(current)
    filtered = 2.0 * operator(first) - current
    gram_matrix = summed_gram(filtered)
    basis = from_lower(jnp.linalg.cholesky(gram_matrix / nodes_all), filtered)
    image = operator(basis)
    projected = jnp.dot(basis.T, image, precision=lax.Precision.HIGHEST)
    ritz = lax.psum(projected, ("row", "col")) / nodes_all
    return (basis, ritz)


def solution(mesh):
    return jax.shard_map(
        shards,
        mesh=mesh,
        in_specs=(
            P(("row", "col"), None),
            P(("row", "col")),
            P("row", "col", None, None, None),
            P("row", "col", None),
            P("row", "col", None),
            P("row", "col"),
        ),
        out_specs=(P(("row", "col"), None), P()),
        check_vma=False,
    )
```

profile of v0, /device:TPU:1, one launch (start us, length us, event | category | flops | bytes accessed | tf_op | source)
XLA Modules:
  0.0 1060.3 jit_solution(9722471756795477844)
XLA Ops:
  7.2 0.8 divide_sqrt_fusion
  8.0 1.0 fusion.40
  9.1 136.9 %psum.21 = f32[64,64]{0,1:T(8,128)S(1)} all-reduce(f32[64,64]{0,1:T(8,128)S(1)} %fusion.40), channel_id=1, replica_groups=mesh['row'=64,'col'=16] {'row','col'}, use_global_device_ids=true, to_apply=%region_0.0 | all-reduce | flops 4096 | bytes 32768 | tf_op jit(solution)/shard_map/psum | solution.py:37
  146.0 0.1 copy.15
  146.1 5.8 cholesky.44
  152.0 0.6 compare_reduce_fusion.1
  152.6 0.7 fusion.15
  153.3 4.9 custom-call.6
  158.2 1.6 broadcast_multiply_fusion.1
  159.8 0.0 reduce-scatter.4.cloned.1.call-start
  160.5 0.7 fusion.37
  161.2 120.3 %all-gather.4.cloned.1.call-done = f32[8192,64]{0,1:T(8,128)} async-done(((f32[128,64]{0,1:T(8,128)}), f32[8192,64]{0,1:T(8,128)}) %all-gather.4.cloned.1.call-update) | async-done | bytes 2097168 | tf_op jit(solution)/shard_map/all_gather | solution.py:12
  281.5 3.2 copy_bitcast_fusion.2
  284.7 2.2 gather_fusion
  286.9 4.1 fusion.4
  291.1 1.1 fusion.10
  292.1 1.0 copy.55
  293.1 0.0 all-gather.6.cloned.1.call-start
  293.2 68.9 %reduce-scatter.4.cloned.1.call-done = f32[128,64]{0,1:T(8,128)} async-done(((f32[2048,64]{0,1:T(8,128)}), f32[128,64]{0,1:T(8,128)}) %reduce-scatter.4.cloned.1.call-update) | async-done | bytes 32784 | tf_op jit(solution)/shard_map/reduce_scatter | solution.py:24
  362.0 1.4 multiply_multiply_fusion
  363.4 0.0 reduce-scatter.6.cloned.1.call-start
  363.5 136.4 %all-gather.6.cloned.1.call-done = f32[8192,64]{0,1:T(8,128)} async-done(((f32[128,64]{0,1:T(8,128)}), f32[8192,64]{0,1:T(8,128)}) %all-gather.6.cloned.1.call-update) | async-done | bytes 2097168 | tf_op jit(solution)/shard_map/all_gather | solution.py:12
  499.9 3.2 copy_bitcast_fusion.1
  503.1 2.2 gather_fusion.1
  505.3 4.1 fusion.2
  509.5 1.1 fusion.8
  510.6 1.0 copy.54
  511.6 68.9 %reduce-scatter.6.cloned.1.call-done = f32[128,64]{0,1:T(8,128)} async-done(((f32[2048,64]{0,1:T(8,128)}), f32[128,64]{0,1:T(8,128)}) %reduce-scatter.6.cloned.1.call-update) | async-done | bytes 32784 | tf_op jit(solution)/shard_map/reduce_scatter | solution.py:24
  580.5 1.0 fusion.29
  581.5 124.0 %psum.22 = f32[64,64]{0,1:T(8,128)S(1)} all-reduce(f32[64,64]{0,1:T(8,128)S(1)} %fusion.29), channel_id=1, replica_groups=mesh['row'=64,'col'=16] {'row','col'}, use_global_device_ids=true, to_apply=%region_5.0 | all-reduce | flops 4096 | bytes 32768 | tf_op jit(solution)/shard_map/psum | solution.py:37
  705.5 0.1 copy.19
  705.6 5.8 cholesky.55
  711.5 0.6 compare_reduce_fusion
  712.1 0.7 fusion.16
  712.8 4.9 custom-call.7
  717.7 1.0 fusion.17
  718.7 0.6 broadcast_multiply_fusion
  719.3 0.0 reduce-scatter.8.cloned.1.call-start
  719.4 128.1 %all-gather.8.cloned.1.call-done = f32[8192,64]{0,1:T(8,128)} async-done(((f32[128,64]{0,1:T(8,128)}), f32[8192,64]{0,1:T(8,128)}) %all-gather.8.cloned.1.call-update) | async-done | bytes 2097168 | tf_op jit(solution)/shard_map/all_gather | solution.py:12
  847.5 3.2 copy_bitcast_fusion
  850.7 2.2 gather_fusion.2
  852.9 4.1 fusion
  857.0 1.1 fusion.6
  858.1 1.0 copy.53
  859.1 68.9 %reduce-scatter.8.cloned.1.call-done = f32[128,64]{0,1:T(8,128)} async-done(((f32[2048,64]{0,1:T(8,128)}), f32[128,64]{0,1:T(8,128)}) %reduce-scatter.8.cloned.1.call-update) | async-done | bytes 32784 | tf_op jit(solution)/shard_map/reduce_scatter | solution.py:24
  928.0 0.9 fusion.26
  929.0 123.8 %psum.23 = f32[64,64]{0,1:T(8,128)S(1)} all-reduce(f32[64,64]{0,1:T(8,128)S(1)} %fusion.26), channel_id=1, replica_groups=mesh['row'=64,'col'=16] {'row','col'}, use_global_device_ids=true, to_apply=%region_7.10 | all-reduce | flops 4096 | bytes 32768 | tf_op jit(solution)/shard_map/psum | solution.py:59
  1052.8 0.7 copy.22
  (23 shorter events, 0.3 us)
Async XLA Ops:
  7.2 279.7 %copy-start = (f32[1,1,32,128,128]{4,3,2,1,0:T(8,128)S(1)}, f32[1,1,32,128,128]{4,3,2,1,0:T(8,128)}, u32[]{:S(2)}) copy-start(f32[1,1,32,128,128]{4,3,2,1,0:T(8,128)} %param.11) | copy-start | bytes 6291460
  7.2 274.3 %all-gather.4.cloned.1.call-start = ((), (), s32[]{:S(2)}) async-start(), calls=%async_computation.3 | async-start | bytes 2129920 | tf_op jit(solution)/shard_map/all_gather | solution.py:12
  159.8 202.2 %reduce-scatter.4.cloned.1.call-start = ((), (), s32[]{:S(2)}) async-start(), calls=%async_computation.4 | async-start | bytes 557056 | tf_op jit(solution)/shard_map/reduce_scatter | solution.py:24
  286.9 4.2 copy-start.2
  293.1 206.8 %all-gather.6.cloned.1.call-start = ((), (), s32[]{:S(2)}) async-start(), calls=%async_computation.5 | async-start | bytes 2129920 | tf_op jit(solution)/shard_map/all_gather | solution.py:12
  363.4 217.0 %reduce-scatter.6.cloned.1.call-start = ((), (), s32[]{:S(2)}) async-start(), calls=%async_computation.6 | async-start | bytes 557056 | tf_op jit(solution)/shard_map/reduce_scatter | solution.py:24
  511.5 336.0 %all-gather.8.cloned.1.call-start = ((), (), s32[]{:S(2)}) async-start(), calls=%async_computation.7 | async-start | bytes 2129920 | tf_op jit(solution)/shard_map/all_gather | solution.py:12
  718.7 209.4 %copy-start.1 = (f32[64,128]{1,0:T(8,128)}, f32[64,128]{1,0:T(8,128)S(1)}, u32[]{:S(2)}) copy-start(f32[64,128]{1,0:T(8,128)S(1)} %fusion.17) | copy-start | bytes 98308
  719.3 208.7 %reduce-scatter.8.cloned.1.call-start = ((), (), s32[]{:S(2)}) async-start(), calls=%async_computation.8 | async-start | bytes 557056 | tf_op jit(solution)/shard_map/reduce_scatter | solution.py:24
Sparse Core Ops, SparseCore 0:
  160.0 121.4 all-gather.3
  293.2 68.7 reduce-scatter.3
  367.4 132.4 all-gather.5
  511.7 68.7 reduce-scatter.5
  719.5 128.0 all-gather.7
  859.2 68.7 reduce-scatter.7
where the time goes:
time: 1060 us
  waiting for transfers between devices  592 us (56%)
  blocking collectives  385 us (36%)
  other arithmetic  27.6 us (3%)
  matrix products  21.3 us (2%)
  local copies, waits for them, and re-layouts  19.8 us (2%)
  between operations  15 us (1%)
    all_gather x3, waiting for transfers between devices, apply_op(): gathered = lax.all_gather(scaled, 'row', axis=0, tiled=True)  385 us
    psum x2, blocking collectives, summed_gram(): return lax.psum(local_gram(filtered), ('row', 'col'))  261 us
    reduce_scatter x3, waiting for transfers between devices, apply_op(): lax.psum_scatter(partial_rows, 'col', scatter_dimension=0, tiled=True)  207 us
    psum x1, blocking collectives, shards(): ritz = lax.psum(projected, ('row', 'col')) / nodes_all  124 us
  transfers between devices with their start and end apart: 6, of which 6 were waited for; matrix products, arithmetic and copies ran while one was open for 0% of the time, Pallas kernels for 0%

commit v1 on v0

v1 whole, which is shorter than its diff:
```python
import functools

import jax
import jax.numpy as jnp
from jax import lax
from jax.experimental import pallas as pl
from jax.experimental.pallas import tpu as pltpu
from jax.sharding import Mesh, PartitionSpec as P

HIGHEST = lax.Precision.HIGHEST
AXES = ("x", "z", "y", "core")
CONTRACT_LAST = (((1,), (1,)), ((), ()))


def exchange(chunks, axes):
    return lax.all_to_all(chunks, axes, 0, 0, tiled=True)


def to_all(value, axes):
    copies = lax.axis_size(axes)
    return exchange(jnp.broadcast_to(value[None], (copies, *value.shape)), axes)


def tile_kernel(rows_ref, cols_ref, count_ref, blocks_ref, gathered_ref, out_ref):
    out_ref[...] = jnp.zeros_like(out_ref)
    count = count_ref[0]
    for slot in range(blocks_ref.shape[0]):
        live = (slot < count).astype(jnp.float32)
        product = lax.dot_general(
            gathered_ref[cols_ref[slot]],
            blocks_ref[slot],
            CONTRACT_LAST,
            precision=HIGHEST,
            preferred_element_type=jnp.float32,
        )
        out_ref[rows_ref[slot]] += product * live


def tile_product(gathered, blocks, rows, cols, count, row_blocks):
    smem = pl.BlockSpec(memory_space=pltpu.SMEM)
    vmem = pl.BlockSpec(memory_space=pltpu.VMEM)
    width, nodes = gathered.shape[1:]
    return pl.pallas_call(
        tile_kernel,
        out_shape=jax.ShapeDtypeStruct((row_blocks, width, nodes), jnp.float32),
        in_specs=[smem, smem, smem, vmem, vmem],
        out_specs=vmem,
        compiler_params=pltpu.CompilerParams(vmem_limit_bytes=24 * 2**20),
    )(rows, cols, count, blocks, gathered)


def gram(left, right):
    return lax.dot_general(left, right, CONTRACT_LAST, precision=HIGHEST)


def matmul(left, right):
    return jnp.dot(left, right, precision=HIGHEST)


def inverse_factor(gram_matrix):
    lower = jnp.linalg.cholesky(gram_matrix)
    eye = jnp.eye(gram_matrix.shape[0], dtype=gram_matrix.dtype)
    return jax.scipy.linalg.solve_triangular(lower, eye, lower=True)


def fold(square):
    half = square.shape[0] // 2
    return jnp.concatenate([square[:half], square[half:]], axis=1)


def unfold(folded):
    half = folded.shape[1] // 2
    return jnp.concatenate([folded[:, :half], folded[:, half:]], axis=0)


def shards(start, degrees, blocks, block_rows, block_cols, block_counts):
    row_devices = lax.axis_size(("x", "z"))
    col_devices = lax.axis_size(("y", "core"))
    nodes, width = start.shape
    nodes_all = nodes * row_devices * col_devices
    scale = jnp.sqrt(16.0 / degrees.astype(jnp.float32))[None, :]
    tile_blocks = blocks.reshape(blocks.shape[2:])
    rows = block_rows.reshape(-1)
    y_devices = lax.axis_size("y")
    rows = (rows % 2) * y_devices + rows // 2
    cols = block_cols.reshape(-1)
    count = block_counts.reshape(-1)

    def gather_rows(vectors, extra=None):
        scaled = vectors * scale
        if extra is not None:
            scaled = jnp.concatenate([scaled, fold(extra)], axis=0)
        along_z = lax.all_gather(scaled, "z", axis=0, tiled=False)
        pieces = along_z[:, :width]
        if extra is None:
            everywhere = to_all(pieces, "x")
            return everywhere.reshape(row_devices, width, nodes), None
        summed = along_z[:, width:].sum(0)
        packed = jnp.concatenate([pieces.reshape(-1, nodes), summed], axis=0)
        everywhere = to_all(packed, "x").reshape(lax.axis_size("x"), -1, nodes)
        cut = pieces.shape[0] * width
        return everywhere[:, :cut].reshape(row_devices, width, nodes), everywhere[:, cut:].sum(0)

    def product(gathered):
        return tile_product(gathered, tile_blocks, rows, cols, count, col_devices)

    def reduce_cols(partial, extra=None):
        halves = partial.reshape(2, -1, nodes)
        if extra is not None:
            halves = jnp.concatenate([halves, jnp.broadcast_to(extra[None], (2, *extra.shape))], axis=1)
        halves = exchange(halves, "core").sum(0)
        cut = y_devices * width
        chunks = halves[:cut].reshape(y_devices, width, nodes)
        if extra is not None:
            rest = jnp.broadcast_to(halves[cut:][None], (y_devices, *extra.shape))
            chunks = jnp.concatenate([chunks, rest], axis=1)
        done = exchange(chunks, "y").sum(0)
        if extra is None:
            return done * scale, None
        return done[:width] * scale, unfold(done[width:])

    first = start.T
    gathered, row_sum = gather_rows(first, gram(first, first))
    once, gram_first = reduce_cols(product(gathered), row_sum)
    gathered, _ = gather_rows(once)
    twice, _ = reduce_cols(product(gathered))
    filtered = matmul(inverse_factor(gram_first / nodes_all), 2.0 * twice - first)

    gathered, _ = gather_rows(filtered)
    own_rows = lax.all_gather(filtered * scale, ("y", "core"), axis=0, tiled=False)
    own_rows = own_rows.reshape(y_devices, 2, width, nodes).swapaxes(0, 1).reshape(col_devices, width, nodes)
    partial = product(gathered)
    projected = jnp.einsum("rfi,rgi->fg", own_rows, partial, precision=HIGHEST)
    both = jnp.concatenate([gram(filtered, filtered), projected], axis=1)
    both = exchange(both.reshape(col_devices, -1, 2 * width), ("y", "core")).sum(0)
    both = to_all(both, ("x", "z")).reshape(row_devices, -1, 2 * width).sum(0)
    both = to_all(both, ("y", "core")).reshape(width, 2 * width) / nodes_all
    inverse = inverse_factor(both[:, :width])
    basis = matmul(inverse, filtered)
    ritz = matmul(matmul(inverse, both[:, width:]), inverse.T)
    return (basis.T, ritz)


def solution(mesh):
    sizes = (4, 16, 8, 2)
    return jax.shard_map(
        shards,
        mesh=Mesh(mesh.devices.reshape(sizes), AXES),
        in_specs=(
            P(AXES, None),
            P(AXES),
            P(("x", "z"), ("y", "core"), None, None, None),
            P(("x", "z"), ("y", "core"), None),
            P(("x", "z"), ("y", "core"), None),
            P(("x", "z"), ("y", "core")),
        ),
        out_specs=(P(AXES, None), P()),
        check_vma=False,
    )
```

time: 1060 us -> 313 us (0.30)
  waiting for transfers between devices: 592 us -> 35.5 us
  blocking collectives: 385 us -> 203 us
  matrix products: 21.3 us -> 4.25 us
  starting transfers between devices: 0.25 us -> 16.9 us
  Pallas kernels: 0 us -> 16 us
  between operations: 15 us -> 1.62 us
  local copies, waits for them, and re-layouts: 19.8 us -> 6.89 us
    all_gather x3 -> x0, waiting for transfers between devices: 385 us -> none  [apply_op(): gathered = lax.all_gather(scaled, 'row', axis=0, tiled=True)]
    psum x3 -> x0, blocking collectives: 385 us -> none  [the longest x2 261 us: summed_gram(): return lax.psum(local_gram(filtered), ('row', 'col'))]
    reduce_scatter x3 -> x0, waiting for transfers between devices: 207 us -> none  [apply_op(): lax.psum_scatter(partial_rows, 'col', scatter_dimension=0, tiled=True)]
    all_gather x0 -> x4, blocking collectives: none -> 110 us  [the longest x3 86.6 us: gather_rows(): along_z = lax.all_gather(scaled, 'z', axis=0, tiled=False)]
    all_to_all x0 -> x6, blocking collectives: none -> 92.9 us  [exchange(): return lax.all_to_all(chunks, axes, 0, 0, tiled=True)]
    all_to_all x0 -> x4, waiting for transfers between devices: none -> 35.5 us  [exchange(): return lax.all_to_all(chunks, axes, 0, 0, tiled=True)]
    all_to_all x0 -> x4, starting transfers between devices: none -> 16.9 us  [exchange(): return lax.all_to_all(chunks, axes, 0, 0, tiled=True)]
    pallas_call x0 -> x3, Pallas kernels: none -> 16 us  [tile_product(): pl.pallas_call(tile_kernel, out_shape=jax.ShapeDtypeStruct((row_blocks, w...]
  transfers between devices with their start and end apart: 6 -> 4, of which waited for: 6 -> 3; matrix products, arithmetic and copies ran while one was open for 0% -> 4% of each run, Pallas kernels for 0% -> 0%
where the time goes in v1:
time: 313 us; the launch traced here: 312 us
  blocking collectives  203 us (65%)
  waiting for transfers between devices  35.5 us (11%)
  other arithmetic  27.8 us (9%)
  starting transfers between devices  16.9 us (5%)
  Pallas kernels  16 us (5%)
  local copies, waits for them, and re-layouts  6.89 us (2%)
  matrix products  4.25 us (1%)
    all_to_all x6, blocking collectives, exchange(): return lax.all_to_all(chunks, axes, 0, 0, tiled=True)  92.9 us
    all_gather x3, blocking collectives, gather_rows(): along_z = lax.all_gather(scaled, 'z', axis=0, tiled=False)  86.6 us
    all_to_all x4, waiting for transfers between devices, exchange(): return lax.all_to_all(chunks, axes, 0, 0, tiled=True)  35.5 us
    all_gather x1, blocking collectives, shards(): lax.all_gather(filtered * scale, ('y', 'core'), axis=0, tiled=False)  23.6 us
    all_to_all x4, starting transfers between devices, exchange(): return lax.all_to_all(chunks, axes, 0, 0, tiled=True)  16.9 us
    pallas_call x3, Pallas kernels, tile_product(): pl.pallas_call(tile_kernel, out_shape=jax.ShapeDtypeStruct((row_blocks, w...  16 us
    another operation x6, other arithmetic, inverse_factor(): lower = jnp.linalg.cholesky(gram_matrix)  13 us
    another operation x4, other arithmetic, inverse_factor(): return jax.scipy.linalg.solve_triangular(lower, eye, lower=True)  11.1 us
  transfers between devices with their start and end apart: 4, of which 3 were waited for; matrix products, arithmetic and copies ran while one was open for 4% of the time, Pallas kernels for 0%

profile of v1, /device:TPU:1, one launch (start us, length us, event | category | flops | bytes accessed | tf_op | source)
XLA Modules:
  0.0 312.1 jit_solution(16643893446251608395)
XLA Ops:
  0.6 0.7 divide_sqrt_fusion
  1.3 1.0 fusion.23
  2.3 0.8 bitcast_multiply_fusion
  3.2 40.7 %all-gather = f32[1536,128]{1,0:T(8,128)S(1)} all-gather(f32[96,128]{1,0:T(8,128)S(1)} %maximum_maximum_fusion), channel_id=2, replica_groups=mesh['x'=4,'z'=16,'y'=8,'core'=2] {'z'}, dimensions={0}, use_global_device_ids=true | all-gather | bytes 835584 | tf_op jit(solution)/shard_map/all_gather | solution.py:93
  43.9 1.5 broadcast_in_dim.14
  45.4 4.6 %all-to-all-start = ((f32[4,1056,128]{2,1,0:T(8,128)}), f32[4,1056,128]{2,1,0:T(8,128)}, u32[]{:S(2)}, u32[]{:S(2)}) async-start(f32[4,1056,128]{2,1,0:T(8,128)} %broadcast_in_dim.14), calls=%async_computation | async-start | bytes 4325376 | tf_op jit(solution)/shard_map/all_to_all | solution.py:16
  50.7 18.4 %all-to-all-done = f32[4,1056,128]{2,1,0:T(8,128)} async-done(((f32[4,1056,128]{2,1,0:T(8,128)}), f32[4,1056,128]{2,1,0:T(8,128)}, u32[]{:S(2)}, u32[]{:S(2)}) %all-to-all-start) | async-done | bytes 2162720 | tf_op jit(solution)/shard_map/all_to_all | solution.py:16
  69.1 1.7 slice.67
  70.9 4.6 %shard_map.77 = f32[16,64,128]{2,1,0:T(8,128)S(1)} custom-call(s32[32]{0:T(128)S(1)} %fusion.19.rows_ref, s32[32]{0:T(128)S(1)} %bitcast.81, s32[1]{0:T(128)} %bitcast.72.count_ref, f32[32,128,128]{2,1,0:T(8,128)S(1)} %bitcast.75, f32[64,64,128]{2,1,0:T(8,128)S(1)} %bitcast.78), custom_call_target="tpu_custom_call" | custom-call | tf_op jit(solution)/shard_map/pallas_call | solution.py:43
  75.5 0.9 slice_reduce_fusion.1
  76.4 12.7 %all_to_all.50 = f32[2,544,128]{2,1,0:T(8,128)S(1)} all-to-all(f32[2,544,128]{2,1,0:T(8,128)S(1)} %pad_maximum_fusion), channel_id=1, replica_groups=mesh['x'=4,'z'=16,'y'=8,'core'=2] {'core'}, dimensions={0} | all-to-all | bytes 1114112 | tf_op jit(solution)/shard_map/all_to_all | solution.py:16
  89.3 20.5 %all_to_all.51 = f32[8,96,128]{2,1,0:T(8,128)S(1)} all-to-all(f32[8,96,128]{2,1,0:T(8,128)S(1)} %pad_maximum_fusion.2), channel_id=1, replica_groups=mesh['x'=4,'z'=16,'y'=8,'core'=2] {'y'}, dimensions={0} | all-to-all | bytes 786432 | tf_op jit(solution)/shard_map/all_to_all | solution.py:16
  109.8 22.2 %all-gather.1 = f32[1024,128]{1,0:T(8,128)S(1)} all-gather(f32[64,128]{1,0:T(8,128)S(1)} %fusion.8), channel_id=3, replica_groups=mesh['x'=4,'z'=16,'y'=8,'core'=2] {'z'}, dimensions={0}, use_global_device_ids=true | all-gather | bytes 557056 | tf_op jit(solution)/shard_map/all_gather | solution.py:93
  132.0 1.6 broadcast_in_dim.17
  133.6 4.4 %all-to-all-start.3 = ((f32[4,16,64,128]{3,2,1,0:T(8,128)}), f32[4,16,64,128]{3,2,1,0:T(8,128)}, u32[]{:S(2)}, u32[]{:S(2)}) async-start(f32[4,16,64,128]{3,2,1,0:T(8,128)} %broadcast_in_dim.17), calls=%async_computation.3 | async-start | bytes 4194304 | tf_op jit(solution)/shard_map/all_to_all | solution.py:16
  138.1 0.1 copy.56
  138.2 0.1 maximum_multiply_fusion
  138.4 0.1 fusion.12
  138.5 5.8 %cholesky.44 = f32[64,64]{1,0:T(8,128)S(1)} custom-call(f32[64,64]{1,0:T(8,128)S(1)} %fusion.12), custom_call_target="Cholesky" | custom-call | tf_op jit(solution)/shard_map/jit(cholesky)/cholesky | solution.py:61
  144.4 11.3 %all-to-all-done.3 = f32[4,16,64,128]{3,2,1,0:T(8,128)} async-done(((f32[4,16,64,128]{3,2,1,0:T(8,128)}), f32[4,16,64,128]{3,2,1,0:T(8,128)}, u32[]{:S(2)}, u32[]{:S(2)}) %all-to-all-start.3) | async-done | bytes 2097184 | tf_op jit(solution)/shard_map/all_to_all | solution.py:16
  155.6 5.7 %shard_map.78 = f32[16,64,128]{2,1,0:T(8,128)S(1)} custom-call(s32[32]{0:T(128)S(1)} %fusion.19.rows_ref, s32[32]{0:T(128)S(1)} %bitcast.82, s32[1]{0:T(128)} %bitcast.73.count_ref, f32[32,128,128]{2,1,0:T(8,128)S(1)} %bitcast.76, f32[64,64,128]{2,1,0:T(8,128)} %bitcast.14.gathered_ref), custom_call_target="tpu_custom_call" | custom-call | tf_op jit(solution)/shard_map/pallas_call | solution.py:43
  161.4 13.5 %all_to_all.52 = f32[2,512,128]{2,1,0:T(8,128)S(1)} all-to-all(f32[2,512,128]{2,1,0:T(8,128)S(1)} %bitcast.80), channel_id=1, replica_groups=mesh['x'=4,'z'=16,'y'=8,'core'=2] {'core'}, dimensions={0} | all-to-all | bytes 1048576 | tf_op jit(solution)/shard_map/all_to_all | solution.py:16
  174.8 0.7 reduce_sum.76
  175.6 3.4 %all-to-all-start.5 = ((f32[8,64,128]{2,1,0:T(8,128)}), f32[8,64,128]{2,1,0:T(8,128)S(1)}, u32[]{:S(2)}, u32[]{:S(2)}) async-start(f32[8,64,128]{2,1,0:T(8,128)} %bitcast.16), calls=%async_computation.5 | async-start | bytes 524288 | tf_op jit(solution)/shard_map/all_to_all | solution.py:16
  179.0 0.6 compare_reduce_fusion.1
  179.6 0.7 fusion.4
  180.3 4.9 %custom-call.6 = f32[1,64,64]{1,2,0:T(8,128)S(1)} custom-call(f32[1,64,64]{2,1,0:T(8,128)S(1)} %fusion.4), custom_call_target="InvertDiagBlocksLowerTriangular" | custom-call | tf_op jit(solution)/shard_map/jit(_solve_triangular)/triangular_solve | solution.py:63
  185.2 0.3 fusion.2
  185.4 5.8 %all-to-all-done.5 = f32[8,64,128]{2,1,0:T(8,128)S(1)} async-done(((f32[8,64,128]{2,1,0:T(8,128)}), f32[8,64,128]{2,1,0:T(8,128)S(1)}, u32[]{:S(2)}, u32[]{:S(2)}) %all-to-all-start.5) | async-done | bytes 262176 | tf_op jit(solution)/shard_map/all_to_all | solution.py:16
  191.3 0.2 broadcast_multiply_fusion.1
  191.5 23.8 %all-gather.3 = f32[1024,128]{1,0:T(8,128)S(1)} all-gather(f32[64,128]{1,0:T(8,128)S(1)} %get-tuple-element.8), channel_id=5, replica_groups=mesh['x'=4,'z'=16,'y'=8,'core'=2] {'z'}, dimensions={0}, use_global_device_ids=true | all-gather | bytes 557056 | tf_op jit(solution)/shard_map/all_gather | solution.py:93
  215.2 1.6 broadcast_in_dim.19
  216.8 4.4 %all-to-all-start.6 = ((f32[4,16,64,128]{3,2,1,0:T(8,128)}), f32[4,16,64,128]{3,2,1,0:T(8,128)}, u32[]{:S(2)}, u32[]{:S(2)}) async-start(f32[4,16,64,128]{3,2,1,0:T(8,128)} %broadcast_in_dim.19), calls=%async_computation.6 | async-start | bytes 4194304 | tf_op jit(solution)/shard_map/all_to_all | solution.py:16
  221.2 23.6 %all-gather.2 = f32[1024,128]{1,0:T(8,128)S(1)} all-gather(f32[64,128]{1,0:T(8,128)S(1)} %get-tuple-element.8), channel_id=4, replica_groups=mesh['x'=4,'z'=16,'y'=8,'core'=2] {'y','core'}, dimensions={0}, use_global_device_ids=true | all-gather | bytes 557056 | tf_op jit(solution)/shard_map/all_gather | solution.py:130
  244.8 0.2 fusion.24
  245.0 5.7 %shard_map.79 = f32[16,64,128]{2,1,0:T(8,128)S(1)} custom-call(s32[32]{0:T(128)S(1)} %fusion.19.rows_ref, s32[32]{0:T(128)S(1)} %bitcast.83, s32[1]{0:T(128)} %bitcast.74.count_ref, f32[32,128,128]{2,1,0:T(8,128)S(1)} %bitcast.77, f32[64,64,128]{2,1,0:T(8,128)} %bitcast.21.gathered_ref), custom_call_target="tpu_custom_call" | custom-call | tf_op jit(solution)/shard_map/pallas_call | solution.py:43
  250.7 0.6 convolution_bitcast_fusion
  251.4 13.4 %all_to_all.53 = f32[16,4,128]{2,1,0:T(4,128)S(1)} all-to-all(f32[16,4,128]{2,1,0:T(4,128)S(1)} %bitcast.95), channel_id=1, replica_groups=mesh['x'=4,'z'=16,'y'=8,'core'=2] {'y','core'}, dimensions={0} | all-to-all | bytes 65536 | tf_op jit(solution)/shard_map/all_to_all | solution.py:16
  264.8 20.7 %all_to_all.54 = f32[64,4,128]{2,1,0:T(4,128)S(1)} all-to-all(f32[64,4,128]{2,1,0:T(4,128)S(1)} %broadcast_in_dim.20), channel_id=1, replica_groups=mesh['x'=4,'z'=16,'y'=8,'core'=2] {'x','z'}, dimensions={0} | all-to-all | bytes 262144 | tf_op jit(solution)/shard_map/all_to_all | solution.py:16
  285.6 12.2 %all_to_all.55 = f32[16,4,128]{2,1,0:T(4,128)S(1)} all-to-all(f32[16,4,128]{2,1,0:T(4,128)S(1)} %broadcast_in_dim.21), channel_id=1, replica_groups=mesh['x'=4,'z'=16,'y'=8,'core'=2] {'y','core'}, dimensions={0} | all-to-all | bytes 65536 | tf_op jit(solution)/shard_map/all_to_all | solution.py:16
  297.9 5.8 %cholesky.55 = f32[64,64]{1,0:T(8,128)S(1)} custom-call(f32[64,64]{1,0:T(8,128)S(1)} %fusion.10), custom_call_target="Cholesky" | custom-call | tf_op jit(solution)/shard_map/jit(cholesky)/cholesky | solution.py:61
  303.8 0.6 compare_reduce_fusion
  304.4 0.7 fusion.5
  305.1 4.9 %custom-call.7 = f32[1,64,64]{1,2,0:T(8,128)S(1)} custom-call(f32[1,64,64]{2,1,0:T(8,128)S(1)} %fusion.5), custom_call_target="InvertDiagBlocksLowerTriangular" | custom-call | tf_op jit(solution)/shard_map/jit(_solve_triangular)/triangular_solve | solution.py:63
  310.0 0.3 fusion
  310.2 0.8 fusion.25
  311.0 0.2 fusion.6
  311.2 0.8 fusion.26
  (39 shorter events, 1.0 us)
Async XLA Ops:
  45.4 5.2 %copy-start.3 = (s32[1,1,32]{2,1,0:T(1,128)S(1)}, s32[1,1,32]{2,1,0:T(1,128)}, u32[]{:S(2)}) copy-start(s32[1,1,32]{2,1,0:T(1,128)} %param.12) | copy-start | bytes 388
  45.4 23.7 %all-to-all-start = ((f32[4,1056,128]{2,1,0:T(8,128)}), f32[4,1056,128]{2,1,0:T(8,128)}, u32[]{:S(2)}, u32[]{:S(2)}) async-start(f32[4,1056,128]{2,1,0:T(8,128)} %broadcast_in_dim.14), calls=%async_computation | async-start | bytes 4325376 | tf_op jit(solution)/shard_map/all_to_all | solution.py:16
  50.7 20.2 %copy-start = (f32[1,1,32,128,128]{4,3,2,1,0:T(8,128)S(1)}, f32[1,1,32,128,128]{4,3,2,1,0:T(8,128)}, u32[]{:S(2)}) copy-start(f32[1,1,32,128,128]{4,3,2,1,0:T(8,128)} %param.11) | copy-start | bytes 6291460
  50.7 20.2 %copy-start.1 = (s32[1,1,32]{2,1,0:T(1,128)S(1)}, s32[1,1,32]{2,1,0:T(1,128)}, u32[]{:S(2)}) copy-start(s32[1,1,32]{2,1,0:T(1,128)} %param.13) | copy-start | bytes 388
  133.6 22.1 %all-to-all-start.3 = ((f32[4,16,64,128]{3,2,1,0:T(8,128)}), f32[4,16,64,128]{3,2,1,0:T(8,128)}, u32[]{:S(2)}, u32[]{:S(2)}) async-start(f32[4,16,64,128]{3,2,1,0:T(8,128)} %broadcast_in_dim.17), calls=%async_computation.3 | async-start | bytes 4194304 | tf_op jit(solution)/shard_map/all_to_all | solution.py:16
  161.3 29.9 %copy-start.2 = (f32[128,64]{0,1:T(8,128)S(1)}, f32[128,64]{0,1:T(8,128)}, u32[]{:S(2)}) copy-start(f32[128,64]{0,1:T(8,128)} %param.9) | copy-start | bytes 98308
  175.6 15.7 %all-to-all-start.5 = ((f32[8,64,128]{2,1,0:T(8,128)}), f32[8,64,128]{2,1,0:T(8,128)S(1)}, u32[]{:S(2)}, u32[]{:S(2)}) async-start(f32[8,64,128]{2,1,0:T(8,128)} %bitcast.16), calls=%async_computation.5 | async-start | bytes 524288 | tf_op jit(solution)/shard_map/all_to_all | solution.py:16
  216.8 28.2 %all-to-all-start.6 = ((f32[4,16,64,128]{3,2,1,0:T(8,128)}), f32[4,16,64,128]{3,2,1,0:T(8,128)}, u32[]{:S(2)}, u32[]{:S(2)}) async-start(f32[4,16,64,128]{3,2,1,0:T(8,128)} %broadcast_in_dim.19), calls=%async_computation.6 | async-start | bytes 4194304 | tf_op jit(solution)/shard_map/all_to_all | solution.py:16

commit v2 on v1

v2 whole, which is shorter than its diff:
```python
import functools

import jax
import jax.numpy as jnp
from jax import lax
from jax.experimental import pallas as pl
from jax.experimental.pallas import tpu as pltpu
from jax.sharding import Mesh, PartitionSpec as P

HIGHEST = lax.Precision.HIGHEST
AXES = ("x", "z", "y", "core")
CONTRACT_LAST = (((1,), (1,)), ((), ()))


def exchange(chunks, axes):
    return lax.all_to_all(chunks, axes, 0, 0, tiled=True)


def to_all(value, axes):
    copies = lax.axis_size(axes)
    return exchange(jnp.broadcast_to(value[None], (copies, *value.shape)), axes)


def split(value):
    high = value.astype(jnp.bfloat16)
    return high, (value - high.astype(jnp.float32)).astype(jnp.bfloat16)


def dot_pieces(left, right):
    return lax.dot_general(left, right, CONTRACT_LAST, preferred_element_type=jnp.float32)


def add_slots(rows_ref, cols_ref, count_ref, blocks_ref, gathered_ref, sums_ref):
    sums_ref[...] = jnp.zeros_like(sums_ref)
    count = count_ref[0]
    width = sums_ref.shape[1]
    for slot in range(blocks_ref.shape[0]):
        live = (slot < count).astype(jnp.float32)
        high, low = split(gathered_ref[cols_ref[slot]] * live)
        block_high, block_low = split(blocks_ref[slot])
        both = dot_pieces(jnp.concatenate([high, low], axis=0), block_high)
        sums_ref[rows_ref[slot]] += both[:width] + both[width:] + dot_pieces(high, block_low)


def tile_kernel(rows_ref, cols_ref, count_ref, blocks_ref, gathered_ref, out_ref):
    add_slots(rows_ref, cols_ref, count_ref, blocks_ref, gathered_ref, out_ref)


def tile_rider_kernel(rows_ref, cols_ref, count_ref, blocks_ref, gathered_ref, rider_ref, out_ref, rider_out_ref):
    add_slots(rows_ref, cols_ref, count_ref, blocks_ref, gathered_ref, out_ref)
    rider_out_ref[...] = jnp.sum(rider_ref[...], axis=0)


def project_kernel(rows_ref, cols_ref, count_ref, blocks_ref, gathered_ref, own_ref, out_ref, rider_out_ref, sums_ref):
    add_slots(rows_ref, cols_ref, count_ref, blocks_ref, gathered_ref, sums_ref)
    row_blocks, width, _ = sums_ref.shape
    half = row_blocks // 2
    total = jnp.zeros((width, width), jnp.float32)
    rider = jnp.zeros(rider_out_ref.shape, jnp.float32)
    for piece in range(row_blocks):
        total += lax.dot_general(
            own_ref[piece, :width],
            sums_ref[(piece % 2) * half + piece // 2],
            CONTRACT_LAST,
            precision=HIGHEST,
            preferred_element_type=jnp.float32,
        )
        rider += own_ref[piece, width:]
    out_ref[...] = fold(total)
    rider_out_ref[...] = rider


def sum_kernel(chunks_ref, rider_ref, copies_ref, rider_out_ref):
    copies_ref[...] = jnp.broadcast_to(jnp.sum(chunks_ref[...], axis=0)[None], copies_ref.shape)
    rider_out_ref[...] = jnp.sum(rider_ref[...], axis=0, keepdims=True)


def inverse_kernel(nodes_all, folded_ref, out_ref):
    size = out_ref.shape[0]
    shape = (size, 2 * size)
    gram_matrix = unfold(jnp.sum(folded_ref[...], axis=0)) / nodes_all
    row_of = lax.broadcasted_iota(jnp.int32, shape, 0)
    eye = (lax.broadcasted_iota(jnp.int32, (size, size), 0) == lax.broadcasted_iota(jnp.int32, (size, size), 1)).astype(
        jnp.float32
    )
    work = jnp.concatenate([gram_matrix, eye], axis=1)
    for j in range(0, size, 2):
        left = jnp.broadcast_to(work[:, j : j + 1], shape)
        right = jnp.broadcast_to(work[:, j + 1 : j + 2], shape)
        upper, lower = work[j : j + 1], work[j + 1 : j + 2]
        inverse_pivot = 1.0 / left[j : j + 1]
        ratio = left[j + 1 : j + 2] * inverse_pivot
        next_pivot = right[j + 1 : j + 2] - ratio * left[j + 1 : j + 2]
        lower = (lower - ratio * upper) * (1.0 / next_pivot)
        right = jnp.where(row_of > j + 1, right - left * ratio, 0.0)
        left = jnp.where(row_of > j, left, 0.0)
        work = work - left * (upper * inverse_pivot) - right * lower
    diagonal = jnp.sum(work[:, :size] * eye, axis=1, keepdims=True)
    out_ref[...] = work[:, size:] * lax.rsqrt(diagonal)


def ritz_kernel(nodes_all, inverse_ref, folded_ref, out_ref):
    inverse = inverse_ref[...]
    half = jnp.dot(inverse, unfold(folded_ref[...]) / nodes_all, precision=HIGHEST, preferred_element_type=jnp.float32)
    out_ref[...] = lax.dot_general(
        half, inverse, CONTRACT_LAST, precision=HIGHEST, preferred_element_type=jnp.float32
    )


SMEM = pl.BlockSpec(memory_space=pltpu.SMEM)
VMEM = pl.BlockSpec(memory_space=pltpu.VMEM)


def call_kernel(kernel, ins, outs, scratch=(), flops=0):
    return pl.pallas_call(
        kernel,
        out_shape=[jax.ShapeDtypeStruct(shape, jnp.float32) for shape in outs],
        in_specs=[SMEM if value.dtype == jnp.int32 else VMEM for value in ins],
        out_specs=[VMEM] * len(outs),
        scratch_shapes=list(scratch),
        compiler_params=pltpu.CompilerParams(vmem_limit_bytes=24 * 2**20),
        cost_estimate=pl.CostEstimate(flops=flops, bytes_accessed=4 * sum(x.size for x in ins), transcendentals=0),
    )(*ins)


def gram(left, right):
    return lax.dot_general(left, right, CONTRACT_LAST, precision=HIGHEST)


def matmul(left, right):
    return jnp.dot(left, right, precision=HIGHEST)


def fold(square):
    half = square.shape[0] // 2
    return jnp.concatenate([square[:half], square[half:]], axis=1)


def unfold(folded):
    half = folded.shape[1] // 2
    return jnp.concatenate([folded[:, :half], folded[:, half:]], axis=0)


def shards(start, degrees, blocks, block_rows, block_cols, block_counts):
    row_devices = lax.axis_size(("x", "z"))
    col_devices = lax.axis_size(("y", "core"))
    nodes, width = start.shape
    nodes_all = nodes * row_devices * col_devices
    scale = jnp.sqrt(16.0 / degrees.astype(jnp.float32))[None, :]
    tile_blocks = blocks.reshape(blocks.shape[2:])
    rows = block_rows.reshape(-1)
    y_devices = lax.axis_size("y")
    rows = (rows % 2) * y_devices + rows // 2
    cols = block_cols.reshape(-1)
    count = block_counts.reshape(-1)

    tile = (rows, cols, count, tile_blocks)
    sums_shape = (col_devices, width, nodes)
    folded_shape = (width // 2, nodes)
    copies_shape = (lax.axis_size("x"), lax.axis_size("z"), width, nodes)
    serial = 5 * 10**9

    def gather(value, axes):
        return lax.all_gather(value, axes, axis=0, tiled=False)

    def spread(along_z):
        return jnp.broadcast_to(along_z[None, :, :width], copies_shape), along_z[:, width:].sum(0)

    def gather_x(copies):
        return exchange(copies, "x").reshape(row_devices, width, nodes)

    def reduce_cols(partial):
        halves = exchange(partial.reshape(2, -1, nodes), "core").sum(0)
        return exchange(halves.reshape(y_devices, width, nodes), "y").sum(0) * scale

    def inverse_factor(folded):
        (inverse,) = call_kernel(
            functools.partial(inverse_kernel, nodes_all), (folded,), [(width, width)], flops=serial
        )
        return inverse

    first = start.T
    copies, rider = spread(gather(jnp.concatenate([first * scale, fold(gram(first, first))], axis=0), "z"))
    partial, rider = call_kernel(
        tile_rider_kernel, (*tile, gather_x(copies), gather(rider, ("y", "core"))), [sums_shape, folded_shape]
    )
    once = reduce_cols(partial)

    copies, _ = spread(gather(once * scale, "z"))
    inverse = inverse_factor(gather(rider, "x"))
    (partial,) = call_kernel(tile_kernel, (*tile, gather_x(copies)), [sums_shape])
    filtered = matmul(inverse, 2.0 * reduce_cols(partial) - first)

    scaled = filtered * scale
    copies, rider = spread(gather(jnp.concatenate([scaled, fold(gram(filtered, filtered))], axis=0), "z"))
    own_rows = gather(jnp.concatenate([scaled, rider], axis=0), ("y", "core"))
    projected, rider = call_kernel(
        project_kernel,
        (*tile, gather_x(copies), own_rows),
        [folded_shape, folded_shape],
        [pltpu.VMEM(sums_shape, jnp.float32)],
    )
    chunk_shape = (folded_shape[0] // col_devices, nodes)
    chunks = exchange(projected.reshape(col_devices, *chunk_shape), ("y", "core"))
    copies, rider = call_kernel(
        sum_kernel, (chunks, gather(rider, "x")), [(row_devices, *chunk_shape), (1, *folded_shape)]
    )
    inverse = inverse_factor(rider)
    basis = matmul(inverse, filtered)
    projected = exchange(copies, ("x", "z")).sum(0)
    projected = to_all(projected, ("y", "core")).reshape(folded_shape)
    (ritz,) = call_kernel(functools.partial(ritz_kernel, nodes_all), (inverse, projected), [(width, width)])
    return (basis.T, ritz)


def solution(mesh):
    sizes = (4, 16, 8, 2)
    return jax.shard_map(
        shards,
        mesh=Mesh(mesh.devices.reshape(sizes), AXES),
        in_specs=(
            P(AXES, None),
            P(AXES),
            P(("x", "z"), ("y", "core"), None, None, None),
            P(("x", "z"), ("y", "core"), None),
            P(("x", "z"), ("y", "core"), None),
            P(("x", "z"), ("y", "core")),
        ),
        out_specs=(P(AXES, None), P()),
        check_vma=False,
    )
```

time: 313 us -> 306 us (0.978)
  other arithmetic: 27.8 us -> 2.51 us
  starting transfers between devices: 16.9 us -> 41.2 us
  waiting for transfers between devices: 35.5 us -> 25.6 us
  Pallas kernels: 16 us -> 20.7 us
    all_gather x4 -> x7, blocking collectives: 110 us -> 170 us  [gather(): return lax.all_gather(value, axes, axis=0, tiled=False)]
    all_to_all x6 -> x3, blocking collectives: 92.9 us -> 36 us  [exchange(): return lax.all_to_all(chunks, axes, 0, 0, tiled=True)]
    all_to_all x4 -> x7, starting transfers between devices: 16.9 us -> 41.2 us  [exchange(): return lax.all_to_all(chunks, axes, 0, 0, tiled=True)]
    another operation x10 -> x0, other arithmetic: 24.1 us -> none  [the longest x6 13 us: inverse_factor(): lower = jnp.linalg.cholesky(gram_matrix)]
    all_to_all x4 -> x7, waiting for transfers between devices: 35.5 us -> 25.6 us  [exchange(): return lax.all_to_all(chunks, axes, 0, 0, tiled=True)]
    broadcast_in_dim x2 -> x3, local copies, waits for them, and re-layouts: 0.02 us -> 4.74 us  [spread(): jnp.broadcast_to(along_z[None, :, :width], copies_shape)]
    pallas_call x3 -> x7, Pallas kernels: 16 us -> 20.7 us  [call_kernel(): pl.pallas_call(kernel, out_shape=[jax.ShapeDtypeStruct(shape, jnp.float32...]
    broadcast_in_dim x5 -> x1, local copies, waits for them, and re-layouts: 4.64 us -> 0.61 us  [to_all(): return exchange(jnp.broadcast_to(value[None], (copies, *value.shape)), axes)]
  transfers between devices with their start and end apart: 4 -> 7, of which waited for: 3 -> 3; matrix products, arithmetic and copies ran while one was open for 4% -> 0% of each run, Pallas kernels for 0% -> 2%
where the time goes in v2:
time: 306 us; the launch traced here: 305 us
  blocking collectives  206 us (67%)
  starting transfers between devices  41.2 us (13%)
  waiting for transfers between devices  25.6 us (8%)
  Pallas kernels  20.7 us (7%)
  local copies, waits for them, and re-layouts  5.45 us (2%)
    all_gather x7, blocking collectives, gather(): return lax.all_gather(value, axes, axis=0, tiled=False)  170 us
    all_to_all x7, starting transfers between devices, exchange(): return lax.all_to_all(chunks, axes, 0, 0, tiled=True)  41.2 us
    all_to_all x3, blocking collectives, exchange(): return lax.all_to_all(chunks, axes, 0, 0, tiled=True)  36 us
    all_to_all x7, waiting for transfers between devices, exchange(): return lax.all_to_all(chunks, axes, 0, 0, tiled=True)  25.6 us
    pallas_call x7, Pallas kernels, call_kernel(): pl.pallas_call(kernel, out_shape=[jax.ShapeDtypeStruct(shape, jnp.float32...  20.7 us
  transfers between devices with their start and end apart: 7, of which 3 were waited for; matrix products, arithmetic and copies ran while one was open for 0% of the time, Pallas kernels for 2%

profile of v2, /device:TPU:1, one launch (start us, length us, event | category | flops | bytes accessed | tf_op | source)
XLA Modules:
  0.0 305.1 jit_solution(16352353328043600230)
XLA Ops:
  0.6 0.7 divide_sqrt_fusion
  1.3 1.0 fusion.11
  2.3 0.8 bitcast_multiply_fusion.1
  3.1 0.1 maximum_maximum_fusion
  3.2 40.7 %all-gather = f32[1536,128]{1,0:T(8,128)S(1)} all-gather(f32[96,128]{1,0:T(8,128)S(1)} %maximum_maximum_fusion), channel_id=2, replica_groups=mesh['x'=4,'z'=16,'y'=8,'core'=2] {'z'}, dimensions={0}, use_global_device_ids=true | all-gather | bytes 835584 | tf_op jit(solution)/shard_map/all_gather | solution.py:164
  43.9 1.6 broadcast_in_dim.8
  45.4 4.6 %all-to-all-start = ((f32[4,16,64,128]{3,2,1,0:T(8,128)}), f32[4,16,64,128]{3,2,1,0:T(8,128)}, u32[]{:S(2)}, u32[]{:S(2)}) async-start(f32[4,16,64,128]{3,2,1,0:T(8,128)} %broadcast_in_dim.8), calls=%async_computation | async-start | bytes 4194304 | tf_op jit(solution)/shard_map/all_to_all | solution.py:16
  50.7 25.8 %all-gather.1 = f32[512,128]{1,0:T(8,128)S(1)} all-gather(f32[32,128]{1,0:T(8,128)S(1)} %slice_reduce_fusion.1), channel_id=3, replica_groups=mesh['x'=4,'z'=16,'y'=8,'core'=2] {'y','core'}, dimensions={0}, use_global_device_ids=true | all-gather | bytes 278528 | tf_op jit(solution)/shard_map/all_gather | solution.py:164
  76.5 0.0 copy-done.3
  76.6 0.0 all-to-all-done
  76.6 3.1 %shard_map.77 = (f32[16,64,128]{2,1,0:T(8,128)S(1)}, f32[32,128]{1,0:T(8,128)S(1)}) custom-call(s32[32]{0:T(128)S(1)} %fusion.7.rows_ref, s32[32]{0:T(128)S(1)} %bitcast.61, s32[1]{0:T(128)} %bitcast.48.count_ref, f32[32,128,128]{2,1,0:T(8,128)S(1)} %bitcast.51, f32[64,64,128]{2,1,0:T(8,128)} %bitcast.6.gathered_ref, f32[16,32,128]{2,1,0:T(8,128)S(1)} %bitcast.56), custom_call_target="tpu_custom_call" | custom-call | bytes 4456708 | tf_op jit(solution)/shard_map/pallas_call | solution.py:115
  79.7 4.6 %all_to_all.50 = f32[2,512,128]{2,1,0:T(8,128)S(1)} all-to-all(f32[2,512,128]{2,1,0:T(8,128)S(1)} %bitcast.57), channel_id=1, replica_groups=mesh['x'=4,'z'=16,'y'=8,'core'=2] {'core'}, dimensions={0} | all-to-all | bytes 1048576 | tf_op jit(solution)/shard_map/all_to_all | solution.py:16
  84.3 17.7 %all_to_all.51 = f32[8,64,128]{2,1,0:T(8,128)S(1)} all-to-all(f32[8,64,128]{2,1,0:T(8,128)S(1)} %bitcast.68), channel_id=1, replica_groups=mesh['x'=4,'z'=16,'y'=8,'core'=2] {'y'}, dimensions={0} | all-to-all | bytes 524288 | tf_op jit(solution)/shard_map/all_to_all | solution.py:16
  102.0 22.2 %all_gather.46 = f32[16,64,128]{2,1,0:T(8,128)S(1)} all-gather(f32[1,64,128]{2,1,0:T(8,128)S(1)} %fusion), channel_id=1, replica_groups=mesh['x'=4,'z'=16,'y'=8,'core'=2] {'z'}, dimensions={0}, use_global_device_ids=true | all-gather | bytes 557056 | tf_op jit(solution)/shard_map/all_gather | solution.py:164
  124.2 1.6 broadcast_in_dim.9
  125.8 4.4 %all-to-all-start.3 = ((f32[4,16,64,128]{3,2,1,0:T(8,128)}), f32[4,16,64,128]{3,2,1,0:T(8,128)}, u32[]{:S(2)}, u32[]{:S(2)}) async-start(f32[4,16,64,128]{3,2,1,0:T(8,128)} %broadcast_in_dim.9), calls=%async_computation.3 | async-start | bytes 4194304 | tf_op jit(solution)/shard_map/all_to_all | solution.py:16
  130.3 22.5 %all-gather.2 = f32[128,128]{1,0:T(8,128)S(1)} all-gather(f32[32,128]{1,0:T(8,128)S(1)} %get-tuple-element.8), channel_id=4, replica_groups=mesh['x'=4,'z'=16,'y'=8,'core'=2] {'x'}, dimensions={0}, use_global_device_ids=true | all-gather | bytes 81920 | tf_op jit(solution)/shard_map/all_gather | solution.py:164
  152.8 0.0 all-to-all-done.3
  152.8 3.1 %shard_map.79 = f32[16,64,128]{2,1,0:T(8,128)S(1)} custom-call(s32[32]{0:T(128)S(1)} %fusion.7.rows_ref, s32[32]{0:T(128)S(1)} %bitcast.62, s32[1]{0:T(128)} %bitcast.49.count_ref, f32[32,128,128]{2,1,0:T(8,128)S(1)} %bitcast.52, f32[64,64,128]{2,1,0:T(8,128)} %bitcast.12.gathered_ref), custom_call_target="tpu_custom_call" | custom-call | bytes 4194564 | tf_op jit(solution)/shard_map/pallas_call | solution.py:115
  155.8 13.7 %all_to_all.52 = f32[2,512,128]{2,1,0:T(8,128)S(1)} all-to-all(f32[2,512,128]{2,1,0:T(8,128)S(1)} %bitcast.55), channel_id=1, replica_groups=mesh['x'=4,'z'=16,'y'=8,'core'=2] {'core'}, dimensions={0} | all-to-all | bytes 1048576 | tf_op jit(solution)/shard_map/all_to_all | solution.py:16
  169.6 0.7 reduce_sum.69
  170.3 3.4 %all-to-all-start.5 = ((f32[8,64,128]{2,1,0:T(8,128)}), f32[8,64,128]{2,1,0:T(8,128)S(1)}, u32[]{:S(2)}, u32[]{:S(2)}) async-start(f32[8,64,128]{2,1,0:T(8,128)} %bitcast.14), calls=%async_computation.5 | async-start | bytes 524288 | tf_op jit(solution)/shard_map/all_to_all | solution.py:16
  173.7 0.0 copy-start.2
  173.7 3.4 %shard_map.78 = f32[64,64]{1,0:T(8,128)S(1)} custom-call(f32[4,32,128]{2,1,0:T(8,128)S(1)} %bitcast.59), custom_call_target="tpu_custom_call" | custom-call | flops 5000000000 | bytes 65536 | tf_op jit(solution)/shard_map/pallas_call | solution.py:115
  177.1 8.9 %all-to-all-done.5 = f32[8,64,128]{2,1,0:T(8,128)S(1)} async-done(((f32[8,64,128]{2,1,0:T(8,128)}), f32[8,64,128]{2,1,0:T(8,128)S(1)}, u32[]{:S(2)}, u32[]{:S(2)}) %all-to-all-start.5) | async-done | bytes 262176 | tf_op jit(solution)/shard_map/all_to_all | solution.py:16
  186.0 0.0 copy-done.2
  186.0 0.2 broadcast_multiply_fusion
  186.2 0.2 fusion.12
  186.4 0.1 pad_maximum_fusion.1
  186.4 25.0 %all-gather.3 = f32[1536,128]{1,0:T(8,128)S(1)} all-gather(f32[96,128]{1,0:T(8,128)S(1)} %pad_maximum_fusion.1), channel_id=5, replica_groups=mesh['x'=4,'z'=16,'y'=8,'core'=2] {'z'}, dimensions={0}, use_global_device_ids=true | all-gather | bytes 835584 | tf_op jit(solution)/shard_map/all_gather | solution.py:164
  211.5 1.6 broadcast_in_dim.10
  213.1 4.4 %all-to-all-start.6 = ((f32[4,16,64,128]{3,2,1,0:T(8,128)}), f32[4,16,64,128]{3,2,1,0:T(8,128)}, u32[]{:S(2)}, u32[]{:S(2)}) async-start(f32[4,16,64,128]{3,2,1,0:T(8,128)} %broadcast_in_dim.10), calls=%async_computation.6 | async-start | bytes 4194304 | tf_op jit(solution)/shard_map/all_to_all | solution.py:16
  217.6 24.4 %all-gather.4 = f32[1536,128]{1,0:T(8,128)S(1)} all-gather(f32[96,128]{1,0:T(8,128)S(1)} %pad_maximum_fusion), channel_id=6, replica_groups=mesh['x'=4,'z'=16,'y'=8,'core'=2] {'y','core'}, dimensions={0}, use_global_device_ids=true | all-gather | bytes 835584 | tf_op jit(solution)/shard_map/all_gather | solution.py:164
  242.0 0.0 all-to-all-done.6
  242.0 6.2 %shard_map.80 = (f32[32,128]{1,0:T(8,128)}, f32[32,128]{1,0:T(8,128)S(1)}) custom-call(s32[32]{0:T(128)S(1)} %fusion.7.rows_ref, s32[32]{0:T(128)S(1)} %bitcast.63, s32[1]{0:T(128)} %bitcast.50.count_ref, f32[32,128,128]{2,1,0:T(8,128)S(1)} %bitcast.53, f32[64,64,128]{2,1,0:T(8,128)} %bitcast.16.gathered_ref, f32[16,96,128]{2,1,0:T(8,128)S(1)} %bitcast.54), custom_call_target="tpu_custom_call" | custom-call | bytes 4980996 | tf_op jit(solution)/shard_map/pallas_call | solution.py:115
  248.2 6.2 %all-to-all-start.7 = ((f32[16,2,128]{2,1,0:T(2,128)}), f32[16,2,128]{2,1,0:T(2,128)S(1)}, u32[]{:S(2)}, u32[]{:S(2)}) async-start(f32[16,2,128]{2,1,0:T(2,128)} %bitcast.18), calls=%async_computation.7 | async-start | bytes 32768 | tf_op jit(solution)/shard_map/all_to_all | solution.py:16
  254.4 9.3 %all-gather.5 = f32[128,128]{1,0:T(8,128)S(1)} all-gather(f32[32,128]{1,0:T(8,128)S(1)} %get-tuple-element.11), channel_id=7, replica_groups=mesh['x'=4,'z'=16,'y'=8,'core'=2] {'x'}, dimensions={0}, use_global_device_ids=true | all-gather | bytes 81920 | tf_op jit(solution)/shard_map/all_gather | solution.py:164
  263.7 0.0 all-to-all-done.7.chunks_ref
  263.7 0.7 shard_map.81
  264.3 7.0 %all-to-all-start.8 = ((f32[64,2,128]{2,1,0:T(2,128)}), f32[64,2,128]{2,1,0:T(2,128)S(1)}, u32[]{:S(2)}, u32[]{:S(2)}) async-start(f32[64,2,128]{2,1,0:T(2,128)} %get-tuple-element.13), calls=%async_computation.8 | async-start | bytes 131072 | tf_op jit(solution)/shard_map/all_to_all | solution.py:16
  271.3 3.4 %shard_map.82.inverse_ref = f32[64,64]{1,0:T(8,128)S(1)} custom-call(f32[1,32,128]{2,1,0:T(8,128)S(1)} %get-tuple-element.12.folded_ref), custom_call_target="tpu_custom_call" | custom-call | flops 5000000000 | bytes 16384 | tf_op jit(solution)/shard_map/pallas_call | solution.py:115
  274.7 10.1 %all-to-all-done.8 = f32[64,2,128]{2,1,0:T(2,128)S(1)} async-done(((f32[64,2,128]{2,1,0:T(2,128)}), f32[64,2,128]{2,1,0:T(2,128)S(1)}, u32[]{:S(2)}, u32[]{:S(2)}) %all-to-all-start.8) | async-done | bytes 65568 | tf_op jit(solution)/shard_map/all_to_all | solution.py:16
  284.8 0.1 reduce_sum.72
  284.9 0.6 broadcast_in_dim.11
  285.5 11.2 %all-to-all-start.9 = ((f32[16,2,128]{2,1,0:T(2,128)}), f32[16,2,128]{2,1,0:T(2,128)S(1)}, u32[]{:S(2)}, u32[]{:S(2)}) async-start(f32[16,2,128]{2,1,0:T(2,128)} %broadcast_in_dim.11), calls=%async_computation.9 | async-start | bytes 32768 | tf_op jit(solution)/shard_map/all_to_all | solution.py:16
  296.7 0.8 fusion.13
  297.5 6.6 %all-to-all-done.9 = f32[16,2,128]{2,1,0:T(2,128)S(1)} async-done(((f32[16,2,128]{2,1,0:T(2,128)}), f32[16,2,128]{2,1,0:T(2,128)S(1)}, u32[]{:S(2)}, u32[]{:S(2)}) %all-to-all-start.9) | async-done | bytes 16416 | tf_op jit(solution)/shard_map/all_to_all | solution.py:16
  304.0 1.0 shard_map.83
  (17 shorter events, 0.2 us)
Async XLA Ops:
  45.4 31.1 %copy-start.3 = (s32[1,1,32]{2,1,0:T(1,128)S(1)}, s32[1,1,32]{2,1,0:T(1,128)}, u32[]{:S(2)}) copy-start(s32[1,1,32]{2,1,0:T(1,128)} %param.9) | copy-start | bytes 388
  45.4 31.1 %copy-start = (f32[1,1,32,128,128]{4,3,2,1,0:T(8,128)S(1)}, f32[1,1,32,128,128]{4,3,2,1,0:T(8,128)}, u32[]{:S(2)}) copy-start(f32[1,1,32,128,128]{4,3,2,1,0:T(8,128)} %param.8) | copy-start | bytes 6291460
  45.4 31.1 %copy-start.1 = (s32[1,1,32]{2,1,0:T(1,128)S(1)}, s32[1,1,32]{2,1,0:T(1,128)}, u32[]{:S(2)}) copy-start(s32[1,1,32]{2,1,0:T(1,128)} %param.10) | copy-start | bytes 388
  45.4 31.1 %all-to-all-start = ((f32[4,16,64,128]{3,2,1,0:T(8,128)}), f32[4,16,64,128]{3,2,1,0:T(8,128)}, u32[]{:S(2)}, u32[]{:S(2)}) async-start(f32[4,16,64,128]{3,2,1,0:T(8,128)} %broadcast_in_dim.8), calls=%async_computation | async-start | bytes 4194304 | tf_op jit(solution)/shard_map/all_to_all | solution.py:16
  125.8 27.0 %all-to-all-start.3 = ((f32[4,16,64,128]{3,2,1,0:T(8,128)}), f32[4,16,64,128]{3,2,1,0:T(8,128)}, u32[]{:S(2)}, u32[]{:S(2)}) async-start(f32[4,16,64,128]{3,2,1,0:T(8,128)} %broadcast_in_dim.9), calls=%async_computation.3 | async-start | bytes 4194304 | tf_op jit(solution)/shard_map/all_to_all | solution.py:16
  170.3 15.7 %all-to-all-start.5 = ((f32[8,64,128]{2,1,0:T(8,128)}), f32[8,64,128]{2,1,0:T(8,128)S(1)}, u32[]{:S(2)}, u32[]{:S(2)}) async-start(f32[8,64,128]{2,1,0:T(8,128)} %bitcast.14), calls=%async_computation.5 | async-start | bytes 524288 | tf_op jit(solution)/shard_map/all_to_all | solution.py:16
  173.7 12.3 %copy-start.2 = (f32[128,64]{0,1:T(8,128)S(1)}, f32[128,64]{0,1:T(8,128)}, u32[]{:S(2)}) copy-start(f32[128,64]{0,1:T(8,128)} %param.6) | copy-start | bytes 98308
  213.1 28.9 %all-to-all-start.6 = ((f32[4,16,64,128]{3,2,1,0:T(8,128)}), f32[4,16,64,128]{3,2,1,0:T(8,128)}, u32[]{:S(2)}, u32[]{:S(2)}) async-start(f32[4,16,64,128]{3,2,1,0:T(8,128)} %broadcast_in_dim.10), calls=%async_computation.6 | async-start | bytes 4194304 | tf_op jit(solution)/shard_map/all_to_all | solution.py:16
  248.2 15.5 %all-to-all-start.7 = ((f32[16,2,128]{2,1,0:T(2,128)}), f32[16,2,128]{2,1,0:T(2,128)S(1)}, u32[]{:S(2)}, u32[]{:S(2)}) async-start(f32[16,2,128]{2,1,0:T(2,128)} %bitcast.18), calls=%async_computation.7 | async-start | bytes 32768 | tf_op jit(solution)/shard_map/all_to_all | solution.py:16
  264.3 20.5 %all-to-all-start.8 = ((f32[64,2,128]{2,1,0:T(2,128)}), f32[64,2,128]{2,1,0:T(2,128)S(1)}, u32[]{:S(2)}, u32[]{:S(2)}) async-start(f32[64,2,128]{2,1,0:T(2,128)} %get-tuple-element.13), calls=%async_computation.8 | async-start | bytes 131072 | tf_op jit(solution)/shard_map/all_to_all | solution.py:16
  285.5 18.5 %all-to-all-start.9 = ((f32[16,2,128]{2,1,0:T(2,128)}), f32[16,2,128]{2,1,0:T(2,128)S(1)}, u32[]{:S(2)}, u32[]{:S(2)}) async-start(f32[16,2,128]{2,1,0:T(2,128)} %broadcast_in_dim.11), calls=%async_computation.9 | async-start | bytes 32768 | tf_op jit(solution)/shard_map/all_to_all | solution.py:16

commit v3 on v2

v3 whole, which is shorter than its diff:
```python
import functools

import jax
import jax.numpy as jnp
from jax import lax
from jax.experimental import pallas as pl
from jax.experimental.pallas import tpu as pltpu
from jax.sharding import Mesh, PartitionSpec as P

HIGHEST = lax.Precision.HIGHEST
AXES = ("x", "zh", "zl", "y", "core")
ROW = ("x", "zh", "zl")
COL = ("y", "core")
CONTRACT_LAST = (((1,), (1,)), ((), ()))


def exchange(chunks, axes):
    return lax.all_to_all(chunks, axes, 0, 0, tiled=True)


def to_all(value, axes):
    copies = lax.axis_size(axes)
    return exchange(jnp.broadcast_to(value[None], (copies, *value.shape)), axes)


def split(value):
    high = value.astype(jnp.bfloat16)
    return high, (value - high.astype(jnp.float32)).astype(jnp.bfloat16)


def dot_pieces(left, right):
    return lax.dot_general(left, right, CONTRACT_LAST, preferred_element_type=jnp.float32)


def add_slots(rows_ref, cols_ref, count_ref, blocks_ref, gathered_ref, sums_ref):
    sums_ref[...] = jnp.zeros_like(sums_ref)
    count = count_ref[0]
    width = sums_ref.shape[1]
    for slot in range(blocks_ref.shape[0]):
        live = (slot < count).astype(jnp.float32)
        high, low = split(gathered_ref[cols_ref[slot]] * live)
        block_high, block_low = split(blocks_ref[slot])
        both = dot_pieces(jnp.concatenate([high, low], axis=0), block_high)
        sums_ref[rows_ref[slot]] += both[:width] + both[width:] + dot_pieces(high, block_low)


def tile_kernel(rows_ref, cols_ref, count_ref, blocks_ref, gathered_ref, out_ref):
    add_slots(rows_ref, cols_ref, count_ref, blocks_ref, gathered_ref, out_ref)


def tile_rider_kernel(rows_ref, cols_ref, count_ref, blocks_ref, gathered_ref, rider_ref, out_ref, rider_out_ref):
    add_slots(rows_ref, cols_ref, count_ref, blocks_ref, gathered_ref, out_ref)
    rider_out_ref[...] = jnp.sum(rider_ref[...], axis=0)


def project_kernel(
    rows_ref, cols_ref, count_ref, blocks_ref, gathered_ref, own_ref, gram_ref, out_ref, sums_ref
):
    add_slots(rows_ref, cols_ref, count_ref, blocks_ref, gathered_ref, sums_ref)
    row_blocks, width, _ = sums_ref.shape
    half = row_blocks // 2
    products = jnp.zeros((2 * width, 2 * width), jnp.float32)
    for piece in range(row_blocks):
        left = jnp.concatenate(split(own_ref[piece]), axis=0)
        right = jnp.concatenate(split(sums_ref[(piece % 2) * half + piece // 2]), axis=0)
        products += dot_pieces(left, right)
    total = products[:width, :width] + products[:width, width:] + products[width:, :width] + products[width:, width:]
    out_ref[...] = jnp.concatenate([total, gram_ref[...]], axis=1)


def sum_kernel(chunks_ref, copies_ref):
    copies_ref[...] = jnp.broadcast_to(jnp.sum(chunks_ref[...], axis=0)[None], copies_ref.shape)


def inverse_factor(gram_matrix):
    size = gram_matrix.shape[0]
    shape = (size, 2 * size)
    row_of = lax.broadcasted_iota(jnp.int32, shape, 0)
    eye = (lax.broadcasted_iota(jnp.int32, (size, size), 0) == lax.broadcasted_iota(jnp.int32, (size, size), 1)).astype(
        jnp.float32
    )
    work = jnp.concatenate([gram_matrix, eye], axis=1)
    for j in range(0, size, 2):
        left = jnp.broadcast_to(work[:, j : j + 1], shape)
        right = jnp.broadcast_to(work[:, j + 1 : j + 2], shape)
        upper, lower = work[j : j + 1], work[j + 1 : j + 2]
        inverse_pivot = 1.0 / left[j : j + 1]
        ratio = left[j + 1 : j + 2] * inverse_pivot
        next_pivot = right[j + 1 : j + 2] - ratio * left[j + 1 : j + 2]
        lower = (lower - ratio * upper) * (1.0 / next_pivot)
        right = jnp.where(row_of > j + 1, right - left * ratio, 0.0)
        left = jnp.where(row_of > j, left, 0.0)
        work = work - left * (upper * inverse_pivot) - right * lower
    diagonal = jnp.sum(work[:, :size] * eye, axis=1, keepdims=True)
    return work[:, size:] * lax.rsqrt(diagonal)


def inverse_kernel(nodes_all, folded_ref, out_ref):
    out_ref[...] = inverse_factor(unfold(folded_ref[...]) / nodes_all)


def finish_kernel(nodes_all, both_ref, filtered_ref, basis_ref, ritz_ref):
    width = filtered_ref.shape[0]
    both = both_ref[...] / nodes_all
    inverse = inverse_factor(both[:, width:])
    half = jnp.dot(inverse, both[:, :width], precision=HIGHEST, preferred_element_type=jnp.float32)
    ritz_ref[...] = lax.dot_general(
        half, inverse, CONTRACT_LAST, precision=HIGHEST, preferred_element_type=jnp.float32
    )
    basis_ref[...] = jnp.dot(inverse, filtered_ref[...], precision=HIGHEST, preferred_element_type=jnp.float32)


SMEM = pl.BlockSpec(memory_space=pltpu.SMEM)
VMEM = pl.BlockSpec(memory_space=pltpu.VMEM)


def call_kernel(kernel, ins, outs, scratch=(), flops=0):
    return pl.pallas_call(
        kernel,
        out_shape=[jax.ShapeDtypeStruct(shape, jnp.float32) for shape in outs],
        in_specs=[SMEM if value.dtype == jnp.int32 else VMEM for value in ins],
        out_specs=[VMEM] * len(outs),
        scratch_shapes=list(scratch),
        compiler_params=pltpu.CompilerParams(vmem_limit_bytes=24 * 2**20),
        cost_estimate=pl.CostEstimate(flops=flops, bytes_accessed=4 * sum(x.size for x in ins), transcendentals=0),
    )(*ins)


def gram(left, right):
    return lax.dot_general(left, right, CONTRACT_LAST, precision=HIGHEST)


def matmul(left, right):
    return jnp.dot(left, right, precision=HIGHEST)


def fold(square):
    half = square.shape[0] // 2
    return jnp.concatenate([square[:half], square[half:]], axis=1)


def unfold(folded):
    half = folded.shape[1] // 2
    return jnp.concatenate([folded[:, :half], folded[:, half:]], axis=0)


def shards(start, degrees, blocks, block_rows, block_cols, block_counts):
    row_devices = lax.axis_size(ROW)
    col_devices = lax.axis_size(COL)
    nodes, width = start.shape
    nodes_all = nodes * row_devices * col_devices
    scale = jnp.sqrt(16.0 / degrees.astype(jnp.float32))[None, :]
    tile_blocks = blocks.reshape(blocks.shape[2:])
    rows = block_rows.reshape(-1)
    y_devices = lax.axis_size("y")
    rows = (rows % 2) * y_devices + rows // 2
    zh_devices, zl_devices = lax.axis_size("zh"), lax.axis_size("zl")
    cols = block_cols.reshape(-1)
    along_z = cols % (zh_devices * zl_devices)
    cols = cols - along_z + (along_z % zl_devices) * zh_devices + along_z // zl_devices
    count = block_counts.reshape(-1)

    tile = (rows, cols, count, tile_blocks)
    sums_shape = (col_devices, width, nodes)
    serial = 5 * 10**9

    def gather(value, axes):
        return lax.all_gather(value, axes, axis=0, tiled=False)

    def gather_rows(along_zh):
        return to_all(along_zh, ("x", "zl")).reshape(row_devices, width, nodes)

    def reduce_cols(partial):
        halves = exchange(partial.reshape(2, -1, nodes), "core").sum(0)
        return exchange(halves.reshape(y_devices, width, nodes), "y").sum(0) * scale

    def sum_to(chunks, copies):
        return call_kernel(sum_kernel, (chunks,), [(copies, *chunks.shape[1:])])[0]

    first = start.T
    gathered = gather_rows(to_all(first * scale, "zh"))
    rider = gather(fold(gram(first, first)), COL)
    partial, rider = call_kernel(tile_rider_kernel, (*tile, gathered, rider), [sums_shape, rider.shape[1:]])
    once = reduce_cols(partial)

    rider = gather(rider, "x").sum(0).reshape(lax.axis_size("x"), -1, nodes)
    rider = lax.dynamic_index_in_dim(rider, lax.axis_index("x"), keepdims=False)
    along_zh = to_all(jnp.concatenate([once * scale, rider], axis=0), "zh")
    gathered = gather_rows(along_zh[:, :width])
    rider = gather(along_zh[:, width:].sum(0), ("x", "zl"))
    rider = rider.reshape(lax.axis_size("x"), zl_devices, -1, nodes).sum(1).reshape(-1, nodes)
    (inverse,) = call_kernel(
        functools.partial(inverse_kernel, nodes_all), (rider,), [(width, width)], flops=serial
    )
    (partial,) = call_kernel(tile_kernel, (*tile, gathered), [sums_shape])
    filtered = matmul(inverse, 2.0 * reduce_cols(partial) - first)

    scaled = filtered * scale
    gathered = gather_rows(to_all(scaled, "zh"))
    (projected,) = call_kernel(
        project_kernel,
        (*tile, gathered, gather(scaled, COL), gram(filtered, filtered)),
        [(width, 2 * width)],
        [pltpu.VMEM(sums_shape, jnp.float32)],
    )
    projected = exchange(projected.reshape(col_devices, -1, 2 * width), COL)
    projected = exchange(sum_to(projected, row_devices), ROW)
    projected = exchange(sum_to(projected, col_devices), COL).reshape(width, 2 * width)
    basis, ritz = call_kernel(
        functools.partial(finish_kernel, nodes_all), (projected, filtered), [(width, nodes), (width, width)]
    )
    return (basis.T, ritz)


def solution(mesh):
    sizes = (4, 8, 2, 8, 2)
    return jax.shard_map(
        shards,
        mesh=Mesh(mesh.devices.reshape(sizes), AXES),
        in_specs=(
            P(AXES, None),
            P(AXES),
            P(ROW, COL, None, None, None),
            P(ROW, COL, None),
            P(ROW, COL, None),
            P(ROW, COL),
        ),
        out_specs=(P(AXES, None), P()),
        check_vma=False,
    )
```

time: 306 us -> 313 us (1.023)
  blocking collectives: 206 us -> 236 us
  starting transfers between devices: 41.2 us -> 25.5 us
  waiting for transfers between devices: 25.6 us -> 22.2 us
    all_to_all x3 -> x8, blocking collectives: 36 us -> 150 us  [exchange(): return lax.all_to_all(chunks, axes, 0, 0, tiled=True)]
    all_gather x7 -> x4, blocking collectives: 170 us -> 86.3 us  [gather(): return lax.all_gather(value, axes, axis=0, tiled=False)]
    all_to_all x7 -> x5, starting transfers between devices: 41.2 us -> 25.5 us  [exchange(): return lax.all_to_all(chunks, axes, 0, 0, tiled=True)]
    broadcast_in_dim x3 -> x0, local copies, waits for them, and re-layouts: 4.74 us -> none  [spread(): jnp.broadcast_to(along_z[None, :, :width], copies_shape)]
    broadcast_in_dim x1 -> x6, local copies, waits for them, and re-layouts: 0.61 us -> 4.71 us  [to_all(): return exchange(jnp.broadcast_to(value[None], (copies, *value.shape)), axes)]
    all_to_all x7 -> x5, waiting for transfers between devices: 25.6 us -> 22.2 us  [exchange(): return lax.all_to_all(chunks, axes, 0, 0, tiled=True)]
  transfers between devices with their start and end apart: 7 -> 5, of which waited for: 3 -> 4; matrix products, arithmetic and copies ran while one was open for 0% -> 0% of each run, Pallas kernels for 2% -> 1%
where the time goes in v3:
time: 313 us; the launch traced here: 312 us
  blocking collectives  236 us (75%)
  starting transfers between devices  25.5 us (8%)
  waiting for transfers between devices  22.2 us (7%)
  Pallas kernels  18 us (6%)
  local copies, waits for them, and re-layouts  4.76 us (2%)
    all_to_all x8, blocking collectives, exchange(): return lax.all_to_all(chunks, axes, 0, 0, tiled=True)  150 us
    all_gather x4, blocking collectives, gather(): return lax.all_gather(value, axes, axis=0, tiled=False)  86.3 us
    all_to_all x5, starting transfers between devices, exchange(): return lax.all_to_all(chunks, axes, 0, 0, tiled=True)  25.5 us
    all_to_all x5, waiting for transfers between devices, exchange(): return lax.all_to_all(chunks, axes, 0, 0, tiled=True)  22.2 us
    pallas_call x7, Pallas kernels, call_kernel(): pl.pallas_call(kernel, out_shape=[jax.ShapeDtypeStruct(shape, jnp.float32...  18 us
  transfers between devices with their start and end apart: 5, of which 4 were waited for; matrix products, arithmetic and copies ran while one was open for 0% of the time, Pallas kernels for 1%

profile of v3, /device:TPU:1, one launch (start us, length us, event | category | flops | bytes accessed | tf_op | source)
XLA Modules:
  0.0 311.9 jit_solution(1266042614735784644)
XLA Ops:
  0.6 0.7 divide_sqrt_fusion
  1.3 0.8 bitcast_multiply_fusion
  2.1 35.8 %all_to_all.65 = f32[8,64,128]{2,1,0:T(8,128)S(1)} all-to-all(f32[8,64,128]{2,1,0:T(8,128)S(1)} %broadcast_in_dim.14), channel_id=1, replica_groups=mesh['x'=4,'zh'=8,'zl'=2,'y'=8,'core'=2] {'zh'}, dimensions={0} | all-to-all | bytes 524288 | tf_op jit(solution)/shard_map/all_to_all | solution.py:18
  37.9 1.6 broadcast_in_dim.15
  39.4 0.0 copy-start.1
  39.4 0.0 copy-start.2
  39.4 0.0 copy-start.3
  39.4 0.0 copy-start
  39.4 6.6 %all-to-all-start.1 = ((f32[8,8,64,128]{3,2,1,0:T(8,128)}), f32[8,8,64,128]{3,2,1,0:T(8,128)}, u32[]{:S(2)}, u32[]{:S(2)}) async-start(f32[8,8,64,128]{3,2,1,0:T(8,128)} %broadcast_in_dim.15), calls=%async_computation.1 | async-start | bytes 4194304 | tf_op jit(solution)/shard_map/all_to_all | solution.py:18
  46.7 0.0 copy-done.1
  46.7 0.2 fusion.13
  46.9 0.1 pad_maximum_fusion.1
  46.9 21.3 %all-gather = f32[512,128]{1,0:T(8,128)S(1)} all-gather(f32[32,128]{1,0:T(8,128)S(1)} %pad_maximum_fusion.1), channel_id=2, replica_groups=mesh['x'=4,'zh'=8,'zl'=2,'y'=8,'core'=2] {'y','core'}, dimensions={0}, use_global_device_ids=true | all-gather | bytes 278528 | tf_op jit(solution)/shard_map/all_gather | solution.py:168
  68.3 0.0 copy-done.2
  68.3 0.0 copy-done.3
  68.3 1.6 all-to-all-done.1
  69.9 0.0 copy-done
  69.9 3.1 shard_map.77
  72.9 7.9 %all_to_all.66 = f32[2,512,128]{2,1,0:T(8,128)S(1)} all-to-all(f32[2,512,128]{2,1,0:T(8,128)S(1)} %bitcast.60), channel_id=1, replica_groups=mesh['x'=4,'zh'=8,'zl'=2,'y'=8,'core'=2] {'core'}, dimensions={0} | all-to-all | bytes 1048576 | tf_op jit(solution)/shard_map/all_to_all | solution.py:18
  80.9 0.7 reduce_sum.63
  81.6 6.8 %all-to-all-start.3 = ((f32[8,64,128]{2,1,0:T(8,128)}), f32[8,64,128]{2,1,0:T(8,128)S(1)}, u32[]{:S(2)}, u32[]{:S(2)}) async-start(f32[8,64,128]{2,1,0:T(8,128)} %bitcast.8), calls=%async_computation.3 | async-start | bytes 524288 | tf_op jit(solution)/shard_map/all_to_all | solution.py:18
  88.4 9.3 %all-gather.1 = f32[128,128]{1,0:T(8,128)S(1)} all-gather(f32[32,128]{1,0:T(8,128)S(1)} %get-tuple-element.7), channel_id=3, replica_groups=mesh['x'=4,'zh'=8,'zl'=2,'y'=8,'core'=2] {'x'}, dimensions={0}, use_global_device_ids=true | all-gather | bytes 81920 | tf_op jit(solution)/shard_map/all_gather | solution.py:168
  97.7 1.8 all-to-all-done.3
  99.6 24.9 %all_to_all.67 = f32[8,72,128]{2,1,0:T(8,128)S(1)} all-to-all(f32[8,72,128]{2,1,0:T(8,128)S(1)} %broadcast_in_dim.16), channel_id=1, replica_groups=mesh['x'=4,'zh'=8,'zl'=2,'y'=8,'core'=2] {'zh'}, dimensions={0} | all-to-all | bytes 589824 | tf_op jit(solution)/shard_map/all_to_all | solution.py:18
  124.4 1.6 broadcast_in_dim.17
  126.0 4.3 %all-to-all-start.5 = ((f32[8,8,64,128]{3,2,1,0:T(8,128)}), f32[8,8,64,128]{3,2,1,0:T(8,128)}, u32[]{:S(2)}, u32[]{:S(2)}) async-start(f32[8,8,64,128]{3,2,1,0:T(8,128)} %broadcast_in_dim.17), calls=%async_computation.5 | async-start | bytes 4194304 | tf_op jit(solution)/shard_map/all_to_all | solution.py:18
  130.4 39.5 %all-gather.2 = f32[64,128]{1,0:T(8,128)S(1)} all-gather(f32[8,128]{1,0:T(8,128)S(1)} %slice_reduce_fusion), channel_id=4, replica_groups=mesh['x'=4,'zh'=8,'zl'=2,'y'=8,'core'=2] {'x','zl'}, dimensions={0}, use_global_device_ids=true | all-gather | bytes 36864 | tf_op jit(solution)/shard_map/all_gather | solution.py:168
  169.8 0.0 all-to-all-done.5
  169.8 3.1 shard_map.79
  172.9 14.1 %all_to_all.68 = f32[2,512,128]{2,1,0:T(8,128)S(1)} all-to-all(f32[2,512,128]{2,1,0:T(8,128)S(1)} %bitcast.58), channel_id=1, replica_groups=mesh['x'=4,'zh'=8,'zl'=2,'y'=8,'core'=2] {'core'}, dimensions={0} | all-to-all | bytes 1048576 | tf_op jit(solution)/shard_map/all_to_all | solution.py:18
  187.0 0.7 reduce_sum.68
  187.8 3.4 %all-to-all-start.7 = ((f32[8,64,128]{2,1,0:T(8,128)}), f32[8,64,128]{2,1,0:T(8,128)S(1)}, u32[]{:S(2)}, u32[]{:S(2)}) async-start(f32[8,64,128]{2,1,0:T(8,128)} %bitcast.16), calls=%async_computation.7 | async-start | bytes 524288 | tf_op jit(solution)/shard_map/all_to_all | solution.py:18
  191.2 3.4 %shard_map.78 = f32[64,64]{1,0:T(8,128)S(1)} custom-call(f32[32,128]{1,0:T(8,128)S(1)} %bitcast.63), custom_call_target="tpu_custom_call" | custom-call | flops 5000000000 | bytes 16384 | tf_op jit(solution)/shard_map/pallas_call | solution.py:118
  194.6 8.8 %all-to-all-done.7 = f32[8,64,128]{2,1,0:T(8,128)S(1)} async-done(((f32[8,64,128]{2,1,0:T(8,128)}), f32[8,64,128]{2,1,0:T(8,128)S(1)}, u32[]{:S(2)}, u32[]{:S(2)}) %all-to-all-start.7) | async-done | bytes 262176 | tf_op jit(solution)/shard_map/all_to_all | solution.py:18
  203.4 0.2 broadcast_multiply_fusion
  203.6 25.1 %all_to_all.69 = f32[8,64,128]{2,1,0:T(8,128)S(1)} all-to-all(f32[8,64,128]{2,1,0:T(8,128)S(1)} %broadcast_in_dim.18), channel_id=1, replica_groups=mesh['x'=4,'zh'=8,'zl'=2,'y'=8,'core'=2] {'zh'}, dimensions={0} | all-to-all | bytes 524288 | tf_op jit(solution)/shard_map/all_to_all | solution.py:18
  228.7 1.6 broadcast_in_dim.19
  230.3 4.3 %all-to-all-start.9 = ((f32[8,8,64,128]{3,2,1,0:T(8,128)}), f32[8,8,64,128]{3,2,1,0:T(8,128)}, u32[]{:S(2)}, u32[]{:S(2)}) async-start(f32[8,8,64,128]{3,2,1,0:T(8,128)} %broadcast_in_dim.19), calls=%async_computation.9 | async-start | bytes 4194304 | tf_op jit(solution)/shard_map/all_to_all | solution.py:18
  234.6 0.2 fusion.14.gram_ref
  234.8 16.2 %all-gather.3 = f32[1024,128]{1,0:T(8,128)S(1)} all-gather(f32[64,128]{1,0:T(8,128)S(1)} %get-tuple-element.12), channel_id=5, replica_groups=mesh['x'=4,'zh'=8,'zl'=2,'y'=8,'core'=2] {'y','core'}, dimensions={0}, use_global_device_ids=true | all-gather | bytes 557056 | tf_op jit(solution)/shard_map/all_gather | solution.py:168
  251.0 10.1 %all-to-all-done.9 = f32[8,8,64,128]{3,2,1,0:T(8,128)} async-done(((f32[8,8,64,128]{3,2,1,0:T(8,128)}), f32[8,8,64,128]{3,2,1,0:T(8,128)}, u32[]{:S(2)}, u32[]{:S(2)}) %all-to-all-start.9) | async-done | bytes 2097184 | tf_op jit(solution)/shard_map/all_to_all | solution.py:18
  261.1 4.0 %shard_map.80 = f32[64,128]{1,0:T(8,128)S(1)} custom-call(s32[32]{0:T(128)S(1)} %get-tuple-element.14.rows_ref, s32[32]{0:T(128)S(1)} %get-tuple-element.15.cols_ref, s32[1]{0:T(128)} %bitcast.53.count_ref, f32[32,128,128]{2,1,0:T(8,128)S(1)} %bitcast.56, f32[64,64,128]{2,1,0:T(8,128)} %bitcast.17.gathered_ref, f32[16,64,128]{2,1,0:T(8,128)S(1)} %bitcast.57, ...), custom_call_target="tpu_custom_call" | custom-call | bytes 4735236 | tf_op jit(solution)/shard_map/pallas_call | solution.py:118
  265.1 11.4 %all_to_all.70.chunks_ref = f32[16,4,128]{2,1,0:T(4,128)S(1)} all-to-all(f32[16,4,128]{2,1,0:T(4,128)S(1)} %bitcast.61), channel_id=1, replica_groups=mesh['x'=4,'zh'=8,'zl'=2,'y'=8,'core'=2] {'y','core'}, dimensions={0} | all-to-all | bytes 65536 | tf_op jit(solution)/shard_map/all_to_all | solution.py:18
  276.5 18.8 %all_to_all.71.chunks_ref = f32[64,4,128]{2,1,0:T(4,128)S(1)} all-to-all(f32[64,4,128]{2,1,0:T(4,128)S(1)} %shard_map.81), channel_id=1, replica_groups=mesh['x'=4,'zh'=8,'zl'=2,'y'=8,'core'=2] {'x','zh','zl'}, dimensions={0} | all-to-all | bytes 262144 | tf_op jit(solution)/shard_map/all_to_all | solution.py:18
  295.3 0.1 shard_map.82
  295.3 12.2 %all_to_all.72 = f32[16,4,128]{2,1,0:T(4,128)S(1)} all-to-all(f32[16,4,128]{2,1,0:T(4,128)S(1)} %shard_map.82), channel_id=1, replica_groups=mesh['x'=4,'zh'=8,'zl'=2,'y'=8,'core'=2] {'y','core'}, dimensions={0} | all-to-all | bytes 65536 | tf_op jit(solution)/shard_map/all_to_all | solution.py:18
  307.5 4.4 %shard_map.83 = (f32[64,128]{1,0:T(8,128)}, f32[64,64]{1,0:T(8,128)}) custom-call(f32[64,128]{1,0:T(8,128)S(1)} %bitcast.62, f32[64,128]{1,0:T(8,128)S(1)} %get-tuple-element.13.filtered_ref), custom_call_target="tpu_custom_call" | custom-call | bytes 65536 | tf_op jit(solution)/shard_map/pallas_call | solution.py:118
  (15 shorter events, 0.2 us)
Async XLA Ops:
  39.4 7.2 %copy-start.1 = (f32[128,64]{0,1:T(8,128)S(1)}, f32[128,64]{0,1:T(8,128)}, u32[]{:S(2)}) copy-start(f32[128,64]{0,1:T(8,128)} %param.6) | copy-start | bytes 98308
  39.4 28.9 %copy-start.2 = (s32[1,1,32]{2,1,0:T(1,128)S(1)}, s32[1,1,32]{2,1,0:T(1,128)}, u32[]{:S(2)}) copy-start(s32[1,1,32]{2,1,0:T(1,128)} %param.9) | copy-start | bytes 388
  39.4 28.9 %copy-start.3 = (s32[1,1,32]{2,1,0:T(1,128)S(1)}, s32[1,1,32]{2,1,0:T(1,128)}, u32[]{:S(2)}) copy-start(s32[1,1,32]{2,1,0:T(1,128)} %param.10) | copy-start | bytes 388
  39.4 30.4 %copy-start = (f32[1,1,32,128,128]{4,3,2,1,0:T(8,128)S(1)}, f32[1,1,32,128,128]{4,3,2,1,0:T(8,128)}, u32[]{:S(2)}) copy-start(f32[1,1,32,128,128]{4,3,2,1,0:T(8,128)} %param.8) | copy-start | bytes 6291460
  39.4 30.4 %all-to-all-start.1 = ((f32[8,8,64,128]{3,2,1,0:T(8,128)}), f32[8,8,64,128]{3,2,1,0:T(8,128)}, u32[]{:S(2)}, u32[]{:S(2)}) async-start(f32[8,8,64,128]{3,2,1,0:T(8,128)} %broadcast_in_dim.15), calls=%async_computation.1 | async-start | bytes 4194304 | tf_op jit(solution)/shard_map/all_to_all | solution.py:18
  81.6 17.9 %all-to-all-start.3 = ((f32[8,64,128]{2,1,0:T(8,128)}), f32[8,64,128]{2,1,0:T(8,128)S(1)}, u32[]{:S(2)}, u32[]{:S(2)}) async-start(f32[8,64,128]{2,1,0:T(8,128)} %bitcast.8), calls=%async_computation.3 | async-start | bytes 524288 | tf_op jit(solution)/shard_map/all_to_all | solution.py:18
  126.0 43.8 %all-to-all-start.5 = ((f32[8,8,64,128]{3,2,1,0:T(8,128)}), f32[8,8,64,128]{3,2,1,0:T(8,128)}, u32[]{:S(2)}, u32[]{:S(2)}) async-start(f32[8,8,64,128]{3,2,1,0:T(8,128)} %broadcast_in_dim.17), calls=%async_computation.5 | async-start | bytes 4194304 | tf_op jit(solution)/shard_map/all_to_all | solution.py:18
  187.8 15.6 %all-to-all-start.7 = ((f32[8,64,128]{2,1,0:T(8,128)}), f32[8,64,128]{2,1,0:T(8,128)S(1)}, u32[]{:S(2)}, u32[]{:S(2)}) async-start(f32[8,64,128]{2,1,0:T(8,128)} %bitcast.16), calls=%async_computation.7 | async-start | bytes 524288 | tf_op jit(solution)/shard_map/all_to_all | solution.py:18
  230.3 30.8 %all-to-all-start.9 = ((f32[8,8,64,128]{3,2,1,0:T(8,128)}), f32[8,8,64,128]{3,2,1,0:T(8,128)}, u32[]{:S(2)}, u32[]{:S(2)}) async-start(f32[8,8,64,128]{3,2,1,0:T(8,128)} %broadcast_in_dim.19), calls=%async_computation.9 | async-start | bytes 4194304 | tf_op jit(solution)/shard_map/all_to_all | solution.py:18

commit v4 on v3

--- a/solution.py
+++ b/solution.py
@@ -46,11 +46,6 @@
 
 def tile_kernel(rows_ref, cols_ref, count_ref, blocks_ref, gathered_ref, out_ref):
     add_slots(rows_ref, cols_ref, count_ref, blocks_ref, gathered_ref, out_ref)
-
-
-def tile_rider_kernel(rows_ref, cols_ref, count_ref, blocks_ref, gathered_ref, rider_ref, out_ref, rider_out_ref):
-    add_slots(rows_ref, cols_ref, count_ref, blocks_ref, gathered_ref, out_ref)
-    rider_out_ref[...] = jnp.sum(rider_ref[...], axis=0)
 
 
 def project_kernel(
@@ -96,7 +91,7 @@
 
 
 def inverse_kernel(nodes_all, folded_ref, out_ref):
-    out_ref[...] = inverse_factor(unfold(folded_ref[...]) / nodes_all)
+    out_ref[...] = inverse_factor(unfold(jnp.sum(folded_ref[...], axis=0)) / nodes_all)
 
 
 def finish_kernel(nodes_all, both_ref, filtered_ref, basis_ref, ritz_ref):
@@ -114,7 +109,7 @@
 VMEM = pl.BlockSpec(memory_space=pltpu.VMEM)
 
 
-def call_kernel(kernel, ins, outs, scratch=(), flops=0):
+def call_kernel(kernel, ins, outs, scratch=()):
     return pl.pallas_call(
         kernel,
         out_shape=[jax.ShapeDtypeStruct(shape, jnp.float32) for shape in outs],
@@ -122,7 +117,6 @@
         out_specs=[VMEM] * len(outs),
         scratch_shapes=list(scratch),
         compiler_params=pltpu.CompilerParams(vmem_limit_bytes=24 * 2**20),
-        cost_estimate=pl.CostEstimate(flops=flops, bytes_accessed=4 * sum(x.size for x in ins), transcendentals=0),
     )(*ins)
 
 
@@ -156,50 +150,52 @@
     rows = (rows % 2) * y_devices + rows // 2
     zh_devices, zl_devices = lax.axis_size("zh"), lax.axis_size("zl")
     cols = block_cols.reshape(-1)
-    along_z = cols % (zh_devices * zl_devices)
-    cols = cols - along_z + (along_z % zl_devices) * zh_devices + along_z // zl_devices
+    z_of = cols % (zh_devices * zl_devices)
+    cols = cols - z_of + (z_of % zl_devices) * zh_devices + z_of // zl_devices
     count = block_counts.reshape(-1)
 
     tile = (rows, cols, count, tile_blocks)
     sums_shape = (col_devices, width, nodes)
-    serial = 5 * 10**9
 
     def gather(value, axes):
         return lax.all_gather(value, axes, axis=0, tiled=False)
 
-    def gather_rows(along_zh):
+    def spread(along_zh):
         return to_all(along_zh, ("x", "zl")).reshape(row_devices, width, nodes)
 
-    def reduce_cols(partial):
-        halves = exchange(partial.reshape(2, -1, nodes), "core").sum(0)
-        return exchange(halves.reshape(y_devices, width, nodes), "y").sum(0) * scale
+    def reduce_core(partial):
+        return exchange(partial.reshape(2, -1, nodes), "core").sum(0).reshape(y_devices, width, nodes)
+
+    def reduce_y(chunks):
+        return exchange(chunks, "y").sum(0) * scale
+
+    def together(*values):
+        return lax.optimization_barrier(values)
 
     def sum_to(chunks, copies):
         return call_kernel(sum_kernel, (chunks,), [(copies, *chunks.shape[1:])])[0]
 
     first = start.T
-    gathered = gather_rows(to_all(first * scale, "zh"))
-    rider = gather(fold(gram(first, first)), COL)
-    partial, rider = call_kernel(tile_rider_kernel, (*tile, gathered, rider), [sums_shape, rider.shape[1:]])
-    once = reduce_cols(partial)
-
-    rider = gather(rider, "x").sum(0).reshape(lax.axis_size("x"), -1, nodes)
-    rider = lax.dynamic_index_in_dim(rider, lax.axis_index("x"), keepdims=False)
+    along_zh, rider = together(to_all(first * scale, "zh"), gather(fold(gram(first, first)), COL))
+    (partial,) = call_kernel(tile_kernel, (*tile, spread(along_zh)), [sums_shape])
+    chunks, rider = together(reduce_core(partial), rider.sum(0))
+    once, rider = together(reduce_y(chunks), gather(rider, "x"))
+
+    rider = rider.sum(0).reshape(2, -1, nodes)
+    half = rider.shape[1]
+    rider = lax.dynamic_index_in_dim(rider, lax.axis_index("core"), keepdims=False)
     along_zh = to_all(jnp.concatenate([once * scale, rider], axis=0), "zh")
-    gathered = gather_rows(along_zh[:, :width])
-    rider = gather(along_zh[:, width:].sum(0), ("x", "zl"))
-    rider = rider.reshape(lax.axis_size("x"), zl_devices, -1, nodes).sum(1).reshape(-1, nodes)
-    (inverse,) = call_kernel(
-        functools.partial(inverse_kernel, nodes_all), (rider,), [(width, width)], flops=serial
-    )
+    gathered, rider = together(spread(along_zh[:, :width]), gather(along_zh[:, width:].sum(0), "core"))
     (partial,) = call_kernel(tile_kernel, (*tile, gathered), [sums_shape])
-    filtered = matmul(inverse, 2.0 * reduce_cols(partial) - first)
+    chunks, rider = together(reduce_core(partial), rider.reshape(2 * half, nodes))
+    (inverse,) = call_kernel(functools.partial(inverse_kernel, nodes_all), (gather(rider, "zl"),), [(width, width)])
+    filtered = matmul(inverse, 2.0 * reduce_y(chunks) - first)
 
     scaled = filtered * scale
-    gathered = gather_rows(to_all(scaled, "zh"))
+    along_zh, own_rows = together(to_all(scaled, "zh"), gather(scaled, COL))
     (projected,) = call_kernel(
         project_kernel,
-        (*tile, gathered, gather(scaled, COL), gram(filtered, filtered)),
+        (*tile, spread(along_zh), own_rows, gram(filtered, filtered)),
         [(width, 2 * width)],
         [pltpu.VMEM(sums_shape, jnp.float32)],
     )

time: 313 us -> 308 us (0.984)
  blocking collectives: 236 us -> 159 us
  waiting for transfers between devices: 22.2 us -> 68.1 us
  starting transfers between devices: 25.5 us -> 49.6 us
    all_to_all x8 -> x6, blocking collectives: 150 us -> 102 us  [exchange(): return lax.all_to_all(chunks, axes, 0, 0, tiled=True)]
    all_to_all x5 -> x7, waiting for transfers between devices: 22.2 us -> 68.1 us  [exchange(): return lax.all_to_all(chunks, axes, 0, 0, tiled=True)]
    all_gather x4 -> x5, blocking collectives: 86.3 us -> 56.9 us  [gather(): return lax.all_gather(value, axes, axis=0, tiled=False)]
    all_to_all x5 -> x7, starting transfers between devices: 25.5 us -> 49.6 us  [exchange(): return lax.all_to_all(chunks, axes, 0, 0, tiled=True)]
  transfers between devices with their start and end apart: 5 -> 7, of which waited for: 4 -> 5; matrix products, arithmetic and copies ran while one was open for 0% -> 0% of each run, Pallas kernels for 1% -> 1%
where the time goes in v4:
time: 308 us; the launch traced here: 307 us
  blocking collectives  159 us (52%)
  waiting for transfers between devices  68.1 us (22%)
  starting transfers between devices  49.6 us (16%)
  Pallas kernels  17.9 us (6%)
  local copies, waits for them, and re-layouts  6.16 us (2%)
    all_to_all x6, blocking collectives, exchange(): return lax.all_to_all(chunks, axes, 0, 0, tiled=True)  102 us
    all_to_all x7, waiting for transfers between devices, exchange(): return lax.all_to_all(chunks, axes, 0, 0, tiled=True)  68.1 us
    all_gather x5, blocking collectives, gather(): return lax.all_gather(value, axes, axis=0, tiled=False)  56.9 us
    all_to_all x7, starting transfers between devices, exchange(): return lax.all_to_all(chunks, axes, 0, 0, tiled=True)  49.6 us
    pallas_call x7, Pallas kernels, call_kernel(): pl.pallas_call(kernel, out_shape=[jax.ShapeDtypeStruct(shape, jnp.float32...  17.9 us
  transfers between devices with their start and end apart: 7, of which 5 were waited for; matrix products, arithmetic and copies ran while one was open for 0% of the time, Pallas kernels for 1%

profile of v4, /device:TPU:1, one launch (start us, length us, event | category | flops | bytes accessed | tf_op | source)
XLA Modules:
  0.0 307.1 jit_solution(7925599148170850554)
XLA Ops:
  0.6 0.7 divide_sqrt_fusion
  1.3 0.8 bitcast_multiply_fusion
  2.1 0.7 broadcast_in_dim.14
  2.8 19.3 %all-to-all-start = ((f32[8,64,128]{2,1,0:T(8,128)}), f32[8,64,128]{2,1,0:T(8,128)S(1)}, u32[]{:S(2)}, u32[]{:S(2)}) async-start(f32[8,64,128]{2,1,0:T(8,128)} %broadcast_in_dim.14), calls=%async_computation | async-start | bytes 524288 | tf_op jit(solution)/shard_map/all_to_all | solution.py:18
  22.1 1.0 fusion.13
  23.1 0.1 pad_maximum_fusion.1
  23.2 19.1 %all-gather = f32[512,128]{1,0:T(8,128)S(1)} all-gather(f32[32,128]{1,0:T(8,128)S(1)} %pad_maximum_fusion.1), channel_id=2, replica_groups=mesh['x'=4,'zh'=8,'zl'=2,'y'=8,'core'=2] {'y','core'}, dimensions={0}, use_global_device_ids=true | all-gather | bytes 278528 | tf_op jit(solution)/shard_map/all_gather | solution.py:161
  42.2 0.0 all-to-all-done
  42.3 1.6 broadcast_in_dim.15
  43.8 5.1 %all-to-all-start.1 = ((f32[8,8,64,128]{3,2,1,0:T(8,128)}), f32[8,8,64,128]{3,2,1,0:T(8,128)}, u32[]{:S(2)}, u32[]{:S(2)}) async-start(f32[8,8,64,128]{3,2,1,0:T(8,128)} %broadcast_in_dim.15), calls=%async_computation.1 | async-start | bytes 4194304 | tf_op jit(solution)/shard_map/all_to_all | solution.py:18
  49.5 0.0 copy-done.2
  49.5 0.0 copy-done.3
  49.6 25.2 %all-to-all-done.1 = f32[8,8,64,128]{3,2,1,0:T(8,128)} async-done(((f32[8,8,64,128]{3,2,1,0:T(8,128)}), f32[8,8,64,128]{3,2,1,0:T(8,128)}, u32[]{:S(2)}, u32[]{:S(2)}) %all-to-all-start.1) | async-done | bytes 2097184 | tf_op jit(solution)/shard_map/all_to_all | solution.py:18
  74.8 3.1 shard_map.77
  77.9 5.9 %all_to_all.65 = f32[2,512,128]{2,1,0:T(8,128)S(1)} all-to-all(f32[2,512,128]{2,1,0:T(8,128)S(1)} %bitcast.59), channel_id=1, replica_groups=mesh['x'=4,'zh'=8,'zl'=2,'y'=8,'core'=2] {'core'}, dimensions={0} | all-to-all | bytes 1048576 | tf_op jit(solution)/shard_map/all_to_all | solution.py:18
  83.8 0.7 reduce_sum.63
  84.5 4.8 %all-to-all-start.3 = ((f32[8,64,128]{2,1,0:T(8,128)}), f32[8,64,128]{2,1,0:T(8,128)S(1)}, u32[]{:S(2)}, u32[]{:S(2)}) async-start(f32[8,64,128]{2,1,0:T(8,128)} %bitcast.8), calls=%async_computation.3 | async-start | bytes 524288 | tf_op jit(solution)/shard_map/all_to_all | solution.py:18
  89.3 9.3 %all-gather.1 = f32[128,128]{1,0:T(8,128)S(1)} all-gather(f32[32,128]{1,0:T(8,128)S(1)} %reduce_sum.64), channel_id=3, replica_groups=mesh['x'=4,'zh'=8,'zl'=2,'y'=8,'core'=2] {'x'}, dimensions={0}, use_global_device_ids=true | all-gather | bytes 81920 | tf_op jit(solution)/shard_map/all_gather | solution.py:161
  98.5 1.8 all-to-all-done.3
  100.5 30.1 %all_to_all.66 = f32[8,80,128]{2,1,0:T(8,128)S(1)} all-to-all(f32[8,80,128]{2,1,0:T(8,128)S(1)} %broadcast_in_dim.16), channel_id=1, replica_groups=mesh['x'=4,'zh'=8,'zl'=2,'y'=8,'core'=2] {'zh'}, dimensions={0} | all-to-all | bytes 655360 | tf_op jit(solution)/shard_map/all_to_all | solution.py:18
  130.6 1.6 broadcast_in_dim.17
  132.2 4.3 %all-to-all-start.5 = ((f32[8,8,64,128]{3,2,1,0:T(8,128)}), f32[8,8,64,128]{3,2,1,0:T(8,128)}, u32[]{:S(2)}, u32[]{:S(2)}) async-start(f32[8,8,64,128]{3,2,1,0:T(8,128)} %broadcast_in_dim.17), calls=%async_computation.5 | async-start | bytes 4194304 | tf_op jit(solution)/shard_map/all_to_all | solution.py:18
  136.5 7.4 %all-gather.2 = f32[32,128]{1,0:T(8,128)S(1)} all-gather(f32[16,128]{1,0:T(8,128)S(1)} %slice_reduce_fusion), channel_id=4, replica_groups=mesh['x'=4,'zh'=8,'zl'=2,'y'=8,'core'=2] {'core'}, dimensions={0}, use_global_device_ids=true | all-gather | bytes 24576 | tf_op jit(solution)/shard_map/all_gather | solution.py:161
  143.9 13.9 %all-to-all-done.5 = f32[8,8,64,128]{3,2,1,0:T(8,128)} async-done(((f32[8,8,64,128]{3,2,1,0:T(8,128)}), f32[8,8,64,128]{3,2,1,0:T(8,128)}, u32[]{:S(2)}, u32[]{:S(2)}) %all-to-all-start.5) | async-done | bytes 2097184 | tf_op jit(solution)/shard_map/all_to_all | solution.py:18
  157.8 3.1 shard_map.78
  160.9 0.0 copy-start.1
  160.9 10.5 %all_to_all.67 = f32[2,512,128]{2,1,0:T(8,128)S(1)} all-to-all(f32[2,512,128]{2,1,0:T(8,128)S(1)} %bitcast.60), channel_id=1, replica_groups=mesh['x'=4,'zh'=8,'zl'=2,'y'=8,'core'=2] {'core'}, dimensions={0} | all-to-all | bytes 1048576 | tf_op jit(solution)/shard_map/all_to_all | solution.py:18
  171.4 0.7 reduce_sum.68
  172.1 5.1 %all-to-all-start.7 = ((f32[8,64,128]{2,1,0:T(8,128)}), f32[8,64,128]{2,1,0:T(8,128)S(1)}, u32[]{:S(2)}, u32[]{:S(2)}) async-start(f32[8,64,128]{2,1,0:T(8,128)} %bitcast.15), calls=%async_computation.7 | async-start | bytes 524288 | tf_op jit(solution)/shard_map/all_to_all | solution.py:18
  177.2 3.3 %all-gather.3 = f32[64,128]{1,0:T(8,128)S(1)} all-gather(f32[32,128]{1,0:T(8,128)S(1)} %all-gather.2), channel_id=5, replica_groups=mesh['x'=4,'zh'=8,'zl'=2,'y'=8,'core'=2] {'zl'}, dimensions={0}, use_global_device_ids=true | all-gather | bytes 49152 | tf_op jit(solution)/shard_map/all_gather | solution.py:161
  180.5 3.4 %shard_map.79 = f32[64,64]{1,0:T(8,128)S(1)} custom-call(f32[2,32,128]{2,1,0:T(8,128)S(1)} %bitcast.63), custom_call_target="tpu_custom_call" | custom-call | tf_op jit(solution)/shard_map/pallas_call | solution.py:113
  183.8 4.5 %all-to-all-done.7 = f32[8,64,128]{2,1,0:T(8,128)S(1)} async-done(((f32[8,64,128]{2,1,0:T(8,128)}), f32[8,64,128]{2,1,0:T(8,128)S(1)}, u32[]{:S(2)}, u32[]{:S(2)}) %all-to-all-start.7) | async-done | bytes 262176 | tf_op jit(solution)/shard_map/all_to_all | solution.py:18
  188.3 0.0 copy-done.1
  188.3 0.2 broadcast_multiply_fusion
  188.5 0.7 broadcast_in_dim.18
  189.2 6.7 %all-to-all-start.8 = ((f32[8,64,128]{2,1,0:T(8,128)}), f32[8,64,128]{2,1,0:T(8,128)S(1)}, u32[]{:S(2)}, u32[]{:S(2)}) async-start(f32[8,64,128]{2,1,0:T(8,128)} %broadcast_in_dim.18), calls=%async_computation.8 | async-start | bytes 524288 | tf_op jit(solution)/shard_map/all_to_all | solution.py:18
  195.9 18.0 %all-gather.4 = f32[1024,128]{1,0:T(8,128)S(1)} all-gather(f32[64,128]{1,0:T(8,128)S(1)} %get-tuple-element.32), channel_id=6, replica_groups=mesh['x'=4,'zh'=8,'zl'=2,'y'=8,'core'=2] {'y','core'}, dimensions={0}, use_global_device_ids=true | all-gather | bytes 557056 | tf_op jit(solution)/shard_map/all_gather | solution.py:161
  213.9 0.0 all-to-all-done.8
  213.9 1.6 broadcast_in_dim.20
  215.5 4.3 %all-to-all-start.9 = ((f32[8,8,64,128]{3,2,1,0:T(8,128)}), f32[8,8,64,128]{3,2,1,0:T(8,128)}, u32[]{:S(2)}, u32[]{:S(2)}) async-start(f32[8,8,64,128]{3,2,1,0:T(8,128)} %broadcast_in_dim.20), calls=%async_computation.9 | async-start | bytes 4194304 | tf_op jit(solution)/shard_map/all_to_all | solution.py:18
  219.8 0.2 fusion.14.gram_ref
  220.0 22.7 %all-to-all-done.9 = f32[8,8,64,128]{3,2,1,0:T(8,128)} async-done(((f32[8,8,64,128]{3,2,1,0:T(8,128)}), f32[8,8,64,128]{3,2,1,0:T(8,128)}, u32[]{:S(2)}, u32[]{:S(2)}) %all-to-all-start.9) | async-done | bytes 2097184 | tf_op jit(solution)/shard_map/all_to_all | solution.py:18
  242.7 4.0 %shard_map.80 = f32[64,128]{1,0:T(8,128)S(1)} custom-call(s32[32]{0:T(128)S(1)} %get-tuple-element.34.rows_ref, s32[32]{0:T(128)S(1)} %get-tuple-element.35.cols_ref, s32[1]{0:T(128)} %bitcast.54.count_ref, f32[32,128,128]{2,1,0:T(8,128)S(1)} %bitcast.57, f32[64,64,128]{2,1,0:T(8,128)} %bitcast.19.gathered_ref, f32[16,64,128]{2,1,0:T(8,128)S(1)} %bitcast.58, ...), custom_call_target="tpu_custom_call" | custom-call | tf_op jit(solution)/shard_map/pallas_call | solution.py:113
  246.7 15.9 %all_to_all.68.chunks_ref = f32[16,4,128]{2,1,0:T(4,128)S(1)} all-to-all(f32[16,4,128]{2,1,0:T(4,128)S(1)} %bitcast.61), channel_id=1, replica_groups=mesh['x'=4,'zh'=8,'zl'=2,'y'=8,'core'=2] {'y','core'}, dimensions={0} | all-to-all | bytes 65536 | tf_op jit(solution)/shard_map/all_to_all | solution.py:18
  262.6 27.9 %all_to_all.69.chunks_ref = f32[64,4,128]{2,1,0:T(4,128)S(1)} all-to-all(f32[64,4,128]{2,1,0:T(4,128)S(1)} %shard_map.81), channel_id=1, replica_groups=mesh['x'=4,'zh'=8,'zl'=2,'y'=8,'core'=2] {'x','zh','zl'}, dimensions={0} | all-to-all | bytes 262144 | tf_op jit(solution)/shard_map/all_to_all | solution.py:18
  290.5 0.1 shard_map.82
  290.6 12.2 %all_to_all.70 = f32[16,4,128]{2,1,0:T(4,128)S(1)} all-to-all(f32[16,4,128]{2,1,0:T(4,128)S(1)} %shard_map.82), channel_id=1, replica_groups=mesh['x'=4,'zh'=8,'zl'=2,'y'=8,'core'=2] {'y','core'}, dimensions={0} | all-to-all | bytes 65536 | tf_op jit(solution)/shard_map/all_to_all | solution.py:18
  302.8 4.4 %shard_map.83 = (f32[64,128]{1,0:T(8,128)}, f32[64,64]{1,0:T(8,128)}) custom-call(f32[64,128]{1,0:T(8,128)S(1)} %bitcast.62, f32[64,128]{1,0:T(8,128)S(1)} %get-tuple-element.33.filtered_ref), custom_call_target="tpu_custom_call" | custom-call | tf_op jit(solution)/shard_map/pallas_call | solution.py:113
  (18 shorter events, 0.2 us)
Async XLA Ops:
  2.8 39.5 %all-to-all-start = ((f32[8,64,128]{2,1,0:T(8,128)}), f32[8,64,128]{2,1,0:T(8,128)S(1)}, u32[]{:S(2)}, u32[]{:S(2)}) async-start(f32[8,64,128]{2,1,0:T(8,128)} %broadcast_in_dim.14), calls=%async_computation | async-start | bytes 524288 | tf_op jit(solution)/shard_map/all_to_all | solution.py:18
  43.8 5.7 %copy-start.2 = (s32[1,1,32]{2,1,0:T(1,128)S(1)}, s32[1,1,32]{2,1,0:T(1,128)}, u32[]{:S(2)}) copy-start(s32[1,1,32]{2,1,0:T(1,128)} %param.9) | copy-start | bytes 388
  43.8 5.7 %copy-start.3 = (s32[1,1,32]{2,1,0:T(1,128)S(1)}, s32[1,1,32]{2,1,0:T(1,128)}, u32[]{:S(2)}) copy-start(s32[1,1,32]{2,1,0:T(1,128)} %param.10) | copy-start | bytes 388
  43.8 31.0 %copy-start = (f32[1,1,32,128,128]{4,3,2,1,0:T(8,128)S(1)}, f32[1,1,32,128,128]{4,3,2,1,0:T(8,128)}, u32[]{:S(2)}) copy-start(f32[1,1,32,128,128]{4,3,2,1,0:T(8,128)} %param.8) | copy-start | bytes 6291460
  43.8 31.0 %all-to-all-start.1 = ((f32[8,8,64,128]{3,2,1,0:T(8,128)}), f32[8,8,64,128]{3,2,1,0:T(8,128)}, u32[]{:S(2)}, u32[]{:S(2)}) async-start(f32[8,8,64,128]{3,2,1,0:T(8,128)} %broadcast_in_dim.15), calls=%async_computation.1 | async-start | bytes 4194304 | tf_op jit(solution)/shard_map/all_to_all | solution.py:18
  84.5 15.9 %all-to-all-start.3 = ((f32[8,64,128]{2,1,0:T(8,128)}), f32[8,64,128]{2,1,0:T(8,128)S(1)}, u32[]{:S(2)}, u32[]{:S(2)}) async-start(f32[8,64,128]{2,1,0:T(8,128)} %bitcast.8), calls=%async_computation.3 | async-start | bytes 524288 | tf_op jit(solution)/shard_map/all_to_all | solution.py:18
  132.2 25.6 %all-to-all-start.5 = ((f32[8,8,64,128]{3,2,1,0:T(8,128)}), f32[8,8,64,128]{3,2,1,0:T(8,128)}, u32[]{:S(2)}, u32[]{:S(2)}) async-start(f32[8,8,64,128]{3,2,1,0:T(8,128)} %broadcast_in_dim.17), calls=%async_computation.5 | async-start | bytes 4194304 | tf_op jit(solution)/shard_map/all_to_all | solution.py:18
  160.9 27.4 %copy-start.1 = (f32[128,64]{0,1:T(8,128)S(1)}, f32[128,64]{0,1:T(8,128)}, u32[]{:S(2)}) copy-start(f32[128,64]{0,1:T(8,128)} %param.6) | copy-start | bytes 98308
  172.1 16.2 %all-to-all-start.7 = ((f32[8,64,128]{2,1,0:T(8,128)}), f32[8,64,128]{2,1,0:T(8,128)S(1)}, u32[]{:S(2)}, u32[]{:S(2)}) async-start(f32[8,64,128]{2,1,0:T(8,128)} %bitcast.15), calls=%async_computation.7 | async-start | bytes 524288 | tf_op jit(solution)/shard_map/all_to_all | solution.py:18
  189.2 24.7 %all-to-all-start.8 = ((f32[8,64,128]{2,1,0:T(8,128)}), f32[8,64,128]{2,1,0:T(8,128)S(1)}, u32[]{:S(2)}, u32[]{:S(2)}) async-start(f32[8,64,128]{2,1,0:T(8,128)} %broadcast_in_dim.18), calls=%async_computation.8 | async-start | bytes 524288 | tf_op jit(solution)/shard_map/all_to_all | solution.py:18
  215.5 27.2 %all-to-all-start.9 = ((f32[8,8,64,128]{3,2,1,0:T(8,128)}), f32[8,8,64,128]{3,2,1,0:T(8,128)}, u32[]{:S(2)}, u32[]{:S(2)}) async-start(f32[8,8,64,128]{3,2,1,0:T(8,128)} %broadcast_in_dim.20), calls=%async_computation.9 | async-start | bytes 4194304 | tf_op jit(solution)/shard_map/all_to_all | solution.py:18

commit v5 on v4

--- a/solution.py
+++ b/solution.py
@@ -8,8 +8,8 @@
 from jax.sharding import Mesh, PartitionSpec as P
 
 HIGHEST = lax.Precision.HIGHEST
-AXES = ("x", "zh", "zl", "y", "core")
-ROW = ("x", "zh", "zl")
+AXES = ("x", "z", "y", "core")
+ROW = ("x", "z")
 COL = ("y", "core")
 CONTRACT_LAST = (((1,), (1,)), ((), ()))
 
@@ -91,7 +91,7 @@
 
 
 def inverse_kernel(nodes_all, folded_ref, out_ref):
-    out_ref[...] = inverse_factor(unfold(jnp.sum(folded_ref[...], axis=0)) / nodes_all)
+    out_ref[...] = inverse_factor(unfold(folded_ref[...]) / nodes_all)
 
 
 def finish_kernel(nodes_all, both_ref, filtered_ref, basis_ref, ritz_ref):
@@ -148,10 +148,7 @@
     rows = block_rows.reshape(-1)
     y_devices = lax.axis_size("y")
     rows = (rows % 2) * y_devices + rows // 2
-    zh_devices, zl_devices = lax.axis_size("zh"), lax.axis_size("zl")
     cols = block_cols.reshape(-1)
-    z_of = cols % (zh_devices * zl_devices)
-    cols = cols - z_of + (z_of % zl_devices) * zh_devices + z_of // zl_devices
     count = block_counts.reshape(-1)
 
     tile = (rows, cols, count, tile_blocks)
@@ -160,8 +157,8 @@
     def gather(value, axes):
         return lax.all_gather(value, axes, axis=0, tiled=False)
 
-    def spread(along_zh):
-        return to_all(along_zh, ("x", "zl")).reshape(row_devices, width, nodes)
+    def spread(along_z):
+        return to_all(along_z, "x").reshape(row_devices, width, nodes)
 
     def reduce_core(partial):
         return exchange(partial.reshape(2, -1, nodes), "core").sum(0).reshape(y_devices, width, nodes)
@@ -176,26 +173,27 @@
         return call_kernel(sum_kernel, (chunks,), [(copies, *chunks.shape[1:])])[0]
 
     first = start.T
-    along_zh, rider = together(to_all(first * scale, "zh"), gather(fold(gram(first, first)), COL))
-    (partial,) = call_kernel(tile_kernel, (*tile, spread(along_zh)), [sums_shape])
+    along_z = gather(first * scale, "z")
+    gathered, rider = together(spread(along_z), gather(fold(gram(first, first)), COL))
+    (partial,) = call_kernel(tile_kernel, (*tile, gathered), [sums_shape])
     chunks, rider = together(reduce_core(partial), rider.sum(0))
     once, rider = together(reduce_y(chunks), gather(rider, "x"))
 
     rider = rider.sum(0).reshape(2, -1, nodes)
     half = rider.shape[1]
     rider = lax.dynamic_index_in_dim(rider, lax.axis_index("core"), keepdims=False)
-    along_zh = to_all(jnp.concatenate([once * scale, rider], axis=0), "zh")
-    gathered, rider = together(spread(along_zh[:, :width]), gather(along_zh[:, width:].sum(0), "core"))
+    along_z = gather(jnp.concatenate([once * scale, rider], axis=0), "z")
+    gathered, rider = together(spread(along_z[:, :width]), gather(along_z[:, width:].sum(0), "core"))
     (partial,) = call_kernel(tile_kernel, (*tile, gathered), [sums_shape])
     chunks, rider = together(reduce_core(partial), rider.reshape(2 * half, nodes))
-    (inverse,) = call_kernel(functools.partial(inverse_kernel, nodes_all), (gather(rider, "zl"),), [(width, width)])
+    (inverse,) = call_kernel(functools.partial(inverse_kernel, nodes_all), (rider,), [(width, width)])
     filtered = matmul(inverse, 2.0 * reduce_y(chunks) - first)
 
     scaled = filtered * scale
-    along_zh, own_rows = together(to_all(scaled, "zh"), gather(scaled, COL))
+    gathered, own_rows = together(spread(gather(scaled, "z")), gather(scaled, COL))
     (projected,) = call_kernel(
         project_kernel,
-        (*tile, spread(along_zh), own_rows, gram(filtered, filtered)),
+        (*tile, gathered, own_rows, gram(filtered, filtered)),
         [(width, 2 * width)],
         [pltpu.VMEM(sums_shape, jnp.float32)],
     )
@@ -209,7 +207,7 @@
 
 
 def solution(mesh):
-    sizes = (4, 8, 2, 8, 2)
+    sizes = (4, 16, 8, 2)
     return jax.shard_map(
         shards,
         mesh=Mesh(mesh.devices.reshape(sizes), AXES),

time: 308 us -> 293 us (0.951)
  blocking collectives: 159 us -> 215 us
  waiting for transfers between devices: 68.1 us -> 18.4 us
  starting transfers between devices: 49.6 us -> 30 us
    all_gather x5 -> x7, blocking collectives: 56.9 us -> 155 us  [gather(): return lax.all_gather(value, axes, axis=0, tiled=False)]
    all_to_all x7 -> x6, waiting for transfers between devices: 68.1 us -> 18.4 us  [exchange(): return lax.all_to_all(chunks, axes, 0, 0, tiled=True)]
    all_to_all x6 -> x4, blocking collectives: 102 us -> 59.4 us  [exchange(): return lax.all_to_all(chunks, axes, 0, 0, tiled=True)]
    all_to_all x7 -> x6, starting transfers between devices: 49.6 us -> 30 us  [exchange(): return lax.all_to_all(chunks, axes, 0, 0, tiled=True)]
  transfers between devices with their start and end apart: 7 -> 6, of which waited for: 5 -> 4; matrix products, arithmetic and copies ran while one was open for 0% -> 0% of each run, Pallas kernels for 1% -> 1%
where the time goes in v5:
time: 293 us; the launch traced here: 292 us
  blocking collectives  215 us (73%)
  starting transfers between devices  30 us (10%)
  Pallas kernels  18.8 us (6%)
  waiting for transfers between devices  18.4 us (6%)
  local copies, waits for them, and re-layouts  4.77 us (2%)
  other arithmetic  3.06 us (1%)
    all_gather x7, blocking collectives, gather(): return lax.all_gather(value, axes, axis=0, tiled=False)  155 us
    all_to_all x4, blocking collectives, exchange(): return lax.all_to_all(chunks, axes, 0, 0, tiled=True)  59.4 us
    all_to_all x6, starting transfers between devices, exchange(): return lax.all_to_all(chunks, axes, 0, 0, tiled=True)  30 us
    pallas_call x7, Pallas kernels, call_kernel(): pl.pallas_call(kernel, out_shape=[jax.ShapeDtypeStruct(shape, jnp.float32...  18.8 us
    all_to_all x6, waiting for transfers between devices, exchange(): return lax.all_to_all(chunks, axes, 0, 0, tiled=True)  18.4 us
  transfers between devices with their start and end apart: 6, of which 4 were waited for; matrix products, arithmetic and copies ran while one was open for 0% of the time, Pallas kernels for 1%

profile of v5, /device:TPU:1, one launch (start us, length us, event | category | flops | bytes accessed | tf_op | source)
XLA Modules:
  0.0 291.7 jit_solution(8727383598147564371)
XLA Ops:
  0.6 0.7 divide_sqrt_fusion
  1.3 0.8 bitcast_multiply_fusion
  2.1 39.2 %all-gather = f32[1024,128]{1,0:T(8,128)S(1)} all-gather(f32[64,128]{1,0:T(8,128)S(1)} %bitcast_multiply_fusion), channel_id=2, replica_groups=mesh['x'=4,'z'=16,'y'=8,'core'=2] {'z'}, dimensions={0}, use_global_device_ids=true | all-gather | bytes 557056 | tf_op jit(solution)/shard_map/all_gather | solution.py:158
  41.3 1.6 broadcast_in_dim.6
  42.8 0.0 copy-start.2
  42.8 0.0 copy-start.3
  42.8 0.0 copy-start
  42.8 0.0 copy-start.1
  42.8 4.6 %all-to-all-start = ((f32[4,16,64,128]{3,2,1,0:T(8,128)}), f32[4,16,64,128]{3,2,1,0:T(8,128)}, u32[]{:S(2)}, u32[]{:S(2)}) async-start(f32[4,16,64,128]{3,2,1,0:T(8,128)} %broadcast_in_dim.6), calls=%async_computation | async-start | bytes 4194304 | tf_op jit(solution)/shard_map/all_to_all | solution.py:18
  48.1 0.0 copy-done.2
  48.1 0.2 fusion.9
  48.3 0.1 pad_maximum_fusion.1
  48.4 25.4 %all-gather.1 = f32[512,128]{1,0:T(8,128)S(1)} all-gather(f32[32,128]{1,0:T(8,128)S(1)} %pad_maximum_fusion.1), channel_id=3, replica_groups=mesh['x'=4,'z'=16,'y'=8,'core'=2] {'y','core'}, dimensions={0}, use_global_device_ids=true | all-gather | bytes 278528 | tf_op jit(solution)/shard_map/all_gather | solution.py:158
  73.8 0.0 copy-done.3
  73.8 0.0 all-to-all-done
  73.8 0.0 copy-done
  73.8 0.0 copy-done.1
  73.8 3.9 %shard_map.77 = f32[16,64,128]{2,1,0:T(8,128)} custom-call(s32[32]{0:T(128)S(1)} %fusion.6.rows_ref, s32[32]{0:T(128)S(1)} %bitcast.58, s32[1]{0:T(128)} %bitcast.48.count_ref, f32[32,128,128]{2,1,0:T(8,128)S(1)} %bitcast.51, f32[64,64,128]{2,1,0:T(8,128)} %bitcast.6.gathered_ref), custom_call_target="tpu_custom_call" | custom-call | tf_op jit(solution)/shard_map/pallas_call | solution.py:113
  77.7 4.4 %all-to-all-start.1 = ((f32[2,512,128]{2,1,0:T(8,128)}), f32[2,512,128]{2,1,0:T(8,128)S(1)}, u32[]{:S(2)}, u32[]{:S(2)}) async-start(f32[2,512,128]{2,1,0:T(8,128)} %bitcast.8), calls=%async_computation.1 | async-start | bytes 1048576 | tf_op jit(solution)/shard_map/all_to_all | solution.py:18
  82.2 1.3 all-to-all-done.1
  83.5 0.7 reduce_sum.63
  84.2 6.8 %all-to-all-start.2 = ((f32[8,64,128]{2,1,0:T(8,128)}), f32[8,64,128]{2,1,0:T(8,128)S(1)}, u32[]{:S(2)}, u32[]{:S(2)}) async-start(f32[8,64,128]{2,1,0:T(8,128)} %bitcast.9), calls=%async_computation.2 | async-start | bytes 524288 | tf_op jit(solution)/shard_map/all_to_all | solution.py:18
  91.0 9.3 %all-gather.2 = f32[128,128]{1,0:T(8,128)S(1)} all-gather(f32[32,128]{1,0:T(8,128)S(1)} %reduce_sum.64), channel_id=4, replica_groups=mesh['x'=4,'z'=16,'y'=8,'core'=2] {'x'}, dimensions={0}, use_global_device_ids=true | all-gather | bytes 81920 | tf_op jit(solution)/shard_map/all_gather | solution.py:158
  100.3 1.8 all-to-all-done.2
  102.2 23.1 %all-gather.3 = f32[1280,128]{1,0:T(8,128)S(1)} all-gather(f32[80,128]{1,0:T(8,128)S(1)} %pad_maximum_fusion), channel_id=5, replica_groups=mesh['x'=4,'z'=16,'y'=8,'core'=2] {'z'}, dimensions={0}, use_global_device_ids=true | all-gather | bytes 696320 | tf_op jit(solution)/shard_map/all_gather | solution.py:158
  125.4 1.6 broadcast_in_dim.7
  126.9 4.4 %all-to-all-start.3 = ((f32[4,16,64,128]{3,2,1,0:T(8,128)}), f32[4,16,64,128]{3,2,1,0:T(8,128)}, u32[]{:S(2)}, u32[]{:S(2)}) async-start(f32[4,16,64,128]{3,2,1,0:T(8,128)} %broadcast_in_dim.7), calls=%async_computation.3 | async-start | bytes 4194304 | tf_op jit(solution)/shard_map/all_to_all | solution.py:18
  131.4 10.0 %all-gather.4 = f32[32,128]{1,0:T(8,128)S(1)} all-gather(f32[16,128]{1,0:T(8,128)S(1)} %slice_reduce_fusion), channel_id=6, replica_groups=mesh['x'=4,'z'=16,'y'=8,'core'=2] {'core'}, dimensions={0}, use_global_device_ids=true | all-gather | bytes 24576 | tf_op jit(solution)/shard_map/all_gather | solution.py:158
  141.5 7.5 %all-to-all-done.3 = f32[4,16,64,128]{3,2,1,0:T(8,128)} async-done(((f32[4,16,64,128]{3,2,1,0:T(8,128)}), f32[4,16,64,128]{3,2,1,0:T(8,128)}, u32[]{:S(2)}, u32[]{:S(2)}) %all-to-all-start.3) | async-done | bytes 2097184 | tf_op jit(solution)/shard_map/all_to_all | solution.py:18
  149.0 3.1 %shard_map.78 = f32[16,64,128]{2,1,0:T(8,128)S(1)} custom-call(s32[32]{0:T(128)S(1)} %fusion.6.rows_ref, s32[32]{0:T(128)S(1)} %bitcast.59, s32[1]{0:T(128)} %bitcast.49.count_ref, f32[32,128,128]{2,1,0:T(8,128)S(1)} %bitcast.52, f32[64,64,128]{2,1,0:T(8,128)} %bitcast.14.gathered_ref), custom_call_target="tpu_custom_call" | custom-call | tf_op jit(solution)/shard_map/pallas_call | solution.py:113
  152.0 13.5 %all_to_all.50 = f32[2,512,128]{2,1,0:T(8,128)S(1)} all-to-all(f32[2,512,128]{2,1,0:T(8,128)S(1)} %bitcast.55), channel_id=1, replica_groups=mesh['x'=4,'z'=16,'y'=8,'core'=2] {'core'}, dimensions={0} | all-to-all | bytes 1048576 | tf_op jit(solution)/shard_map/all_to_all | solution.py:18
  165.6 0.7 reduce_sum.68
  166.3 5.3 %all-to-all-start.5 = ((f32[8,64,128]{2,1,0:T(8,128)}), f32[8,64,128]{2,1,0:T(8,128)S(1)}, u32[]{:S(2)}, u32[]{:S(2)}) async-start(f32[8,64,128]{2,1,0:T(8,128)} %bitcast.17), calls=%async_computation.5 | async-start | bytes 524288 | tf_op jit(solution)/shard_map/all_to_all | solution.py:18
  171.6 3.4 %shard_map.79 = f32[64,64]{1,0:T(8,128)S(1)} custom-call(f32[32,128]{1,0:T(8,128)S(1)} %all-gather.4), custom_call_target="tpu_custom_call" | custom-call | tf_op jit(solution)/shard_map/pallas_call | solution.py:113
  174.9 7.7 %all-to-all-done.5 = f32[8,64,128]{2,1,0:T(8,128)S(1)} async-done(((f32[8,64,128]{2,1,0:T(8,128)}), f32[8,64,128]{2,1,0:T(8,128)S(1)}, u32[]{:S(2)}, u32[]{:S(2)}) %all-to-all-start.5) | async-done | bytes 262176 | tf_op jit(solution)/shard_map/all_to_all | solution.py:18
  182.7 0.2 broadcast_multiply_fusion
  182.8 23.1 %all-gather.5 = f32[1024,128]{1,0:T(8,128)S(1)} all-gather(f32[64,128]{1,0:T(8,128)S(1)} %get-tuple-element.32), channel_id=7, replica_groups=mesh['x'=4,'z'=16,'y'=8,'core'=2] {'z'}, dimensions={0}, use_global_device_ids=true | all-gather | bytes 557056 | tf_op jit(solution)/shard_map/all_gather | solution.py:158
  205.9 1.6 broadcast_in_dim.8
  207.5 4.4 %all-to-all-start.6 = ((f32[4,16,64,128]{3,2,1,0:T(8,128)}), f32[4,16,64,128]{3,2,1,0:T(8,128)}, u32[]{:S(2)}, u32[]{:S(2)}) async-start(f32[4,16,64,128]{3,2,1,0:T(8,128)} %broadcast_in_dim.8), calls=%async_computation.6 | async-start | bytes 4194304 | tf_op jit(solution)/shard_map/all_to_all | solution.py:18
  212.0 0.2 fusion.10.gram_ref
  212.2 25.2 %all-gather.6 = f32[1024,128]{1,0:T(8,128)S(1)} all-gather(f32[64,128]{1,0:T(8,128)S(1)} %get-tuple-element.32), channel_id=8, replica_groups=mesh['x'=4,'z'=16,'y'=8,'core'=2] {'y','core'}, dimensions={0}, use_global_device_ids=true | all-gather | bytes 557056 | tf_op jit(solution)/shard_map/all_gather | solution.py:158
  237.4 0.0 all-to-all-done.6
  237.4 4.0 %shard_map.80 = f32[64,128]{1,0:T(8,128)S(1)} custom-call(s32[32]{0:T(128)S(1)} %fusion.6.rows_ref, s32[32]{0:T(128)S(1)} %bitcast.60, s32[1]{0:T(128)} %bitcast.50.count_ref, f32[32,128,128]{2,1,0:T(8,128)S(1)} %bitcast.53, f32[64,64,128]{2,1,0:T(8,128)} %bitcast.20.gathered_ref, f32[16,64,128]{2,1,0:T(8,128)S(1)} %bitcast.54, f32[64,64]{1,0:T(8,128)S(1)} %fusion.10.gram_ref), custom_call_target="tpu_custom_call" | custom-call | tf_op jit(solution)/shard_map/pallas_call | solution.py:113
  241.4 12.0 %all_to_all.51.chunks_ref = f32[16,4,128]{2,1,0:T(4,128)S(1)} all-to-all(f32[16,4,128]{2,1,0:T(4,128)S(1)} %bitcast.56), channel_id=1, replica_groups=mesh['x'=4,'z'=16,'y'=8,'core'=2] {'y','core'}, dimensions={0} | all-to-all | bytes 65536 | tf_op jit(solution)/shard_map/all_to_all | solution.py:18
  253.4 21.7 %all_to_all.52.chunks_ref = f32[64,4,128]{2,1,0:T(4,128)S(1)} all-to-all(f32[64,4,128]{2,1,0:T(4,128)S(1)} %shard_map.81), channel_id=1, replica_groups=mesh['x'=4,'z'=16,'y'=8,'core'=2] {'x','z'}, dimensions={0} | all-to-all | bytes 262144 | tf_op jit(solution)/shard_map/all_to_all | solution.py:18
  275.1 0.1 shard_map.82
  275.2 12.2 %all_to_all.53 = f32[16,4,128]{2,1,0:T(4,128)S(1)} all-to-all(f32[16,4,128]{2,1,0:T(4,128)S(1)} %shard_map.82), channel_id=1, replica_groups=mesh['x'=4,'z'=16,'y'=8,'core'=2] {'y','core'}, dimensions={0} | all-to-all | bytes 65536 | tf_op jit(solution)/shard_map/all_to_all | solution.py:18
  287.4 4.4 %shard_map.83 = (f32[64,128]{1,0:T(8,128)}, f32[64,64]{1,0:T(8,128)}) custom-call(f32[64,128]{1,0:T(8,128)S(1)} %bitcast.57, f32[64,128]{1,0:T(8,128)S(1)} %get-tuple-element.33.filtered_ref), custom_call_target="tpu_custom_call" | custom-call | tf_op jit(solution)/shard_map/pallas_call | solution.py:113
  (13 shorter events, 0.2 us)
Async XLA Ops:
  42.8 5.3 %copy-start.2 = (f32[128,64]{0,1:T(8,128)S(1)}, f32[128,64]{0,1:T(8,128)}, u32[]{:S(2)}) copy-start(f32[128,64]{0,1:T(8,128)} %param.6) | copy-start | bytes 98308
  42.8 31.0 %copy-start.3 = (s32[1,1,32]{2,1,0:T(1,128)S(1)}, s32[1,1,32]{2,1,0:T(1,128)}, u32[]{:S(2)}) copy-start(s32[1,1,32]{2,1,0:T(1,128)} %param.9) | copy-start | bytes 388
  42.8 31.0 %copy-start = (f32[1,1,32,128,128]{4,3,2,1,0:T(8,128)S(1)}, f32[1,1,32,128,128]{4,3,2,1,0:T(8,128)}, u32[]{:S(2)}) copy-start(f32[1,1,32,128,128]{4,3,2,1,0:T(8,128)} %param.8) | copy-start | bytes 6291460
  42.8 31.0 %copy-start.1 = (s32[1,1,32]{2,1,0:T(1,128)S(1)}, s32[1,1,32]{2,1,0:T(1,128)}, u32[]{:S(2)}) copy-start(s32[1,1,32]{2,1,0:T(1,128)} %param.10) | copy-start | bytes 388
  42.8 31.0 %all-to-all-start = ((f32[4,16,64,128]{3,2,1,0:T(8,128)}), f32[4,16,64,128]{3,2,1,0:T(8,128)}, u32[]{:S(2)}, u32[]{:S(2)}) async-start(f32[4,16,64,128]{3,2,1,0:T(8,128)} %broadcast_in_dim.6), calls=%async_computation | async-start | bytes 4194304 | tf_op jit(solution)/shard_map/all_to_all | solution.py:18
  77.7 5.8 %all-to-all-start.1 = ((f32[2,512,128]{2,1,0:T(8,128)}), f32[2,512,128]{2,1,0:T(8,128)S(1)}, u32[]{:S(2)}, u32[]{:S(2)}) async-start(f32[2,512,128]{2,1,0:T(8,128)} %bitcast.8), calls=%async_computation.1 | async-start | bytes 1048576 | tf_op jit(solution)/shard_map/all_to_all | solution.py:18
  84.2 17.9 %all-to-all-start.2 = ((f32[8,64,128]{2,1,0:T(8,128)}), f32[8,64,128]{2,1,0:T(8,128)S(1)}, u32[]{:S(2)}, u32[]{:S(2)}) async-start(f32[8,64,128]{2,1,0:T(8,128)} %bitcast.9), calls=%async_computation.2 | async-start | bytes 524288 | tf_op jit(solution)/shard_map/all_to_all | solution.py:18
  126.9 22.0 %all-to-all-start.3 = ((f32[4,16,64,128]{3,2,1,0:T(8,128)}), f32[4,16,64,128]{3,2,1,0:T(8,128)}, u32[]{:S(2)}, u32[]{:S(2)}) async-start(f32[4,16,64,128]{3,2,1,0:T(8,128)} %broadcast_in_dim.7), calls=%async_computation.3 | async-start | bytes 4194304 | tf_op jit(solution)/shard_map/all_to_all | solution.py:18
  166.3 16.3 %all-to-all-start.5 = ((f32[8,64,128]{2,1,0:T(8,128)}), f32[8,64,128]{2,1,0:T(8,128)S(1)}, u32[]{:S(2)}, u32[]{:S(2)}) async-start(f32[8,64,128]{2,1,0:T(8,128)} %bitcast.17), calls=%async_computation.5 | async-start | bytes 524288 | tf_op jit(solution)/shard_map/all_to_all | solution.py:18
  207.5 29.9 %all-to-all-start.6 = ((f32[4,16,64,128]{3,2,1,0:T(8,128)}), f32[4,16,64,128]{3,2,1,0:T(8,128)}, u32[]{:S(2)}, u32[]{:S(2)}) async-start(f32[4,16,64,128]{3,2,1,0:T(8,128)} %broadcast_in_dim.8), calls=%async_computation.6 | async-start | bytes 4194304 | tf_op jit(solution)/shard_map/all_to_all | solution.py:18

commit v6 on v5

--- a/solution.py
+++ b/solution.py
@@ -8,8 +8,8 @@
 from jax.sharding import Mesh, PartitionSpec as P
 
 HIGHEST = lax.Precision.HIGHEST
-AXES = ("x", "z", "y", "core")
-ROW = ("x", "z")
+AXES = ("x", "za", "zb", "y", "core")
+ROW = ("x", "za", "zb")
 COL = ("y", "core")
 CONTRACT_LAST = (((1,), (1,)), ((), ()))
 
@@ -148,7 +148,10 @@
     rows = block_rows.reshape(-1)
     y_devices = lax.axis_size("y")
     rows = (rows % 2) * y_devices + rows // 2
+    za_devices, zb_devices = lax.axis_size("za"), lax.axis_size("zb")
     cols = block_cols.reshape(-1)
+    z_of = cols % (za_devices * zb_devices)
+    cols = cols - z_of + (z_of % zb_devices) * za_devices + z_of // zb_devices
     count = block_counts.reshape(-1)
 
     tile = (rows, cols, count, tile_blocks)
@@ -157,6 +160,10 @@
     def gather(value, axes):
         return lax.all_gather(value, axes, axis=0, tiled=False)
 
+    def gather_z(value):
+        along_z = gather(gather(value, "za"), "zb")
+        return along_z.reshape(-1, *value.shape)
+
     def spread(along_z):
         return to_all(along_z, "x").reshape(row_devices, width, nodes)
 
@@ -173,7 +180,7 @@
         return call_kernel(sum_kernel, (chunks,), [(copies, *chunks.shape[1:])])[0]
 
     first = start.T
-    along_z = gather(first * scale, "z")
+    along_z = gather_z(first * scale)
     gathered, rider = together(spread(along_z), gather(fold(gram(first, first)), COL))
     (partial,) = call_kernel(tile_kernel, (*tile, gathered), [sums_shape])
     chunks, rider = together(reduce_core(partial), rider.sum(0))
@@ -182,7 +189,7 @@
     rider = rider.sum(0).reshape(2, -1, nodes)
     half = rider.shape[1]
     rider = lax.dynamic_index_in_dim(rider, lax.axis_index("core"), keepdims=False)
-    along_z = gather(jnp.concatenate([once * scale, rider], axis=0), "z")
+    along_z = gather_z(jnp.concatenate([once * scale, rider], axis=0))
     gathered, rider = together(spread(along_z[:, :width]), gather(along_z[:, width:].sum(0), "core"))
     (partial,) = call_kernel(tile_kernel, (*tile, gathered), [sums_shape])
     chunks, rider = together(reduce_core(partial), rider.reshape(2 * half, nodes))
@@ -190,7 +197,7 @@
     filtered = matmul(inverse, 2.0 * reduce_y(chunks) - first)
 
     scaled = filtered * scale
-    gathered, own_rows = together(spread(gather(scaled, "z")), gather(scaled, COL))
+    gathered, own_rows = together(spread(gather_z(scaled)), gather(scaled, COL))
     (projected,) = call_kernel(
         project_kernel,
         (*tile, gathered, own_rows, gram(filtered, filtered)),
@@ -207,7 +214,7 @@
 
 
 def solution(mesh):
-    sizes = (4, 16, 8, 2)
+    sizes = (4, 4, 4, 8, 2)
     return jax.shard_map(
         shards,
         mesh=Mesh(mesh.devices.reshape(sizes), AXES),

time: 293 us -> 310 us (1.058)
  blocking collectives: 215 us -> 227 us
  waiting for transfers between devices: 18.4 us -> 22.8 us
    all_gather x7 -> x10, blocking collectives: 155 us -> 165 us  [gather(): return lax.all_gather(value, axes, axis=0, tiled=False)]
    all_to_all x6, waiting for transfers between devices: 18.4 us -> 22.8 us  [exchange(): return lax.all_to_all(chunks, axes, 0, 0, tiled=True)]
where the time goes in v6:
time: 310 us; the launch traced here: 309 us
  blocking collectives  227 us (73%)
  starting transfers between devices  30.6 us (10%)
  waiting for transfers between devices  22.8 us (7%)
  Pallas kernels  18.8 us (6%)
  local copies, waits for them, and re-layouts  4.77 us (2%)
    all_gather x10, blocking collectives, gather(): return lax.all_gather(value, axes, axis=0, tiled=False)  165 us
    all_to_all x4, blocking collectives, exchange(): return lax.all_to_all(chunks, axes, 0, 0, tiled=True)  61.3 us
    all_to_all x6, starting transfers between devices, exchange(): return lax.all_to_all(chunks, axes, 0, 0, tiled=True)  30.6 us
    all_to_all x6, waiting for transfers between devices, exchange(): return lax.all_to_all(chunks, axes, 0, 0, tiled=True)  22.8 us
    pallas_call x7, Pallas kernels, call_kernel(): pl.pallas_call(kernel, out_shape=[jax.ShapeDtypeStruct(shape, jnp.float32...  18.8 us
  transfers between devices with their start and end apart: 6, of which 4 were waited for; matrix products, arithmetic and copies ran while one was open for 0% of the time, Pallas kernels for 1%

profile of v6, /device:TPU:1, one launch (start us, length us, event | category | flops | bytes accessed | tf_op | source)
XLA Modules:
  0.0 308.8 jit_solution(197415933728358498)
XLA Ops:
  0.6 0.7 divide_sqrt_fusion
  1.3 0.8 bitcast_multiply_fusion
  2.1 27.9 %all-gather = f32[256,128]{1,0:T(8,128)S(1)} all-gather(f32[64,128]{1,0:T(8,128)S(1)} %bitcast_multiply_fusion), channel_id=2, replica_groups=mesh['x'=4,'za'=4,'zb'=4,'y'=8,'core'=2] {'za'}, dimensions={0}, use_global_device_ids=true | all-gather | bytes 163840 | tf_op jit(solution)/shard_map/all_gather | solution.py:161
  29.9 13.6 %all-gather.1 = f32[16,64,128]{2,1,0:T(8,128)S(1)} all-gather(f32[4,64,128]{2,1,0:T(8,128)S(1)} %bitcast.66), channel_id=3, replica_groups=mesh['x'=4,'za'=4,'zb'=4,'y'=8,'core'=2] {'zb'}, dimensions={0}, use_global_device_ids=true | all-gather | bytes 655360 | tf_op jit(solution)/shard_map/all_gather | solution.py:161
  43.6 1.6 broadcast_in_dim.22
  45.1 0.0 copy-start.2
  45.1 4.6 %all-to-all-start = ((f32[4,16,64,128]{3,2,1,0:T(8,128)}), f32[4,16,64,128]{3,2,1,0:T(8,128)}, u32[]{:S(2)}, u32[]{:S(2)}) async-start(f32[4,16,64,128]{3,2,1,0:T(8,128)} %broadcast_in_dim.22), calls=%async_computation | async-start | bytes 4194304 | tf_op jit(solution)/shard_map/all_to_all | solution.py:18
  50.4 0.0 copy-done.1
  50.4 0.2 fusion.13
  50.6 0.1 pad_maximum_fusion.1
  50.7 24.2 %all-gather.2 = f32[512,128]{1,0:T(8,128)S(1)} all-gather(f32[32,128]{1,0:T(8,128)S(1)} %pad_maximum_fusion.1), channel_id=4, replica_groups=mesh['x'=4,'za'=4,'zb'=4,'y'=8,'core'=2] {'y','core'}, dimensions={0}, use_global_device_ids=true | all-gather | bytes 278528 | tf_op jit(solution)/shard_map/all_gather | solution.py:161
  74.9 0.0 copy-done.2
  74.9 0.0 copy-done.3
  74.9 0.0 all-to-all-done
  74.9 0.0 copy-done
  74.9 3.9 %shard_map.77 = f32[16,64,128]{2,1,0:T(8,128)} custom-call(s32[32]{0:T(128)S(1)} %get-tuple-element.34.rows_ref, s32[32]{0:T(128)S(1)} %get-tuple-element.35.cols_ref, s32[1]{0:T(128)} %bitcast.54.count_ref, f32[32,128,128]{2,1,0:T(8,128)S(1)} %bitcast.57, f32[64,64,128]{2,1,0:T(8,128)} %bitcast.6.gathered_ref), custom_call_target="tpu_custom_call" | custom-call | tf_op jit(solution)/shard_map/pallas_call | solution.py:113
  78.8 5.6 %all-to-all-start.1 = ((f32[2,512,128]{2,1,0:T(8,128)}), f32[2,512,128]{2,1,0:T(8,128)S(1)}, u32[]{:S(2)}, u32[]{:S(2)}) async-start(f32[2,512,128]{2,1,0:T(8,128)} %bitcast.8), calls=%async_computation.1 | async-start | bytes 1048576 | tf_op jit(solution)/shard_map/all_to_all | solution.py:18
  84.5 1.3 all-to-all-done.1
  85.8 0.7 reduce_sum.63
  86.5 6.6 %all-to-all-start.2 = ((f32[8,64,128]{2,1,0:T(8,128)}), f32[8,64,128]{2,1,0:T(8,128)S(1)}, u32[]{:S(2)}, u32[]{:S(2)}) async-start(f32[8,64,128]{2,1,0:T(8,128)} %bitcast.9), calls=%async_computation.2 | async-start | bytes 524288 | tf_op jit(solution)/shard_map/all_to_all | solution.py:18
  93.2 9.3 %all-gather.3 = f32[128,128]{1,0:T(8,128)S(1)} all-gather(f32[32,128]{1,0:T(8,128)S(1)} %reduce_sum.64), channel_id=5, replica_groups=mesh['x'=4,'za'=4,'zb'=4,'y'=8,'core'=2] {'x'}, dimensions={0}, use_global_device_ids=true | all-gather | bytes 81920 | tf_op jit(solution)/shard_map/all_gather | solution.py:161
  102.5 1.8 all-to-all-done.2
  104.4 15.8 %all-gather.4 = f32[320,128]{1,0:T(8,128)S(1)} all-gather(f32[80,128]{1,0:T(8,128)S(1)} %pad_maximum_fusion), channel_id=6, replica_groups=mesh['x'=4,'za'=4,'zb'=4,'y'=8,'core'=2] {'za'}, dimensions={0}, use_global_device_ids=true | all-gather | bytes 204800 | tf_op jit(solution)/shard_map/all_gather | solution.py:161
  120.1 15.3 %all-gather.5 = f32[16,80,128]{2,1,0:T(8,128)S(1)} all-gather(f32[4,80,128]{2,1,0:T(8,128)S(1)} %bitcast.65), channel_id=7, replica_groups=mesh['x'=4,'za'=4,'zb'=4,'y'=8,'core'=2] {'zb'}, dimensions={0}, use_global_device_ids=true | all-gather | bytes 819200 | tf_op jit(solution)/shard_map/all_gather | solution.py:161
  135.5 1.6 broadcast_in_dim.23
  137.0 4.4 %all-to-all-start.3 = ((f32[4,16,64,128]{3,2,1,0:T(8,128)}), f32[4,16,64,128]{3,2,1,0:T(8,128)}, u32[]{:S(2)}, u32[]{:S(2)}) async-start(f32[4,16,64,128]{3,2,1,0:T(8,128)} %broadcast_in_dim.23), calls=%async_computation.3 | async-start | bytes 4194304 | tf_op jit(solution)/shard_map/all_to_all | solution.py:18
  141.5 7.8 %all-gather.6 = f32[32,128]{1,0:T(8,128)S(1)} all-gather(f32[16,128]{1,0:T(8,128)S(1)} %slice_reduce_fusion), channel_id=8, replica_groups=mesh['x'=4,'za'=4,'zb'=4,'y'=8,'core'=2] {'core'}, dimensions={0}, use_global_device_ids=true | all-gather | bytes 24576 | tf_op jit(solution)/shard_map/all_gather | solution.py:161
  149.3 12.0 %all-to-all-done.3 = f32[4,16,64,128]{3,2,1,0:T(8,128)} async-done(((f32[4,16,64,128]{3,2,1,0:T(8,128)}), f32[4,16,64,128]{3,2,1,0:T(8,128)}, u32[]{:S(2)}, u32[]{:S(2)}) %all-to-all-start.3) | async-done | bytes 2097184 | tf_op jit(solution)/shard_map/all_to_all | solution.py:18
  161.3 3.1 shard_map.78
  164.3 11.3 %all_to_all.50 = f32[2,512,128]{2,1,0:T(8,128)S(1)} all-to-all(f32[2,512,128]{2,1,0:T(8,128)S(1)} %bitcast.61), channel_id=1, replica_groups=mesh['x'=4,'za'=4,'zb'=4,'y'=8,'core'=2] {'core'}, dimensions={0} | all-to-all | bytes 1048576 | tf_op jit(solution)/shard_map/all_to_all | solution.py:18
  175.7 0.7 reduce_sum.68
  176.4 4.9 %all-to-all-start.5 = ((f32[8,64,128]{2,1,0:T(8,128)}), f32[8,64,128]{2,1,0:T(8,128)S(1)}, u32[]{:S(2)}, u32[]{:S(2)}) async-start(f32[8,64,128]{2,1,0:T(8,128)} %bitcast.17), calls=%async_computation.5 | async-start | bytes 524288 | tf_op jit(solution)/shard_map/all_to_all | solution.py:18
  181.3 3.4 %shard_map.79 = f32[64,64]{1,0:T(8,128)S(1)} custom-call(f32[32,128]{1,0:T(8,128)S(1)} %all-gather.6), custom_call_target="tpu_custom_call" | custom-call | tf_op jit(solution)/shard_map/pallas_call | solution.py:113
  184.7 7.7 %all-to-all-done.5 = f32[8,64,128]{2,1,0:T(8,128)S(1)} async-done(((f32[8,64,128]{2,1,0:T(8,128)}), f32[8,64,128]{2,1,0:T(8,128)S(1)}, u32[]{:S(2)}, u32[]{:S(2)}) %all-to-all-start.5) | async-done | bytes 262176 | tf_op jit(solution)/shard_map/all_to_all | solution.py:18
  192.4 0.2 broadcast_multiply_fusion
  192.6 14.9 %all-gather.7 = f32[256,128]{1,0:T(8,128)S(1)} all-gather(f32[64,128]{1,0:T(8,128)S(1)} %get-tuple-element.32), channel_id=9, replica_groups=mesh['x'=4,'za'=4,'zb'=4,'y'=8,'core'=2] {'za'}, dimensions={0}, use_global_device_ids=true | all-gather | bytes 163840 | tf_op jit(solution)/shard_map/all_gather | solution.py:161
  207.5 14.2 %all-gather.8 = f32[16,64,128]{2,1,0:T(8,128)S(1)} all-gather(f32[4,64,128]{2,1,0:T(8,128)S(1)} %bitcast.67), channel_id=10, replica_groups=mesh['x'=4,'za'=4,'zb'=4,'y'=8,'core'=2] {'zb'}, dimensions={0}, use_global_device_ids=true | all-gather | bytes 655360 | tf_op jit(solution)/shard_map/all_gather | solution.py:161
  221.6 1.6 broadcast_in_dim.25
  223.2 4.4 %all-to-all-start.6 = ((f32[4,16,64,128]{3,2,1,0:T(8,128)}), f32[4,16,64,128]{3,2,1,0:T(8,128)}, u32[]{:S(2)}, u32[]{:S(2)}) async-start(f32[4,16,64,128]{3,2,1,0:T(8,128)} %broadcast_in_dim.25), calls=%async_computation.6 | async-start | bytes 4194304 | tf_op jit(solution)/shard_map/all_to_all | solution.py:18
  227.6 0.2 fusion.14.gram_ref
  227.8 22.5 %all-gather.9 = f32[1024,128]{1,0:T(8,128)S(1)} all-gather(f32[64,128]{1,0:T(8,128)S(1)} %get-tuple-element.32), channel_id=11, replica_groups=mesh['x'=4,'za'=4,'zb'=4,'y'=8,'core'=2] {'y','core'}, dimensions={0}, use_global_device_ids=true | all-gather | bytes 557056 | tf_op jit(solution)/shard_map/all_gather | solution.py:161
  250.4 0.0 all-to-all-done.6
  250.4 4.0 %shard_map.80 = f32[64,128]{1,0:T(8,128)S(1)} custom-call(s32[32]{0:T(128)S(1)} %get-tuple-element.34.rows_ref, s32[32]{0:T(128)S(1)} %get-tuple-element.35.cols_ref, s32[1]{0:T(128)} %bitcast.56.count_ref, f32[32,128,128]{2,1,0:T(8,128)S(1)} %bitcast.59, f32[64,64,128]{2,1,0:T(8,128)} %bitcast.20.gathered_ref, f32[16,64,128]{2,1,0:T(8,128)S(1)} %bitcast.60, ...), custom_call_target="tpu_custom_call" | custom-call | tf_op jit(solution)/shard_map/pallas_call | solution.py:113
  254.4 14.5 %all_to_all.51.chunks_ref = f32[16,4,128]{2,1,0:T(4,128)S(1)} all-to-all(f32[16,4,128]{2,1,0:T(4,128)S(1)} %bitcast.62), channel_id=1, replica_groups=mesh['x'=4,'za'=4,'zb'=4,'y'=8,'core'=2] {'y','core'}, dimensions={0} | all-to-all | bytes 65536 | tf_op jit(solution)/shard_map/all_to_all | solution.py:18
  268.9 23.3 %all_to_all.52.chunks_ref = f32[64,4,128]{2,1,0:T(4,128)S(1)} all-to-all(f32[64,4,128]{2,1,0:T(4,128)S(1)} %shard_map.81), channel_id=1, replica_groups=mesh['x'=4,'za'=4,'zb'=4,'y'=8,'core'=2] {'x','za','zb'}, dimensions={0} | all-to-all | bytes 262144 | tf_op jit(solution)/shard_map/all_to_all | solution.py:18
  292.2 0.1 shard_map.82
  292.3 12.2 %all_to_all.53 = f32[16,4,128]{2,1,0:T(4,128)S(1)} all-to-all(f32[16,4,128]{2,1,0:T(4,128)S(1)} %shard_map.82), channel_id=1, replica_groups=mesh['x'=4,'za'=4,'zb'=4,'y'=8,'core'=2] {'y','core'}, dimensions={0} | all-to-all | bytes 65536 | tf_op jit(solution)/shard_map/all_to_all | solution.py:18
  304.4 4.4 %shard_map.83 = (f32[64,128]{1,0:T(8,128)}, f32[64,64]{1,0:T(8,128)}) custom-call(f32[64,128]{1,0:T(8,128)S(1)} %bitcast.63, f32[64,128]{1,0:T(8,128)S(1)} %get-tuple-element.33.filtered_ref), custom_call_target="tpu_custom_call" | custom-call | tf_op jit(solution)/shard_map/pallas_call | solution.py:113
  (16 shorter events, 0.2 us)
Async XLA Ops:
  45.1 5.3 %copy-start.1 = (f32[128,64]{0,1:T(8,128)S(1)}, f32[128,64]{0,1:T(8,128)}, u32[]{:S(2)}) copy-start(f32[128,64]{0,1:T(8,128)} %param.6) | copy-start | bytes 98308
  45.1 29.8 %copy-start.2 = (s32[1,1,32]{2,1,0:T(1,128)S(1)}, s32[1,1,32]{2,1,0:T(1,128)}, u32[]{:S(2)}) copy-start(s32[1,1,32]{2,1,0:T(1,128)} %param.9) | copy-start | bytes 388
  45.1 29.8 %copy-start.3 = (s32[1,1,32]{2,1,0:T(1,128)S(1)}, s32[1,1,32]{2,1,0:T(1,128)}, u32[]{:S(2)}) copy-start(s32[1,1,32]{2,1,0:T(1,128)} %param.10) | copy-start | bytes 388
  45.1 29.8 %copy-start = (f32[1,1,32,128,128]{4,3,2,1,0:T(8,128)S(1)}, f32[1,1,32,128,128]{4,3,2,1,0:T(8,128)}, u32[]{:S(2)}) copy-start(f32[1,1,32,128,128]{4,3,2,1,0:T(8,128)} %param.8) | copy-start | bytes 6291460
  45.1 29.8 %all-to-all-start = ((f32[4,16,64,128]{3,2,1,0:T(8,128)}), f32[4,16,64,128]{3,2,1,0:T(8,128)}, u32[]{:S(2)}, u32[]{:S(2)}) async-start(f32[4,16,64,128]{3,2,1,0:T(8,128)} %broadcast_in_dim.22), calls=%async_computation | async-start | bytes 4194304 | tf_op jit(solution)/shard_map/all_to_all | solution.py:18
  78.8 7.0 %all-to-all-start.1 = ((f32[2,512,128]{2,1,0:T(8,128)}), f32[2,512,128]{2,1,0:T(8,128)S(1)}, u32[]{:S(2)}, u32[]{:S(2)}) async-start(f32[2,512,128]{2,1,0:T(8,128)} %bitcast.8), calls=%async_computation.1 | async-start | bytes 1048576 | tf_op jit(solution)/shard_map/all_to_all | solution.py:18
  86.5 17.7 %all-to-all-start.2 = ((f32[8,64,128]{2,1,0:T(8,128)}), f32[8,64,128]{2,1,0:T(8,128)S(1)}, u32[]{:S(2)}, u32[]{:S(2)}) async-start(f32[8,64,128]{2,1,0:T(8,128)} %bitcast.9), calls=%async_computation.2 | async-start | bytes 524288 | tf_op jit(solution)/shard_map/all_to_all | solution.py:18
  137.0 24.3 %all-to-all-start.3 = ((f32[4,16,64,128]{3,2,1,0:T(8,128)}), f32[4,16,64,128]{3,2,1,0:T(8,128)}, u32[]{:S(2)}, u32[]{:S(2)}) async-start(f32[4,16,64,128]{3,2,1,0:T(8,128)} %broadcast_in_dim.23), calls=%async_computation.3 | async-start | bytes 4194304 | tf_op jit(solution)/shard_map/all_to_all | solution.py:18
  176.4 16.0 %all-to-all-start.5 = ((f32[8,64,128]{2,1,0:T(8,128)}), f32[8,64,128]{2,1,0:T(8,128)S(1)}, u32[]{:S(2)}, u32[]{:S(2)}) async-start(f32[8,64,128]{2,1,0:T(8,128)} %bitcast.17), calls=%async_computation.5 | async-start | bytes 524288 | tf_op jit(solution)/shard_map/all_to_all | solution.py:18
  223.2 27.2 %all-to-all-start.6 = ((f32[4,16,64,128]{3,2,1,0:T(8,128)}), f32[4,16,64,128]{3,2,1,0:T(8,128)}, u32[]{:S(2)}, u32[]{:S(2)}) async-start(f32[4,16,64,128]{3,2,1,0:T(8,128)} %broadcast_in_dim.25), calls=%async_computation.6 | async-start | bytes 4194304 | tf_op jit(solution)/shard_map/all_to_all | solution.py:18

commit v7 on v5

--- a/solution.py
+++ b/solution.py
@@ -36,9 +36,12 @@
     sums_ref[...] = jnp.zeros_like(sums_ref)
     count = count_ref[0]
     width = sums_ref.shape[1]
+    pieces = gathered_ref.shape[1] // width
     for slot in range(blocks_ref.shape[0]):
         live = (slot < count).astype(jnp.float32)
-        high, low = split(gathered_ref[cols_ref[slot]] * live)
+        col = cols_ref[slot]
+        first_row = pl.multiple_of((col % pieces) * width, width)
+        high, low = split(gathered_ref[col // pieces, pl.ds(first_row, width)] * live)
         block_high, block_low = split(blocks_ref[slot])
         both = dot_pieces(jnp.concatenate([high, low], axis=0), block_high)
         sums_ref[rows_ref[slot]] += both[:width] + both[width:] + dot_pieces(high, block_low)
@@ -46,6 +49,26 @@
 
 def tile_kernel(rows_ref, cols_ref, count_ref, blocks_ref, gathered_ref, out_ref):
     add_slots(rows_ref, cols_ref, count_ref, blocks_ref, gathered_ref, out_ref)
+
+
+def tile_rider_kernel(rows_ref, cols_ref, count_ref, blocks_ref, gathered_ref, out_ref, rider_ref):
+    add_slots(rows_ref, cols_ref, count_ref, blocks_ref, gathered_ref, out_ref)
+    pieces_end = gathered_ref.shape[1] - rider_ref.shape[0]
+    rider_ref[...] = jnp.sum(gathered_ref[:, pieces_end:], axis=0)
+
+
+def scale_kernel(degrees_hbm, vectors_hbm, scale_ref, scaled_ref, degrees_ref, vectors_ref, sems):
+    fetches = [
+        pltpu.make_async_copy(degrees_hbm, degrees_ref, sems.at[0]),
+        pltpu.make_async_copy(vectors_hbm, vectors_ref, sems.at[1]),
+    ]
+    for fetch in fetches:
+        fetch.start()
+    for fetch in fetches:
+        fetch.wait()
+    scale = jnp.sqrt(16.0 / degrees_ref[...].astype(jnp.float32))
+    scale_ref[...] = scale
+    scaled_ref[...] = vectors_ref[...] * scale
 
 
 def project_kernel(
@@ -53,11 +76,10 @@
 ):
     add_slots(rows_ref, cols_ref, count_ref, blocks_ref, gathered_ref, sums_ref)
     row_blocks, width, _ = sums_ref.shape
-    half = row_blocks // 2
     products = jnp.zeros((2 * width, 2 * width), jnp.float32)
     for piece in range(row_blocks):
         left = jnp.concatenate(split(own_ref[piece]), axis=0)
-        right = jnp.concatenate(split(sums_ref[(piece % 2) * half + piece // 2]), axis=0)
+        right = jnp.concatenate(split(sums_ref[piece]), axis=0)
         products += dot_pieces(left, right)
     total = products[:width, :width] + products[:width, width:] + products[width:, :width] + products[width:, width:]
     out_ref[...] = jnp.concatenate([total, gram_ref[...]], axis=1)
@@ -107,13 +129,15 @@
 
 SMEM = pl.BlockSpec(memory_space=pltpu.SMEM)
 VMEM = pl.BlockSpec(memory_space=pltpu.VMEM)
-
-
-def call_kernel(kernel, ins, outs, scratch=()):
+HBM = pl.BlockSpec(memory_space=pltpu.HBM)
+
+
+def call_kernel(kernel, ins, outs, scratch=(), in_specs=None):
     return pl.pallas_call(
         kernel,
         out_shape=[jax.ShapeDtypeStruct(shape, jnp.float32) for shape in outs],
-        in_specs=[SMEM if value.dtype == jnp.int32 else VMEM for value in ins],
+        in_specs=in_specs
+        or [SMEM if value.dtype == jnp.int32 and value.ndim == 1 else VMEM for value in ins],
         out_specs=[VMEM] * len(outs),
         scratch_shapes=list(scratch),
         compiler_params=pltpu.CompilerParams(vmem_limit_bytes=24 * 2**20),
@@ -143,11 +167,8 @@
     col_devices = lax.axis_size(COL)
     nodes, width = start.shape
     nodes_all = nodes * row_devices * col_devices
-    scale = jnp.sqrt(16.0 / degrees.astype(jnp.float32))[None, :]
     tile_blocks = blocks.reshape(blocks.shape[2:])
     rows = block_rows.reshape(-1)
-    y_devices = lax.axis_size("y")
-    rows = (rows % 2) * y_devices + rows // 2
     cols = block_cols.reshape(-1)
     count = block_counts.reshape(-1)
 
@@ -157,14 +178,9 @@
     def gather(value, axes):
         return lax.all_gather(value, axes, axis=0, tiled=False)
 
-    def spread(along_z):
-        return to_all(along_z, "x").reshape(row_devices, width, nodes)
-
-    def reduce_core(partial):
-        return exchange(partial.reshape(2, -1, nodes), "core").sum(0).reshape(y_devices, width, nodes)
-
-    def reduce_y(chunks):
-        return exchange(chunks, "y").sum(0) * scale
+    def reduce_cols(partial):
+        along_y = exchange(partial.reshape(lax.axis_size("y"), -1, nodes), "y").sum(0)
+        return exchange(along_y.reshape(lax.axis_size("core"), width, nodes), "core").sum(0) * scale
 
     def together(*values):
         return lax.optimization_barrier(values)
@@ -173,24 +189,30 @@
         return call_kernel(sum_kernel, (chunks,), [(copies, *chunks.shape[1:])])[0]
 
     first = start.T
-    along_z = gather(first * scale, "z")
-    gathered, rider = together(spread(along_z), gather(fold(gram(first, first)), COL))
+    scale, scaled = call_kernel(
+        scale_kernel,
+        (degrees[None], first),
+        [(1, nodes), (width, nodes)],
+        [pltpu.VMEM((1, nodes), jnp.int32), pltpu.VMEM((width, nodes), jnp.float32), pltpu.SemaphoreType.DMA((2,))],
+        [HBM, HBM],
+    )
+    along_z = gather(scaled, "z").reshape(-1, nodes)
+    rider = gather(fold(gram(first, first)), COL).sum(0).reshape(lax.axis_size("core"), -1, nodes)
+    half_shape = rider.shape[1:]
+    rider = lax.dynamic_index_in_dim(rider, lax.axis_index("core"), keepdims=False)
+    gathered, rider = together(to_all(along_z, "x"), rider)
     (partial,) = call_kernel(tile_kernel, (*tile, gathered), [sums_shape])
-    chunks, rider = together(reduce_core(partial), rider.sum(0))
-    once, rider = together(reduce_y(chunks), gather(rider, "x"))
-
-    rider = rider.sum(0).reshape(2, -1, nodes)
-    half = rider.shape[1]
-    rider = lax.dynamic_index_in_dim(rider, lax.axis_index("core"), keepdims=False)
+    once = reduce_cols(partial)
+
     along_z = gather(jnp.concatenate([once * scale, rider], axis=0), "z")
-    gathered, rider = together(spread(along_z[:, :width]), gather(along_z[:, width:].sum(0), "core"))
-    (partial,) = call_kernel(tile_kernel, (*tile, gathered), [sums_shape])
-    chunks, rider = together(reduce_core(partial), rider.reshape(2 * half, nodes))
+    along_z = jnp.concatenate([along_z[:, :width].reshape(-1, nodes), along_z[:, width:].sum(0)], axis=0)
+    partial, rider = call_kernel(tile_rider_kernel, (*tile, to_all(along_z, "x")), [sums_shape, half_shape])
+    rider = gather(rider, "core").reshape(-1, nodes)
     (inverse,) = call_kernel(functools.partial(inverse_kernel, nodes_all), (rider,), [(width, width)])
-    filtered = matmul(inverse, 2.0 * reduce_y(chunks) - first)
+    filtered = matmul(inverse, 2.0 * reduce_cols(partial) - first)
 
     scaled = filtered * scale
-    gathered, own_rows = together(spread(gather(scaled, "z")), gather(scaled, COL))
+    gathered, own_rows = together(to_all(gather(scaled, "z").reshape(-1, nodes), "x"), gather(scaled, COL))
     (projected,) = call_kernel(
         project_kernel,
         (*tile, gathered, own_rows, gram(filtered, filtered)),

time: 293 us -> 290 us (0.990)
  blocking collectives: 215 us -> 252 us
  waiting for transfers between devices: 18.4 us -> 0.01 us
  starting transfers between devices: 30 us -> 12.5 us
    all_to_all x4 -> x7, blocking collectives: 59.4 us -> 107 us  [exchange(): return lax.all_to_all(chunks, axes, 0, 0, tiled=True)]
    all_to_all x6 -> x3, waiting for transfers between devices: 18.4 us -> 0.01 us  [exchange(): return lax.all_to_all(chunks, axes, 0, 0, tiled=True)]
    all_to_all x6 -> x3, starting transfers between devices: 30 us -> 12.5 us  [exchange(): return lax.all_to_all(chunks, axes, 0, 0, tiled=True)]
    all_gather x7 -> x6, blocking collectives: 155 us -> 145 us  [gather(): return lax.all_gather(value, axes, axis=0, tiled=False)]
    pallas_call x7 -> x8, Pallas kernels: 18.8 us -> 17.6 us  [call_kernel(): pl.pallas_call(kernel, out_shape=[jax.ShapeDtypeStruct(shape, jnp.float32...]
  transfers between devices with their start and end apart: 6 -> 3, of which waited for: 4 -> 0; matrix products, arithmetic and copies ran while one was open for 0% -> 0% of each run, Pallas kernels for 1% -> 1%
where the time goes in v7:
time: 290 us; the launch traced here: 289 us
  blocking collectives  252 us (87%)
  Pallas kernels  17.6 us (6%)
  starting transfers between devices  12.5 us (4%)
  local copies, waits for them, and re-layouts  4.48 us (2%)
    all_gather x6, blocking collectives, gather(): return lax.all_gather(value, axes, axis=0, tiled=False)  145 us
    all_to_all x7, blocking collectives, exchange(): return lax.all_to_all(chunks, axes, 0, 0, tiled=True)  107 us
    pallas_call x8, Pallas kernels, call_kernel(): pl.pallas_call(kernel, out_shape=[jax.ShapeDtypeStruct(shape, jnp.float32...  17.6 us
    all_to_all x3, starting transfers between devices, exchange(): return lax.all_to_all(chunks, axes, 0, 0, tiled=True)  12.5 us
  transfers between devices with their start and end apart: 3, of which 0 were waited for; matrix products, arithmetic and copies ran while one was open for 0% of the time, Pallas kernels for 1%

profile of v7, /device:TPU:1, one launch (start us, length us, event | category | flops | bytes accessed | tf_op | source)
XLA Modules:
  0.0 288.7 jit_solution(2478101745269393028)
XLA Ops:
  0.6 0.0 copy-start.1
  0.6 0.7 copy-done.1
  1.4 0.0 copy-start.5
  1.4 0.7 copy-done.5
  2.0 0.1 shard_map.77
  2.1 39.2 %all-gather = f32[1024,128]{1,0:T(8,128)S(1)} all-gather(f32[64,128]{1,0:T(8,128)S(1)} %get-tuple-element.12), channel_id=2, replica_groups=mesh['x'=4,'z'=16,'y'=8,'core'=2] {'z'}, dimensions={0}, use_global_device_ids=true | all-gather | bytes 557056 | tf_op jit(solution)/shard_map/all_gather | solution.py:179
  41.3 1.4 broadcast_in_dim.25
  42.8 0.0 copy-start.2
  42.8 0.0 copy-start
  42.8 0.0 copy-start.3
  42.8 0.0 copy-start.4
  42.8 4.6 %all-to-all-start = ((f32[4,1024,128]{2,1,0:T(8,128)}), f32[4,1024,128]{2,1,0:T(8,128)}, u32[]{:S(2)}, u32[]{:S(2)}) async-start(f32[4,1024,128]{2,1,0:T(8,128)} %broadcast_in_dim.25), calls=%async_computation | async-start | bytes 4194304 | tf_op jit(solution)/shard_map/all_to_all | solution.py:18
  48.0 0.0 copy-done.2
  48.0 0.2 fusion.9
  48.2 0.1 pad_maximum_fusion.2
  48.3 25.4 %all-gather.1 = f32[512,128]{1,0:T(8,128)S(1)} all-gather(f32[32,128]{1,0:T(8,128)S(1)} %pad_maximum_fusion.2), channel_id=3, replica_groups=mesh['x'=4,'z'=16,'y'=8,'core'=2] {'y','core'}, dimensions={0}, use_global_device_ids=true | all-gather | bytes 278528 | tf_op jit(solution)/shard_map/all_gather | solution.py:179
  73.8 0.0 all-to-all-done.gathered_ref
  73.8 0.0 copy-done
  73.8 0.0 copy-done.3
  73.8 0.0 copy-done.4
  73.8 3.0 %shard_map.78 = f32[16,64,128]{2,1,0:T(8,128)S(1)} custom-call(s32[32]{0:T(128)S(1)} %bitcast.43, s32[32]{0:T(128)S(1)} %bitcast.46, s32[1]{0:T(128)} %bitcast.32.count_ref, f32[32,128,128]{2,1,0:T(8,128)S(1)} %bitcast.35, f32[4,1024,128]{2,1,0:T(8,128)} %all-to-all-done.gathered_ref), custom_call_target="tpu_custom_call" | custom-call | tf_op jit(solution)/shard_map/pallas_call | solution.py:136
  76.8 16.9 %all_to_all.50 = f32[8,128,128]{2,1,0:T(8,128)S(1)} all-to-all(f32[8,128,128]{2,1,0:T(8,128)S(1)} %bitcast.39), channel_id=1, replica_groups=mesh['x'=4,'z'=16,'y'=8,'core'=2] {'y'}, dimensions={0} | all-to-all | bytes 1048576 | tf_op jit(solution)/shard_map/all_to_all | solution.py:18
  93.7 8.9 %all_to_all.51 = f32[2,64,128]{2,1,0:T(8,128)S(1)} all-to-all(f32[2,64,128]{2,1,0:T(8,128)S(1)} %bitcast.56), channel_id=1, replica_groups=mesh['x'=4,'z'=16,'y'=8,'core'=2] {'core'}, dimensions={0} | all-to-all | bytes 131072 | tf_op jit(solution)/shard_map/all_to_all | solution.py:18
  102.6 22.9 %all-gather.2 = f32[1280,128]{1,0:T(8,128)S(1)} all-gather(f32[80,128]{1,0:T(8,128)S(1)} %pad_maximum_fusion.1), channel_id=4, replica_groups=mesh['x'=4,'z'=16,'y'=8,'core'=2] {'z'}, dimensions={0}, use_global_device_ids=true | all-gather | bytes 696320 | tf_op jit(solution)/shard_map/all_gather | solution.py:179
  125.7 0.1 broadcast_in_dim.26
  125.8 23.5 %all_to_all.52.gathered_ref = f32[4,1040,128]{2,1,0:T(8,128)S(1)} all-to-all(f32[4,1040,128]{2,1,0:T(8,128)S(1)} %broadcast_in_dim.26), channel_id=1, replica_groups=mesh['x'=4,'z'=16,'y'=8,'core'=2] {'x'}, dimensions={0} | all-to-all | bytes 4259840 | tf_op jit(solution)/shard_map/all_to_all | solution.py:18
  149.3 2.8 shard_map.79
  152.1 3.5 %all-to-all-start.4 = ((f32[8,128,128]{2,1,0:T(8,128)}), f32[8,128,128]{2,1,0:T(8,128)S(1)}, u32[]{:S(2)}, u32[]{:S(2)}) async-start(f32[8,128,128]{2,1,0:T(8,128)} %bitcast.14), calls=%async_computation.4 | async-start | bytes 1048576 | tf_op jit(solution)/shard_map/all_to_all | solution.py:18
  155.6 9.9 %all-gather.3.folded_ref = f32[32,128]{1,0:T(8,128)S(1)} all-gather(f32[16,128]{1,0:T(8,128)S(1)} %get-tuple-element.16), channel_id=5, replica_groups=mesh['x'=4,'z'=16,'y'=8,'core'=2] {'core'}, dimensions={0}, use_global_device_ids=true | all-gather | bytes 24576 | tf_op jit(solution)/shard_map/all_gather | solution.py:179
  165.5 3.4 %shard_map.80 = f32[64,64]{1,0:T(8,128)S(1)} custom-call(f32[32,128]{1,0:T(8,128)S(1)} %all-gather.3.folded_ref), custom_call_target="tpu_custom_call" | custom-call | tf_op jit(solution)/shard_map/pallas_call | solution.py:136
  168.9 0.0 all-to-all-done.4
  168.9 11.8 %all_to_all.53 = f32[2,64,128]{2,1,0:T(8,128)S(1)} all-to-all(f32[2,64,128]{2,1,0:T(8,128)S(1)} %bitcast.57), channel_id=1, replica_groups=mesh['x'=4,'z'=16,'y'=8,'core'=2] {'core'}, dimensions={0} | all-to-all | bytes 131072 | tf_op jit(solution)/shard_map/all_to_all | solution.py:18
  180.7 0.2 broadcast_multiply_fusion
  180.9 24.1 %all-gather.4 = f32[1024,128]{1,0:T(8,128)S(1)} all-gather(f32[64,128]{1,0:T(8,128)S(1)} %get-tuple-element.24), channel_id=6, replica_groups=mesh['x'=4,'z'=16,'y'=8,'core'=2] {'z'}, dimensions={0}, use_global_device_ids=true | all-gather | bytes 557056 | tf_op jit(solution)/shard_map/all_gather | solution.py:179
  205.0 1.4 broadcast_in_dim.28
  206.4 4.4 %all-to-all-start.6 = ((f32[4,1024,128]{2,1,0:T(8,128)}), f32[4,1024,128]{2,1,0:T(8,128)}, u32[]{:S(2)}, u32[]{:S(2)}) async-start(f32[4,1024,128]{2,1,0:T(8,128)} %broadcast_in_dim.28), calls=%async_computation.6 | async-start | bytes 4194304 | tf_op jit(solution)/shard_map/all_to_all | solution.py:18
  210.9 0.2 fusion.10.gram_ref
  211.1 23.1 %all-gather.5 = f32[1024,128]{1,0:T(8,128)S(1)} all-gather(f32[64,128]{1,0:T(8,128)S(1)} %get-tuple-element.24), channel_id=7, replica_groups=mesh['x'=4,'z'=16,'y'=8,'core'=2] {'y','core'}, dimensions={0}, use_global_device_ids=true | all-gather | bytes 557056 | tf_op jit(solution)/shard_map/all_gather | solution.py:179
  234.2 0.0 all-to-all-done.6.gathered_ref
  234.2 3.9 %shard_map.81 = f32[64,128]{1,0:T(8,128)S(1)} custom-call(s32[32]{0:T(128)S(1)} %bitcast.45, s32[32]{0:T(128)S(1)} %bitcast.48, s32[1]{0:T(128)} %bitcast.34.count_ref, f32[32,128,128]{2,1,0:T(8,128)S(1)} %bitcast.37, f32[4,1024,128]{2,1,0:T(8,128)} %all-to-all-done.6.gathered_ref, f32[16,64,128]{2,1,0:T(8,128)S(1)} %bitcast.38, f32[64,64]{1,0:T(8,128)S(1)} %fusion.10.gram_ref), custom_call_target="tpu_custom_call" | custom-call | tf_op jit(solution)/shard_map/pallas_call | solution.py:136
  238.1 13.9 %all_to_all.54.chunks_ref = f32[16,4,128]{2,1,0:T(4,128)S(1)} all-to-all(f32[16,4,128]{2,1,0:T(4,128)S(1)} %bitcast.41), channel_id=1, replica_groups=mesh['x'=4,'z'=16,'y'=8,'core'=2] {'y','core'}, dimensions={0} | all-to-all | bytes 65536 | tf_op jit(solution)/shard_map/all_to_all | solution.py:18
  252.0 20.1 %all_to_all.55.chunks_ref = f32[64,4,128]{2,1,0:T(4,128)S(1)} all-to-all(f32[64,4,128]{2,1,0:T(4,128)S(1)} %shard_map.82), channel_id=1, replica_groups=mesh['x'=4,'z'=16,'y'=8,'core'=2] {'x','z'}, dimensions={0} | all-to-all | bytes 262144 | tf_op jit(solution)/shard_map/all_to_all | solution.py:18
  272.2 0.1 shard_map.83
  272.2 12.2 %all_to_all.56 = f32[16,4,128]{2,1,0:T(4,128)S(1)} all-to-all(f32[16,4,128]{2,1,0:T(4,128)S(1)} %shard_map.83), channel_id=1, replica_groups=mesh['x'=4,'z'=16,'y'=8,'core'=2] {'y','core'}, dimensions={0} | all-to-all | bytes 65536 | tf_op jit(solution)/shard_map/all_to_all | solution.py:18
  284.4 4.4 %shard_map.84 = (f32[64,128]{1,0:T(8,128)}, f32[64,64]{1,0:T(8,128)}) custom-call(f32[64,128]{1,0:T(8,128)S(1)} %bitcast.42, f32[64,128]{1,0:T(8,128)S(1)} %get-tuple-element.25.filtered_ref), custom_call_target="tpu_custom_call" | custom-call | tf_op jit(solution)/shard_map/pallas_call | solution.py:136
  (13 shorter events, 0.3 us)
Async XLA Ops:
  0.6 0.8 copy-start.1
  1.4 0.7 copy-start.5
  42.8 5.3 %copy-start.2 = (f32[128,64]{0,1:T(8,128)S(1)}, f32[128,64]{0,1:T(8,128)}, u32[]{:S(2)}) copy-start(f32[128,64]{0,1:T(8,128)} %param.6) | copy-start | bytes 98308
  42.8 31.0 %copy-start = (f32[1,1,32,128,128]{4,3,2,1,0:T(8,128)S(1)}, f32[1,1,32,128,128]{4,3,2,1,0:T(8,128)}, u32[]{:S(2)}) copy-start(f32[1,1,32,128,128]{4,3,2,1,0:T(8,128)} %param.8) | copy-start | bytes 6291460
  42.8 31.0 %copy-start.3 = (s32[1,1,32]{2,1,0:T(1,128)S(1)}, s32[1,1,32]{2,1,0:T(1,128)}, u32[]{:S(2)}) copy-start(s32[1,1,32]{2,1,0:T(1,128)} %param.9) | copy-start | bytes 388
  42.8 31.0 %copy-start.4 = (s32[1,1,32]{2,1,0:T(1,128)S(1)}, s32[1,1,32]{2,1,0:T(1,128)}, u32[]{:S(2)}) copy-start(s32[1,1,32]{2,1,0:T(1,128)} %param.10) | copy-start | bytes 388
  42.8 31.0 %all-to-all-start = ((f32[4,1024,128]{2,1,0:T(8,128)}), f32[4,1024,128]{2,1,0:T(8,128)}, u32[]{:S(2)}, u32[]{:S(2)}) async-start(f32[4,1024,128]{2,1,0:T(8,128)} %broadcast_in_dim.25), calls=%async_computation | async-start | bytes 4194304 | tf_op jit(solution)/shard_map/all_to_all | solution.py:18
  152.1 16.8 %all-to-all-start.4 = ((f32[8,128,128]{2,1,0:T(8,128)}), f32[8,128,128]{2,1,0:T(8,128)S(1)}, u32[]{:S(2)}, u32[]{:S(2)}) async-start(f32[8,128,128]{2,1,0:T(8,128)} %bitcast.14), calls=%async_computation.4 | async-start | bytes 1048576 | tf_op jit(solution)/shard_map/all_to_all | solution.py:18
  206.4 27.7 %all-to-all-start.6 = ((f32[4,1024,128]{2,1,0:T(8,128)}), f32[4,1024,128]{2,1,0:T(8,128)}, u32[]{:S(2)}, u32[]{:S(2)}) async-start(f32[4,1024,128]{2,1,0:T(8,128)} %broadcast_in_dim.28), calls=%async_computation.6 | async-start | bytes 4194304 | tf_op jit(solution)/shard_map/all_to_all | solution.py:18

commit v8 on v7

--- a/solution.py
+++ b/solution.py
@@ -35,16 +35,15 @@
 def add_slots(rows_ref, cols_ref, count_ref, blocks_ref, gathered_ref, sums_ref):
     sums_ref[...] = jnp.zeros_like(sums_ref)
     count = count_ref[0]
-    width = sums_ref.shape[1]
+    width, nodes = sums_ref.shape[1:]
     pieces = gathered_ref.shape[1] // width
     for slot in range(blocks_ref.shape[0]):
         live = (slot < count).astype(jnp.float32)
         col = cols_ref[slot]
         first_row = pl.multiple_of((col % pieces) * width, width)
-        high, low = split(gathered_ref[col // pieces, pl.ds(first_row, width)] * live)
-        block_high, block_low = split(blocks_ref[slot])
-        both = dot_pieces(jnp.concatenate([high, low], axis=0), block_high)
-        sums_ref[rows_ref[slot]] += both[:width] + both[width:] + dot_pieces(high, block_low)
+        vectors = jnp.concatenate(split(gathered_ref[col // pieces, pl.ds(first_row, width)] * live), axis=0)
+        products = dot_pieces(vectors, jnp.concatenate(split(blocks_ref[slot]), axis=0))
+        sums_ref[rows_ref[slot]] += products[:width, :nodes] + products[width:, :nodes] + products[:width, nodes:]
 
 
 def tile_kernel(rows_ref, cols_ref, count_ref, blocks_ref, gathered_ref, out_ref):
@@ -89,7 +88,7 @@
     copies_ref[...] = jnp.broadcast_to(jnp.sum(chunks_ref[...], axis=0)[None], copies_ref.shape)
 
 
-def inverse_factor(gram_matrix):
+def inverse_factor(gram_matrix, pivots=4):
     size = gram_matrix.shape[0]
     shape = (size, 2 * size)
     row_of = lax.broadcasted_iota(jnp.int32, shape, 0)
@@ -97,17 +96,19 @@
         jnp.float32
     )
     work = jnp.concatenate([gram_matrix, eye], axis=1)
-    for j in range(0, size, 2):
-        left = jnp.broadcast_to(work[:, j : j + 1], shape)
-        right = jnp.broadcast_to(work[:, j + 1 : j + 2], shape)
-        upper, lower = work[j : j + 1], work[j + 1 : j + 2]
-        inverse_pivot = 1.0 / left[j : j + 1]
-        ratio = left[j + 1 : j + 2] * inverse_pivot
-        next_pivot = right[j + 1 : j + 2] - ratio * left[j + 1 : j + 2]
-        lower = (lower - ratio * upper) * (1.0 / next_pivot)
-        right = jnp.where(row_of > j + 1, right - left * ratio, 0.0)
-        left = jnp.where(row_of > j, left, 0.0)
-        work = work - left * (upper * inverse_pivot) - right * lower
+    for first in range(0, size, pivots):
+        columns = [jnp.broadcast_to(work[:, j : j + 1], shape) for j in range(first, first + pivots)]
+        upper = [work[j : j + 1] for j in range(first, first + pivots)]
+        taken = jnp.zeros(shape, jnp.float32)
+        for k in range(pivots):
+            inverse_pivot = 1.0 / columns[k][first + k : first + k + 1]
+            upper[k] = upper[k] * inverse_pivot
+            for m in range(k + 1, pivots):
+                factor = columns[k][first + m : first + m + 1]
+                upper[m] = upper[m] - factor * upper[k]
+                columns[m] = columns[m] - columns[k] * (factor * inverse_pivot)
+            taken += jnp.where(row_of > first + k, columns[k], 0.0) * upper[k]
+        work = work - taken
     diagonal = jnp.sum(work[:, :size] * eye, axis=1, keepdims=True)
     return work[:, size:] * lax.rsqrt(diagonal)
 

time: 290 us -> 287 us (0.990)
  Pallas kernels: 17.6 us -> 13.6 us
    pallas_call x8, Pallas kernels: 17.6 us -> 13.6 us  [call_kernel(): pl.pallas_call(kernel, out_shape=[jax.ShapeDtypeStruct(shape, jnp.float32...]
where the time goes in v8:
time: 287 us; the launch traced here: 286 us
  blocking collectives  253 us (88%)
  Pallas kernels  13.6 us (5%)
  starting transfers between devices  12.5 us (4%)
  local copies, waits for them, and re-layouts  4.48 us (2%)
    all_gather x6, blocking collectives, gather(): return lax.all_gather(value, axes, axis=0, tiled=False)  145 us
    all_to_all x7, blocking collectives, exchange(): return lax.all_to_all(chunks, axes, 0, 0, tiled=True)  108 us
    pallas_call x8, Pallas kernels, call_kernel(): pl.pallas_call(kernel, out_shape=[jax.ShapeDtypeStruct(shape, jnp.float32...  13.6 us
    all_to_all x3, starting transfers between devices, exchange(): return lax.all_to_all(chunks, axes, 0, 0, tiled=True)  12.5 us
  transfers between devices with their start and end apart: 3, of which 0 were waited for; matrix products, arithmetic and copies ran while one was open for 0% of the time, Pallas kernels for 1%

profile of v8, /device:TPU:1, one launch (start us, length us, event | category | flops | bytes accessed | tf_op | source)
XLA Modules:
  0.0 285.8 jit_solution(4393739108852102482)
XLA Ops:
  0.6 0.0 copy-start.1
  0.6 0.7 copy-done.1
  1.4 0.0 copy-start.5
  1.4 0.7 copy-done.5
  2.0 0.1 shard_map.77
  2.1 39.2 %all-gather = f32[1024,128]{1,0:T(8,128)S(1)} all-gather(f32[64,128]{1,0:T(8,128)S(1)} %get-tuple-element.12), channel_id=2, replica_groups=mesh['x'=4,'z'=16,'y'=8,'core'=2] {'z'}, dimensions={0}, use_global_device_ids=true | all-gather | bytes 557056 | tf_op jit(solution)/shard_map/all_gather | solution.py:180
  41.3 1.4 broadcast_in_dim.25
  42.8 0.0 copy-start.2
  42.8 0.0 copy-start
  42.8 0.0 copy-start.3
  42.8 0.0 copy-start.4
  42.8 4.6 %all-to-all-start = ((f32[4,1024,128]{2,1,0:T(8,128)}), f32[4,1024,128]{2,1,0:T(8,128)}, u32[]{:S(2)}, u32[]{:S(2)}) async-start(f32[4,1024,128]{2,1,0:T(8,128)} %broadcast_in_dim.25), calls=%async_computation | async-start | bytes 4194304 | tf_op jit(solution)/shard_map/all_to_all | solution.py:18
  48.0 0.0 copy-done.2
  48.0 0.2 fusion.9
  48.2 0.1 pad_maximum_fusion.2
  48.3 25.4 %all-gather.1 = f32[512,128]{1,0:T(8,128)S(1)} all-gather(f32[32,128]{1,0:T(8,128)S(1)} %pad_maximum_fusion.2), channel_id=3, replica_groups=mesh['x'=4,'z'=16,'y'=8,'core'=2] {'y','core'}, dimensions={0}, use_global_device_ids=true | all-gather | bytes 278528 | tf_op jit(solution)/shard_map/all_gather | solution.py:180
  73.8 0.0 all-to-all-done.gathered_ref
  73.8 0.0 copy-done
  73.8 0.0 copy-done.3
  73.8 0.0 copy-done.4
  73.8 2.3 shard_map.78
  76.2 16.9 %all_to_all.50 = f32[8,128,128]{2,1,0:T(8,128)S(1)} all-to-all(f32[8,128,128]{2,1,0:T(8,128)S(1)} %bitcast.39), channel_id=1, replica_groups=mesh['x'=4,'z'=16,'y'=8,'core'=2] {'y'}, dimensions={0} | all-to-all | bytes 1048576 | tf_op jit(solution)/shard_map/all_to_all | solution.py:18
  93.1 8.9 %all_to_all.51 = f32[2,64,128]{2,1,0:T(8,128)S(1)} all-to-all(f32[2,64,128]{2,1,0:T(8,128)S(1)} %bitcast.56), channel_id=1, replica_groups=mesh['x'=4,'z'=16,'y'=8,'core'=2] {'core'}, dimensions={0} | all-to-all | bytes 131072 | tf_op jit(solution)/shard_map/all_to_all | solution.py:18
  102.0 22.9 %all-gather.2 = f32[1280,128]{1,0:T(8,128)S(1)} all-gather(f32[80,128]{1,0:T(8,128)S(1)} %pad_maximum_fusion.1), channel_id=4, replica_groups=mesh['x'=4,'z'=16,'y'=8,'core'=2] {'z'}, dimensions={0}, use_global_device_ids=true | all-gather | bytes 696320 | tf_op jit(solution)/shard_map/all_gather | solution.py:180
  125.0 0.1 broadcast_in_dim.26
  125.1 23.5 %all_to_all.52.gathered_ref = f32[4,1040,128]{2,1,0:T(8,128)S(1)} all-to-all(f32[4,1040,128]{2,1,0:T(8,128)S(1)} %broadcast_in_dim.26), channel_id=1, replica_groups=mesh['x'=4,'z'=16,'y'=8,'core'=2] {'x'}, dimensions={0} | all-to-all | bytes 4259840 | tf_op jit(solution)/shard_map/all_to_all | solution.py:18
  148.6 2.1 shard_map.79
  150.7 3.5 %all-to-all-start.4 = ((f32[8,128,128]{2,1,0:T(8,128)}), f32[8,128,128]{2,1,0:T(8,128)S(1)}, u32[]{:S(2)}, u32[]{:S(2)}) async-start(f32[8,128,128]{2,1,0:T(8,128)} %bitcast.14), calls=%async_computation.4 | async-start | bytes 1048576 | tf_op jit(solution)/shard_map/all_to_all | solution.py:18
  154.2 9.9 %all-gather.3.folded_ref = f32[32,128]{1,0:T(8,128)S(1)} all-gather(f32[16,128]{1,0:T(8,128)S(1)} %get-tuple-element.16), channel_id=5, replica_groups=mesh['x'=4,'z'=16,'y'=8,'core'=2] {'core'}, dimensions={0}, use_global_device_ids=true | all-gather | bytes 24576 | tf_op jit(solution)/shard_map/all_gather | solution.py:180
  164.1 2.3 shard_map.80
  166.5 0.0 all-to-all-done.4
  166.5 12.8 %all_to_all.53 = f32[2,64,128]{2,1,0:T(8,128)S(1)} all-to-all(f32[2,64,128]{2,1,0:T(8,128)S(1)} %bitcast.57), channel_id=1, replica_groups=mesh['x'=4,'z'=16,'y'=8,'core'=2] {'core'}, dimensions={0} | all-to-all | bytes 131072 | tf_op jit(solution)/shard_map/all_to_all | solution.py:18
  179.3 0.2 broadcast_multiply_fusion
  179.5 24.1 %all-gather.4 = f32[1024,128]{1,0:T(8,128)S(1)} all-gather(f32[64,128]{1,0:T(8,128)S(1)} %get-tuple-element.24), channel_id=6, replica_groups=mesh['x'=4,'z'=16,'y'=8,'core'=2] {'z'}, dimensions={0}, use_global_device_ids=true | all-gather | bytes 557056 | tf_op jit(solution)/shard_map/all_gather | solution.py:180
  203.6 1.4 broadcast_in_dim.28
  205.1 4.4 %all-to-all-start.6 = ((f32[4,1024,128]{2,1,0:T(8,128)}), f32[4,1024,128]{2,1,0:T(8,128)}, u32[]{:S(2)}, u32[]{:S(2)}) async-start(f32[4,1024,128]{2,1,0:T(8,128)} %broadcast_in_dim.28), calls=%async_computation.6 | async-start | bytes 4194304 | tf_op jit(solution)/shard_map/all_to_all | solution.py:18
  209.5 0.2 fusion.10.gram_ref
  209.7 23.1 %all-gather.5 = f32[1024,128]{1,0:T(8,128)S(1)} all-gather(f32[64,128]{1,0:T(8,128)S(1)} %get-tuple-element.24), channel_id=7, replica_groups=mesh['x'=4,'z'=16,'y'=8,'core'=2] {'y','core'}, dimensions={0}, use_global_device_ids=true | all-gather | bytes 557056 | tf_op jit(solution)/shard_map/all_gather | solution.py:180
  232.8 0.0 all-to-all-done.6.gathered_ref
  232.8 3.3 %shard_map.81 = f32[64,128]{1,0:T(8,128)S(1)} custom-call(s32[32]{0:T(128)S(1)} %bitcast.45, s32[32]{0:T(128)S(1)} %bitcast.48, s32[1]{0:T(128)} %bitcast.34.count_ref, f32[32,128,128]{2,1,0:T(8,128)S(1)} %bitcast.37, f32[4,1024,128]{2,1,0:T(8,128)} %all-to-all-done.6.gathered_ref, f32[16,64,128]{2,1,0:T(8,128)S(1)} %bitcast.38, f32[64,64]{1,0:T(8,128)S(1)} %fusion.10.gram_ref), custom_call_target="tpu_custom_call" | custom-call | tf_op jit(solution)/shard_map/pallas_call | solution.py:137
  236.1 13.9 %all_to_all.54.chunks_ref = f32[16,4,128]{2,1,0:T(4,128)S(1)} all-to-all(f32[16,4,128]{2,1,0:T(4,128)S(1)} %bitcast.41), channel_id=1, replica_groups=mesh['x'=4,'z'=16,'y'=8,'core'=2] {'y','core'}, dimensions={0} | all-to-all | bytes 65536 | tf_op jit(solution)/shard_map/all_to_all | solution.py:18
  250.0 20.1 %all_to_all.55.chunks_ref = f32[64,4,128]{2,1,0:T(4,128)S(1)} all-to-all(f32[64,4,128]{2,1,0:T(4,128)S(1)} %shard_map.82), channel_id=1, replica_groups=mesh['x'=4,'z'=16,'y'=8,'core'=2] {'x','z'}, dimensions={0} | all-to-all | bytes 262144 | tf_op jit(solution)/shard_map/all_to_all | solution.py:18
  270.2 0.1 shard_map.83
  270.3 12.2 %all_to_all.56 = f32[16,4,128]{2,1,0:T(4,128)S(1)} all-to-all(f32[16,4,128]{2,1,0:T(4,128)S(1)} %shard_map.83), channel_id=1, replica_groups=mesh['x'=4,'z'=16,'y'=8,'core'=2] {'y','core'}, dimensions={0} | all-to-all | bytes 65536 | tf_op jit(solution)/shard_map/all_to_all | solution.py:18
  282.4 3.3 %shard_map.84 = (f32[64,128]{1,0:T(8,128)}, f32[64,64]{1,0:T(8,128)}) custom-call(f32[64,128]{1,0:T(8,128)S(1)} %bitcast.42, f32[64,128]{1,0:T(8,128)S(1)} %get-tuple-element.25.filtered_ref), custom_call_target="tpu_custom_call" | custom-call | tf_op jit(solution)/shard_map/pallas_call | solution.py:137
  (13 shorter events, 0.3 us)
Async XLA Ops:
  0.6 0.8 copy-start.1
  1.4 0.7 copy-start.5
  42.8 5.3 %copy-start.2 = (f32[128,64]{0,1:T(8,128)S(1)}, f32[128,64]{0,1:T(8,128)}, u32[]{:S(2)}) copy-start(f32[128,64]{0,1:T(8,128)} %param.6) | copy-start | bytes 98308
  42.8 31.0 %copy-start = (f32[1,1,32,128,128]{4,3,2,1,0:T(8,128)S(1)}, f32[1,1,32,128,128]{4,3,2,1,0:T(8,128)}, u32[]{:S(2)}) copy-start(f32[1,1,32,128,128]{4,3,2,1,0:T(8,128)} %param.8) | copy-start | bytes 6291460
  42.8 31.0 %copy-start.3 = (s32[1,1,32]{2,1,0:T(1,128)S(1)}, s32[1,1,32]{2,1,0:T(1,128)}, u32[]{:S(2)}) copy-start(s32[1,1,32]{2,1,0:T(1,128)} %param.9) | copy-start | bytes 388
  42.8 31.0 %copy-start.4 = (s32[1,1,32]{2,1,0:T(1,128)S(1)}, s32[1,1,32]{2,1,0:T(1,128)}, u32[]{:S(2)}) copy-start(s32[1,1,32]{2,1,0:T(1,128)} %param.10) | copy-start | bytes 388
  42.8 31.0 %all-to-all-start = ((f32[4,1024,128]{2,1,0:T(8,128)}), f32[4,1024,128]{2,1,0:T(8,128)}, u32[]{:S(2)}, u32[]{:S(2)}) async-start(f32[4,1024,128]{2,1,0:T(8,128)} %broadcast_in_dim.25), calls=%async_computation | async-start | bytes 4194304 | tf_op jit(solution)/shard_map/all_to_all | solution.py:18
  150.7 15.8 %all-to-all-start.4 = ((f32[8,128,128]{2,1,0:T(8,128)}), f32[8,128,128]{2,1,0:T(8,128)S(1)}, u32[]{:S(2)}, u32[]{:S(2)}) async-start(f32[8,128,128]{2,1,0:T(8,128)} %bitcast.14), calls=%async_computation.4 | async-start | bytes 1048576 | tf_op jit(solution)/shard_map/all_to_all | solution.py:18
  205.1 27.7 %all-to-all-start.6 = ((f32[4,1024,128]{2,1,0:T(8,128)}), f32[4,1024,128]{2,1,0:T(8,128)}, u32[]{:S(2)}, u32[]{:S(2)}) async-start(f32[4,1024,128]{2,1,0:T(8,128)} %broadcast_in_dim.28), calls=%async_computation.6 | async-start | bytes 4194304 | tf_op jit(solution)/shard_map/all_to_all | solution.py:18

commit v9 on v8

--- a/solution.py
+++ b/solution.py
@@ -54,20 +54,6 @@
     add_slots(rows_ref, cols_ref, count_ref, blocks_ref, gathered_ref, out_ref)
     pieces_end = gathered_ref.shape[1] - rider_ref.shape[0]
     rider_ref[...] = jnp.sum(gathered_ref[:, pieces_end:], axis=0)
-
-
-def scale_kernel(degrees_hbm, vectors_hbm, scale_ref, scaled_ref, degrees_ref, vectors_ref, sems):
-    fetches = [
-        pltpu.make_async_copy(degrees_hbm, degrees_ref, sems.at[0]),
-        pltpu.make_async_copy(vectors_hbm, vectors_ref, sems.at[1]),
-    ]
-    for fetch in fetches:
-        fetch.start()
-    for fetch in fetches:
-        fetch.wait()
-    scale = jnp.sqrt(16.0 / degrees_ref[...].astype(jnp.float32))
-    scale_ref[...] = scale
-    scaled_ref[...] = vectors_ref[...] * scale
 
 
 def project_kernel(
@@ -130,15 +116,13 @@
 
 SMEM = pl.BlockSpec(memory_space=pltpu.SMEM)
 VMEM = pl.BlockSpec(memory_space=pltpu.VMEM)
-HBM = pl.BlockSpec(memory_space=pltpu.HBM)
-
-
-def call_kernel(kernel, ins, outs, scratch=(), in_specs=None):
+
+
+def call_kernel(kernel, ins, outs, scratch=()):
     return pl.pallas_call(
         kernel,
         out_shape=[jax.ShapeDtypeStruct(shape, jnp.float32) for shape in outs],
-        in_specs=in_specs
-        or [SMEM if value.dtype == jnp.int32 and value.ndim == 1 else VMEM for value in ins],
+        in_specs=[SMEM if value.dtype == jnp.int32 and value.ndim == 1 else VMEM for value in ins],
         out_specs=[VMEM] * len(outs),
         scratch_shapes=list(scratch),
         compiler_params=pltpu.CompilerParams(vmem_limit_bytes=24 * 2**20),
@@ -173,15 +157,21 @@
     cols = block_cols.reshape(-1)
     count = block_counts.reshape(-1)
 
+    y_devices = lax.axis_size("y")
     tile = (rows, cols, count, tile_blocks)
+    tile_core_first = ((rows % 2) * y_devices + rows // 2, cols, count, tile_blocks)
     sums_shape = (col_devices, width, nodes)
 
     def gather(value, axes):
         return lax.all_gather(value, axes, axis=0, tiled=False)
 
     def reduce_cols(partial):
-        along_y = exchange(partial.reshape(lax.axis_size("y"), -1, nodes), "y").sum(0)
-        return exchange(along_y.reshape(lax.axis_size("core"), width, nodes), "core").sum(0) * scale
+        along_y = exchange(partial.reshape(y_devices, -1, nodes), "y").sum(0)
+        return exchange(along_y.reshape(-1, width, nodes), "core").sum(0) * scale
+
+    def reduce_core_first(partial):
+        halves = exchange(partial.reshape(-1, y_devices * width, nodes), "core").sum(0)
+        return exchange(halves.reshape(y_devices, width, nodes), "y").sum(0) * scale
 
     def together(*values):
         return lax.optimization_barrier(values)
@@ -190,20 +180,14 @@
         return call_kernel(sum_kernel, (chunks,), [(copies, *chunks.shape[1:])])[0]
 
     first = start.T
-    scale, scaled = call_kernel(
-        scale_kernel,
-        (degrees[None], first),
-        [(1, nodes), (width, nodes)],
-        [pltpu.VMEM((1, nodes), jnp.int32), pltpu.VMEM((width, nodes), jnp.float32), pltpu.SemaphoreType.DMA((2,))],
-        [HBM, HBM],
-    )
-    along_z = gather(scaled, "z").reshape(-1, nodes)
+    scale = jnp.sqrt(16.0 / degrees.astype(jnp.float32))[None, :]
+    along_z = gather(first * scale, "z").reshape(-1, nodes)
     rider = gather(fold(gram(first, first)), COL).sum(0).reshape(lax.axis_size("core"), -1, nodes)
     half_shape = rider.shape[1:]
     rider = lax.dynamic_index_in_dim(rider, lax.axis_index("core"), keepdims=False)
     gathered, rider = together(to_all(along_z, "x"), rider)
-    (partial,) = call_kernel(tile_kernel, (*tile, gathered), [sums_shape])
-    once = reduce_cols(partial)
+    (partial,) = call_kernel(tile_kernel, (*tile_core_first, gathered), [sums_shape])
+    once = reduce_core_first(partial)
 
     along_z = gather(jnp.concatenate([once * scale, rider], axis=0), "z")
     along_z = jnp.concatenate([along_z[:, :width].reshape(-1, nodes), along_z[:, width:].sum(0)], axis=0)

time: 287 us -> 281 us (0.979)
  blocking collectives: 253 us -> 248 us
    all_to_all x7, blocking collectives: 108 us -> 101 us  [exchange(): return lax.all_to_all(chunks, axes, 0, 0, tiled=True)]
    pallas_call x8 -> x7, Pallas kernels: 13.6 us -> 13.5 us  [call_kernel(): pl.pallas_call(kernel, out_shape=[jax.ShapeDtypeStruct(shape, jnp.float32...]
where the time goes in v9:
time: 281 us
  blocking collectives  248 us (88%)
  Pallas kernels  13.5 us (5%)
  starting transfers between devices  12.6 us (4%)
  local copies, waits for them, and re-layouts  3.07 us (1%)
    all_gather x6, blocking collectives, gather(): return lax.all_gather(value, axes, axis=0, tiled=False)  146 us
    all_to_all x7, blocking collectives, exchange(): return lax.all_to_all(chunks, axes, 0, 0, tiled=True)  101 us
    pallas_call x7, Pallas kernels, call_kernel(): pl.pallas_call(kernel, out_shape=[jax.ShapeDtypeStruct(shape, jnp.float32...  13.5 us
    all_to_all x3, starting transfers between devices, exchange(): return lax.all_to_all(chunks, axes, 0, 0, tiled=True)  12.6 us
  transfers between devices with their start and end apart: 3, of which 0 were waited for; matrix products, arithmetic and copies ran while one was open for 0% of the time, Pallas kernels for 1%

profile of v9, /device:TPU:1, one launch (start us, length us, event | category | flops | bytes accessed | tf_op | source)
XLA Modules:
  0.0 280.5 jit_solution(9913813776820844927)
XLA Ops:
  0.6 0.7 divide_sqrt_fusion
  1.3 0.8 bitcast_multiply_fusion
  2.1 39.2 %all-gather = f32[1024,128]{1,0:T(8,128)S(1)} all-gather(f32[64,128]{1,0:T(8,128)S(1)} %bitcast_multiply_fusion), channel_id=2, replica_groups=mesh['x'=4,'z'=16,'y'=8,'core'=2] {'z'}, dimensions={0}, use_global_device_ids=true | all-gather | bytes 557056 | tf_op jit(solution)/shard_map/all_gather | solution.py:166
  41.3 1.4 broadcast_in_dim.22
  42.7 0.0 copy-start.3
  42.7 0.0 copy-start.2
  42.7 0.0 copy-start
  42.7 0.0 copy-start.1
  42.7 4.6 %all-to-all-start = ((f32[4,1024,128]{2,1,0:T(8,128)}), f32[4,1024,128]{2,1,0:T(8,128)}, u32[]{:S(2)}, u32[]{:S(2)}) async-start(f32[4,1024,128]{2,1,0:T(8,128)} %broadcast_in_dim.22), calls=%async_computation | async-start | bytes 4194304 | tf_op jit(solution)/shard_map/all_to_all | solution.py:18
  47.9 0.0 copy-done.3
  48.0 0.2 fusion.9
  48.2 0.1 pad_maximum_fusion.2
  48.2 25.4 %all-gather.1 = f32[512,128]{1,0:T(8,128)S(1)} all-gather(f32[32,128]{1,0:T(8,128)S(1)} %pad_maximum_fusion.2), channel_id=3, replica_groups=mesh['x'=4,'z'=16,'y'=8,'core'=2] {'y','core'}, dimensions={0}, use_global_device_ids=true | all-gather | bytes 278528 | tf_op jit(solution)/shard_map/all_gather | solution.py:166
  73.7 0.0 copy-done.2
  73.7 0.0 all-to-all-done.gathered_ref
  73.7 0.0 copy-done
  73.7 0.0 copy-done.1
  73.8 2.4 shard_map.77
  76.1 4.7 %all_to_all.50 = f32[2,512,128]{2,1,0:T(8,128)S(1)} all-to-all(f32[2,512,128]{2,1,0:T(8,128)S(1)} %bitcast.37), channel_id=1, replica_groups=mesh['x'=4,'z'=16,'y'=8,'core'=2] {'core'}, dimensions={0} | all-to-all | bytes 1048576 | tf_op jit(solution)/shard_map/all_to_all | solution.py:18
  80.8 17.7 %all_to_all.51 = f32[8,64,128]{2,1,0:T(8,128)S(1)} all-to-all(f32[8,64,128]{2,1,0:T(8,128)S(1)} %bitcast.49), channel_id=1, replica_groups=mesh['x'=4,'z'=16,'y'=8,'core'=2] {'y'}, dimensions={0} | all-to-all | bytes 524288 | tf_op jit(solution)/shard_map/all_to_all | solution.py:18
  98.6 23.1 %all-gather.2 = f32[1280,128]{1,0:T(8,128)S(1)} all-gather(f32[80,128]{1,0:T(8,128)S(1)} %pad_maximum_fusion.1), channel_id=4, replica_groups=mesh['x'=4,'z'=16,'y'=8,'core'=2] {'z'}, dimensions={0}, use_global_device_ids=true | all-gather | bytes 696320 | tf_op jit(solution)/shard_map/all_gather | solution.py:166
  121.8 0.1 broadcast_in_dim.23
  121.9 20.3 %all_to_all.52.gathered_ref = f32[4,1040,128]{2,1,0:T(8,128)S(1)} all-to-all(f32[4,1040,128]{2,1,0:T(8,128)S(1)} %broadcast_in_dim.23), channel_id=1, replica_groups=mesh['x'=4,'z'=16,'y'=8,'core'=2] {'x'}, dimensions={0} | all-to-all | bytes 4259840 | tf_op jit(solution)/shard_map/all_to_all | solution.py:18
  142.3 2.1 shard_map.78
  144.3 3.6 %all-to-all-start.4 = ((f32[8,128,128]{2,1,0:T(8,128)}), f32[8,128,128]{2,1,0:T(8,128)S(1)}, u32[]{:S(2)}, u32[]{:S(2)}) async-start(f32[8,128,128]{2,1,0:T(8,128)} %bitcast.12), calls=%async_computation.4 | async-start | bytes 1048576 | tf_op jit(solution)/shard_map/all_to_all | solution.py:18
  148.0 11.1 %all-gather.3.folded_ref = f32[32,128]{1,0:T(8,128)S(1)} all-gather(f32[16,128]{1,0:T(8,128)S(1)} %get-tuple-element.12), channel_id=5, replica_groups=mesh['x'=4,'z'=16,'y'=8,'core'=2] {'core'}, dimensions={0}, use_global_device_ids=true | all-gather | bytes 24576 | tf_op jit(solution)/shard_map/all_gather | solution.py:166
  159.1 2.3 shard_map.79
  161.4 0.0 all-to-all-done.4
  161.5 12.8 %all_to_all.53 = f32[2,64,128]{2,1,0:T(8,128)S(1)} all-to-all(f32[2,64,128]{2,1,0:T(8,128)S(1)} %bitcast.50), channel_id=1, replica_groups=mesh['x'=4,'z'=16,'y'=8,'core'=2] {'core'}, dimensions={0} | all-to-all | bytes 131072 | tf_op jit(solution)/shard_map/all_to_all | solution.py:18
  174.3 0.2 broadcast_multiply_fusion
  174.5 24.0 %all-gather.4 = f32[1024,128]{1,0:T(8,128)S(1)} all-gather(f32[64,128]{1,0:T(8,128)S(1)} %get-tuple-element.20), channel_id=6, replica_groups=mesh['x'=4,'z'=16,'y'=8,'core'=2] {'z'}, dimensions={0}, use_global_device_ids=true | all-gather | bytes 557056 | tf_op jit(solution)/shard_map/all_gather | solution.py:166
  198.4 1.4 broadcast_in_dim.25
  199.9 4.4 %all-to-all-start.6 = ((f32[4,1024,128]{2,1,0:T(8,128)}), f32[4,1024,128]{2,1,0:T(8,128)}, u32[]{:S(2)}, u32[]{:S(2)}) async-start(f32[4,1024,128]{2,1,0:T(8,128)} %broadcast_in_dim.25), calls=%async_computation.6 | async-start | bytes 4194304 | tf_op jit(solution)/shard_map/all_to_all | solution.py:18
  204.3 0.2 fusion.10.gram_ref
  204.5 23.4 %all-gather.5 = f32[1024,128]{1,0:T(8,128)S(1)} all-gather(f32[64,128]{1,0:T(8,128)S(1)} %get-tuple-element.20), channel_id=7, replica_groups=mesh['x'=4,'z'=16,'y'=8,'core'=2] {'y','core'}, dimensions={0}, use_global_device_ids=true | all-gather | bytes 557056 | tf_op jit(solution)/shard_map/all_gather | solution.py:166
  227.9 0.0 all-to-all-done.6.gathered_ref
  227.9 3.3 %shard_map.80 = f32[64,128]{1,0:T(8,128)S(1)} custom-call(s32[32]{0:T(128)S(1)} %bitcast.44, s32[32]{0:T(128)S(1)} %bitcast.42, s32[1]{0:T(128)} %bitcast.32.count_ref, f32[32,128,128]{2,1,0:T(8,128)S(1)} %bitcast.35, f32[4,1024,128]{2,1,0:T(8,128)} %all-to-all-done.6.gathered_ref, f32[16,64,128]{2,1,0:T(8,128)S(1)} %bitcast.36, f32[64,64]{1,0:T(8,128)S(1)} %fusion.10.gram_ref), custom_call_target="tpu_custom_call" | custom-call | tf_op jit(solution)/shard_map/pallas_call | solution.py:122
  231.2 13.6 %all_to_all.54.chunks_ref = f32[16,4,128]{2,1,0:T(4,128)S(1)} all-to-all(f32[16,4,128]{2,1,0:T(4,128)S(1)} %bitcast.38), channel_id=1, replica_groups=mesh['x'=4,'z'=16,'y'=8,'core'=2] {'y','core'}, dimensions={0} | all-to-all | bytes 65536 | tf_op jit(solution)/shard_map/all_to_all | solution.py:18
  244.9 20.1 %all_to_all.55.chunks_ref = f32[64,4,128]{2,1,0:T(4,128)S(1)} all-to-all(f32[64,4,128]{2,1,0:T(4,128)S(1)} %shard_map.81), channel_id=1, replica_groups=mesh['x'=4,'z'=16,'y'=8,'core'=2] {'x','z'}, dimensions={0} | all-to-all | bytes 262144 | tf_op jit(solution)/shard_map/all_to_all | solution.py:18
  265.0 0.1 shard_map.82
  265.0 12.2 %all_to_all.56 = f32[16,4,128]{2,1,0:T(4,128)S(1)} all-to-all(f32[16,4,128]{2,1,0:T(4,128)S(1)} %shard_map.82), channel_id=1, replica_groups=mesh['x'=4,'z'=16,'y'=8,'core'=2] {'y','core'}, dimensions={0} | all-to-all | bytes 65536 | tf_op jit(solution)/shard_map/all_to_all | solution.py:18
  277.2 3.3 %shard_map.83 = (f32[64,128]{1,0:T(8,128)}, f32[64,64]{1,0:T(8,128)}) custom-call(f32[64,128]{1,0:T(8,128)S(1)} %bitcast.39, f32[64,128]{1,0:T(8,128)S(1)} %get-tuple-element.21.filtered_ref), custom_call_target="tpu_custom_call" | custom-call | tf_op jit(solution)/shard_map/pallas_call | solution.py:122
  (14 shorter events, 0.3 us)
Async XLA Ops:
  42.7 5.3 %copy-start.3 = (f32[128,64]{0,1:T(8,128)S(1)}, f32[128,64]{0,1:T(8,128)}, u32[]{:S(2)}) copy-start(f32[128,64]{0,1:T(8,128)} %param.6) | copy-start | bytes 98308
  42.7 31.0 %copy-start.2 = (s32[1,1,32]{2,1,0:T(1,128)S(1)}, s32[1,1,32]{2,1,0:T(1,128)}, u32[]{:S(2)}) copy-start(s32[1,1,32]{2,1,0:T(1,128)} %param.9) | copy-start | bytes 388
  42.7 31.0 %copy-start = (f32[1,1,32,128,128]{4,3,2,1,0:T(8,128)S(1)}, f32[1,1,32,128,128]{4,3,2,1,0:T(8,128)}, u32[]{:S(2)}) copy-start(f32[1,1,32,128,128]{4,3,2,1,0:T(8,128)} %param.8) | copy-start | bytes 6291460
  42.7 31.1 %copy-start.1 = (s32[1,1,32]{2,1,0:T(1,128)S(1)}, s32[1,1,32]{2,1,0:T(1,128)}, u32[]{:S(2)}) copy-start(s32[1,1,32]{2,1,0:T(1,128)} %param.10) | copy-start | bytes 388
  42.7 31.0 %all-to-all-start = ((f32[4,1024,128]{2,1,0:T(8,128)}), f32[4,1024,128]{2,1,0:T(8,128)}, u32[]{:S(2)}, u32[]{:S(2)}) async-start(f32[4,1024,128]{2,1,0:T(8,128)} %broadcast_in_dim.22), calls=%async_computation | async-start | bytes 4194304 | tf_op jit(solution)/shard_map/all_to_all | solution.py:18
  144.3 17.1 %all-to-all-start.4 = ((f32[8,128,128]{2,1,0:T(8,128)}), f32[8,128,128]{2,1,0:T(8,128)S(1)}, u32[]{:S(2)}, u32[]{:S(2)}) async-start(f32[8,128,128]{2,1,0:T(8,128)} %bitcast.12), calls=%async_computation.4 | async-start | bytes 1048576 | tf_op jit(solution)/shard_map/all_to_all | solution.py:18
  199.9 28.0 %all-to-all-start.6 = ((f32[4,1024,128]{2,1,0:T(8,128)}), f32[4,1024,128]{2,1,0:T(8,128)}, u32[]{:S(2)}, u32[]{:S(2)}) async-start(f32[4,1024,128]{2,1,0:T(8,128)} %broadcast_in_dim.25), calls=%async_computation.6 | async-start | bytes 4194304 | tf_op jit(solution)/shard_map/all_to_all | solution.py:18

commit v10 on v9

--- a/solution.py
+++ b/solution.py
@@ -166,10 +166,6 @@
         return lax.all_gather(value, axes, axis=0, tiled=False)
 
     def reduce_cols(partial):
-        along_y = exchange(partial.reshape(y_devices, -1, nodes), "y").sum(0)
-        return exchange(along_y.reshape(-1, width, nodes), "core").sum(0) * scale
-
-    def reduce_core_first(partial):
         halves = exchange(partial.reshape(-1, y_devices * width, nodes), "core").sum(0)
         return exchange(halves.reshape(y_devices, width, nodes), "y").sum(0) * scale
 
@@ -187,11 +183,11 @@
     rider = lax.dynamic_index_in_dim(rider, lax.axis_index("core"), keepdims=False)
     gathered, rider = together(to_all(along_z, "x"), rider)
     (partial,) = call_kernel(tile_kernel, (*tile_core_first, gathered), [sums_shape])
-    once = reduce_core_first(partial)
+    once = reduce_cols(partial)
 
     along_z = gather(jnp.concatenate([once * scale, rider], axis=0), "z")
     along_z = jnp.concatenate([along_z[:, :width].reshape(-1, nodes), along_z[:, width:].sum(0)], axis=0)
-    partial, rider = call_kernel(tile_rider_kernel, (*tile, to_all(along_z, "x")), [sums_shape, half_shape])
+    partial, rider = call_kernel(tile_rider_kernel, (*tile_core_first, to_all(along_z, "x")), [sums_shape, half_shape])
     rider = gather(rider, "core").reshape(-1, nodes)
     (inverse,) = call_kernel(functools.partial(inverse_kernel, nodes_all), (rider,), [(width, width)])
     filtered = matmul(inverse, 2.0 * reduce_cols(partial) - first)

time: 281 us -> 281 us (level)
  blocking collectives: 248 us -> 239 us
  waiting for transfers between devices: 0.01 us -> 8.06 us
    all_gather x6, blocking collectives: 146 us -> 137 us  [gather(): return lax.all_gather(value, axes, axis=0, tiled=False)]
    all_to_all x3, waiting for transfers between devices: 0.01 us -> 8.06 us  [exchange(): return lax.all_to_all(chunks, axes, 0, 0, tiled=True)]
  transfers between devices with their start and end apart: 3 -> 3, of which waited for: 0 -> 1; matrix products, arithmetic and copies ran while one was open for 0% -> 0% of each run, Pallas kernels for 1% -> 1%
where the time goes in v10:
time: 281 us; the launch traced here: 280 us
  blocking collectives  239 us (85%)
  Pallas kernels  12.7 us (5%)
  starting transfers between devices  12.4 us (4%)
  waiting for transfers between devices  8.06 us (3%)
  local copies, waits for them, and re-layouts  3.07 us (1%)
    all_gather x6, blocking collectives, gather(): return lax.all_gather(value, axes, axis=0, tiled=False)  137 us
    all_to_all x7, blocking collectives, exchange(): return lax.all_to_all(chunks, axes, 0, 0, tiled=True)  102 us
    pallas_call x7, Pallas kernels, call_kernel(): pl.pallas_call(kernel, out_shape=[jax.ShapeDtypeStruct(shape, jnp.float32...  12.7 us
    all_to_all x3, starting transfers between devices, exchange(): return lax.all_to_all(chunks, axes, 0, 0, tiled=True)  12.4 us
    all_to_all x3, waiting for transfers between devices, exchange(): return lax.all_to_all(chunks, axes, 0, 0, tiled=True)  8.06 us
  transfers between devices with their start and end apart: 3, of which 1 were waited for; matrix products, arithmetic and copies ran while one was open for 0% of the time, Pallas kernels for 1%

profile of v10, /device:TPU:1, one launch (start us, length us, event | category | flops | bytes accessed | tf_op | source)
XLA Modules:
  0.0 279.9 jit_solution(11052021861225852058)
XLA Ops:
  0.6 0.7 divide_sqrt_fusion
  1.3 0.8 bitcast_multiply_fusion
  2.1 39.2 %all-gather = f32[1024,128]{1,0:T(8,128)S(1)} all-gather(f32[64,128]{1,0:T(8,128)S(1)} %bitcast_multiply_fusion), channel_id=2, replica_groups=mesh['x'=4,'z'=16,'y'=8,'core'=2] {'z'}, dimensions={0}, use_global_device_ids=true | all-gather | bytes 557056 | tf_op jit(solution)/shard_map/all_gather | solution.py:166
  41.3 1.4 broadcast_in_dim.22
  42.7 0.0 copy-start.3
  42.7 0.0 copy-start.2
  42.7 0.0 copy-start
  42.7 0.0 copy-start.1
  42.7 4.6 %all-to-all-start = ((f32[4,1024,128]{2,1,0:T(8,128)}), f32[4,1024,128]{2,1,0:T(8,128)}, u32[]{:S(2)}, u32[]{:S(2)}) async-start(f32[4,1024,128]{2,1,0:T(8,128)} %broadcast_in_dim.22), calls=%async_computation | async-start | bytes 4194304 | tf_op jit(solution)/shard_map/all_to_all | solution.py:18
  47.9 0.0 copy-done.3
  48.0 0.2 fusion.9
  48.2 0.1 pad_maximum_fusion.2
  48.2 25.4 %all-gather.1 = f32[512,128]{1,0:T(8,128)S(1)} all-gather(f32[32,128]{1,0:T(8,128)S(1)} %pad_maximum_fusion.2), channel_id=3, replica_groups=mesh['x'=4,'z'=16,'y'=8,'core'=2] {'y','core'}, dimensions={0}, use_global_device_ids=true | all-gather | bytes 278528 | tf_op jit(solution)/shard_map/all_gather | solution.py:166
  73.7 0.0 copy-done.2
  73.7 0.0 all-to-all-done.gathered_ref
  73.7 0.0 copy-done
  73.7 0.0 copy-done.1
  73.8 2.4 shard_map.77
  76.1 4.7 %all_to_all.50 = f32[2,512,128]{2,1,0:T(8,128)S(1)} all-to-all(f32[2,512,128]{2,1,0:T(8,128)S(1)} %bitcast.37), channel_id=1, replica_groups=mesh['x'=4,'z'=16,'y'=8,'core'=2] {'core'}, dimensions={0} | all-to-all | bytes 1048576 | tf_op jit(solution)/shard_map/all_to_all | solution.py:18
  80.8 17.7 %all_to_all.51 = f32[8,64,128]{2,1,0:T(8,128)S(1)} all-to-all(f32[8,64,128]{2,1,0:T(8,128)S(1)} %bitcast.49), channel_id=1, replica_groups=mesh['x'=4,'z'=16,'y'=8,'core'=2] {'y'}, dimensions={0} | all-to-all | bytes 524288 | tf_op jit(solution)/shard_map/all_to_all | solution.py:18
  98.6 23.1 %all-gather.2 = f32[1280,128]{1,0:T(8,128)S(1)} all-gather(f32[80,128]{1,0:T(8,128)S(1)} %pad_maximum_fusion.1), channel_id=4, replica_groups=mesh['x'=4,'z'=16,'y'=8,'core'=2] {'z'}, dimensions={0}, use_global_device_ids=true | all-gather | bytes 696320 | tf_op jit(solution)/shard_map/all_gather | solution.py:166
  121.8 0.1 broadcast_in_dim.23
  121.9 20.3 %all_to_all.52.gathered_ref = f32[4,1040,128]{2,1,0:T(8,128)S(1)} all-to-all(f32[4,1040,128]{2,1,0:T(8,128)S(1)} %broadcast_in_dim.23), channel_id=1, replica_groups=mesh['x'=4,'z'=16,'y'=8,'core'=2] {'x'}, dimensions={0} | all-to-all | bytes 4259840 | tf_op jit(solution)/shard_map/all_to_all | solution.py:18
  142.3 1.3 shard_map.78
  143.6 13.5 %all_to_all.53 = f32[2,512,128]{2,1,0:T(8,128)S(1)} all-to-all(f32[2,512,128]{2,1,0:T(8,128)S(1)} %bitcast.38), channel_id=1, replica_groups=mesh['x'=4,'z'=16,'y'=8,'core'=2] {'core'}, dimensions={0} | all-to-all | bytes 1048576 | tf_op jit(solution)/shard_map/all_to_all | solution.py:18
  157.1 0.7 reduce_sum.58
  157.8 3.4 %all-to-all-start.5 = ((f32[8,64,128]{2,1,0:T(8,128)}), f32[8,64,128]{2,1,0:T(8,128)S(1)}, u32[]{:S(2)}, u32[]{:S(2)}) async-start(f32[8,64,128]{2,1,0:T(8,128)} %bitcast.13), calls=%async_computation.5 | async-start | bytes 524288 | tf_op jit(solution)/shard_map/all_to_all | solution.py:18
  161.2 1.9 all-gather.3.folded_ref
  163.1 2.3 shard_map.79
  165.4 8.1 %all-to-all-done.5 = f32[8,64,128]{2,1,0:T(8,128)S(1)} async-done(((f32[8,64,128]{2,1,0:T(8,128)}), f32[8,64,128]{2,1,0:T(8,128)S(1)}, u32[]{:S(2)}, u32[]{:S(2)}) %all-to-all-start.5) | async-done | bytes 262176 | tf_op jit(solution)/shard_map/all_to_all | solution.py:18
  173.5 0.2 broadcast_multiply_fusion
  173.7 23.8 %all-gather.4 = f32[1024,128]{1,0:T(8,128)S(1)} all-gather(f32[64,128]{1,0:T(8,128)S(1)} %get-tuple-element.20), channel_id=6, replica_groups=mesh['x'=4,'z'=16,'y'=8,'core'=2] {'z'}, dimensions={0}, use_global_device_ids=true | all-gather | bytes 557056 | tf_op jit(solution)/shard_map/all_gather | solution.py:166
  197.5 1.4 broadcast_in_dim.25
  198.9 4.4 %all-to-all-start.6 = ((f32[4,1024,128]{2,1,0:T(8,128)}), f32[4,1024,128]{2,1,0:T(8,128)}, u32[]{:S(2)}, u32[]{:S(2)}) async-start(f32[4,1024,128]{2,1,0:T(8,128)} %broadcast_in_dim.25), calls=%async_computation.6 | async-start | bytes 4194304 | tf_op jit(solution)/shard_map/all_to_all | solution.py:18
  203.3 0.2 fusion.10.gram_ref
  203.5 23.4 %all-gather.5 = f32[1024,128]{1,0:T(8,128)S(1)} all-gather(f32[64,128]{1,0:T(8,128)S(1)} %get-tuple-element.20), channel_id=7, replica_groups=mesh['x'=4,'z'=16,'y'=8,'core'=2] {'y','core'}, dimensions={0}, use_global_device_ids=true | all-gather | bytes 557056 | tf_op jit(solution)/shard_map/all_gather | solution.py:166
  227.0 0.0 all-to-all-done.6.gathered_ref
  227.0 3.3 %shard_map.80 = f32[64,128]{1,0:T(8,128)S(1)} custom-call(s32[32]{0:T(128)S(1)} %bitcast.44, s32[32]{0:T(128)S(1)} %bitcast.43, s32[1]{0:T(128)} %bitcast.32.count_ref, f32[32,128,128]{2,1,0:T(8,128)S(1)} %bitcast.35, f32[4,1024,128]{2,1,0:T(8,128)} %all-to-all-done.6.gathered_ref, f32[16,64,128]{2,1,0:T(8,128)S(1)} %bitcast.36, f32[64,64]{1,0:T(8,128)S(1)} %fusion.10.gram_ref), custom_call_target="tpu_custom_call" | custom-call | tf_op jit(solution)/shard_map/pallas_call | solution.py:122
  230.3 13.6 %all_to_all.54.chunks_ref = f32[16,4,128]{2,1,0:T(4,128)S(1)} all-to-all(f32[16,4,128]{2,1,0:T(4,128)S(1)} %bitcast.39), channel_id=1, replica_groups=mesh['x'=4,'z'=16,'y'=8,'core'=2] {'y','core'}, dimensions={0} | all-to-all | bytes 65536 | tf_op jit(solution)/shard_map/all_to_all | solution.py:18
  243.9 20.4 %all_to_all.55.chunks_ref = f32[64,4,128]{2,1,0:T(4,128)S(1)} all-to-all(f32[64,4,128]{2,1,0:T(4,128)S(1)} %shard_map.81), channel_id=1, replica_groups=mesh['x'=4,'z'=16,'y'=8,'core'=2] {'x','z'}, dimensions={0} | all-to-all | bytes 262144 | tf_op jit(solution)/shard_map/all_to_all | solution.py:18
  264.3 0.1 shard_map.82
  264.4 12.2 %all_to_all.56 = f32[16,4,128]{2,1,0:T(4,128)S(1)} all-to-all(f32[16,4,128]{2,1,0:T(4,128)S(1)} %shard_map.82), channel_id=1, replica_groups=mesh['x'=4,'z'=16,'y'=8,'core'=2] {'y','core'}, dimensions={0} | all-to-all | bytes 65536 | tf_op jit(solution)/shard_map/all_to_all | solution.py:18
  276.5 3.3 %shard_map.83 = (f32[64,128]{1,0:T(8,128)}, f32[64,64]{1,0:T(8,128)}) custom-call(f32[64,128]{1,0:T(8,128)S(1)} %bitcast.40, f32[64,128]{1,0:T(8,128)S(1)} %get-tuple-element.21.filtered_ref), custom_call_target="tpu_custom_call" | custom-call | tf_op jit(solution)/shard_map/pallas_call | solution.py:122
  (13 shorter events, 0.3 us)
Async XLA Ops:
  42.7 5.3 %copy-start.3 = (f32[128,64]{0,1:T(8,128)S(1)}, f32[128,64]{0,1:T(8,128)}, u32[]{:S(2)}) copy-start(f32[128,64]{0,1:T(8,128)} %param.6) | copy-start | bytes 98308
  42.7 31.0 %copy-start.2 = (s32[1,1,32]{2,1,0:T(1,128)S(1)}, s32[1,1,32]{2,1,0:T(1,128)}, u32[]{:S(2)}) copy-start(s32[1,1,32]{2,1,0:T(1,128)} %param.9) | copy-start | bytes 388
  42.7 31.0 %copy-start = (f32[1,1,32,128,128]{4,3,2,1,0:T(8,128)S(1)}, f32[1,1,32,128,128]{4,3,2,1,0:T(8,128)}, u32[]{:S(2)}) copy-start(f32[1,1,32,128,128]{4,3,2,1,0:T(8,128)} %param.8) | copy-start | bytes 6291460
  42.7 31.1 %copy-start.1 = (s32[1,1,32]{2,1,0:T(1,128)S(1)}, s32[1,1,32]{2,1,0:T(1,128)}, u32[]{:S(2)}) copy-start(s32[1,1,32]{2,1,0:T(1,128)} %param.10) | copy-start | bytes 388
  42.7 31.0 %all-to-all-start = ((f32[4,1024,128]{2,1,0:T(8,128)}), f32[4,1024,128]{2,1,0:T(8,128)}, u32[]{:S(2)}, u32[]{:S(2)}) async-start(f32[4,1024,128]{2,1,0:T(8,128)} %broadcast_in_dim.22), calls=%async_computation | async-start | bytes 4194304 | tf_op jit(solution)/shard_map/all_to_all | solution.py:18
  157.8 15.7 %all-to-all-start.5 = ((f32[8,64,128]{2,1,0:T(8,128)}), f32[8,64,128]{2,1,0:T(8,128)S(1)}, u32[]{:S(2)}, u32[]{:S(2)}) async-start(f32[8,64,128]{2,1,0:T(8,128)} %bitcast.13), calls=%async_computation.5 | async-start | bytes 524288 | tf_op jit(solution)/shard_map/all_to_all | solution.py:18
  198.9 28.1 %all-to-all-start.6 = ((f32[4,1024,128]{2,1,0:T(8,128)}), f32[4,1024,128]{2,1,0:T(8,128)}, u32[]{:S(2)}, u32[]{:S(2)}) async-start(f32[4,1024,128]{2,1,0:T(8,128)} %broadcast_in_dim.25), calls=%async_computation.6 | async-start | bytes 4194304 | tf_op jit(solution)/shard_map/all_to_all | solution.py:18

commit v11 on v10

--- a/solution.py
+++ b/solution.py
@@ -32,26 +32,30 @@
     return lax.dot_general(left, right, CONTRACT_LAST, preferred_element_type=jnp.float32)
 
 
-def add_slots(rows_ref, cols_ref, count_ref, blocks_ref, gathered_ref, sums_ref):
+def add_slots(rows_ref, cols_ref, count_ref, blocks_ref, gathered_ref, sums_ref, core_first=False):
     sums_ref[...] = jnp.zeros_like(sums_ref)
-    count = count_ref[0]
+    half = sums_ref.shape[0] // 2
     width, nodes = sums_ref.shape[1:]
+    count = jnp.broadcast_to(count_ref[...], (width, nodes))
     pieces = gathered_ref.shape[1] // width
     for slot in range(blocks_ref.shape[0]):
-        live = (slot < count).astype(jnp.float32)
+        row = rows_ref[slot]
+        if core_first:
+            row = (row % 2) * half + row // 2
         col = cols_ref[slot]
         first_row = pl.multiple_of((col % pieces) * width, width)
-        vectors = jnp.concatenate(split(gathered_ref[col // pieces, pl.ds(first_row, width)] * live), axis=0)
+        piece = jnp.where(slot < count, gathered_ref[col // pieces, pl.ds(first_row, width)], 0.0)
+        vectors = jnp.concatenate(split(piece), axis=0)
         products = dot_pieces(vectors, jnp.concatenate(split(blocks_ref[slot]), axis=0))
-        sums_ref[rows_ref[slot]] += products[:width, :nodes] + products[width:, :nodes] + products[:width, nodes:]
+        sums_ref[row] += products[:width, :nodes] + products[width:, :nodes] + products[:width, nodes:]
 
 
 def tile_kernel(rows_ref, cols_ref, count_ref, blocks_ref, gathered_ref, out_ref):
-    add_slots(rows_ref, cols_ref, count_ref, blocks_ref, gathered_ref, out_ref)
+    add_slots(rows_ref, cols_ref, count_ref, blocks_ref, gathered_ref, out_ref, core_first=True)
 
 
 def tile_rider_kernel(rows_ref, cols_ref, count_ref, blocks_ref, gathered_ref, out_ref, rider_ref):
-    add_slots(rows_ref, cols_ref, count_ref, blocks_ref, gathered_ref, out_ref)
+    add_slots(rows_ref, cols_ref, count_ref, blocks_ref, gathered_ref, out_ref, core_first=True)
     pieces_end = gathered_ref.shape[1] - rider_ref.shape[0]
     rider_ref[...] = jnp.sum(gathered_ref[:, pieces_end:], axis=0)
 
@@ -122,7 +126,7 @@
     return pl.pallas_call(
         kernel,
         out_shape=[jax.ShapeDtypeStruct(shape, jnp.float32) for shape in outs],
-        in_specs=[SMEM if value.dtype == jnp.int32 and value.ndim == 1 else VMEM for value in ins],
+        in_specs=[SMEM if value.ndim == 1 else VMEM for value in ins],
         out_specs=[VMEM] * len(outs),
         scratch_shapes=list(scratch),
         compiler_params=pltpu.CompilerParams(vmem_limit_bytes=24 * 2**20),
@@ -155,19 +159,25 @@
     tile_blocks = blocks.reshape(blocks.shape[2:])
     rows = block_rows.reshape(-1)
     cols = block_cols.reshape(-1)
-    count = block_counts.reshape(-1)
-
+    tile = (rows, cols, block_counts, tile_blocks)
     y_devices = lax.axis_size("y")
-    tile = (rows, cols, count, tile_blocks)
-    tile_core_first = ((rows % 2) * y_devices + rows // 2, cols, count, tile_blocks)
     sums_shape = (col_devices, width, nodes)
 
     def gather(value, axes):
         return lax.all_gather(value, axes, axis=0, tiled=False)
 
-    def reduce_cols(partial):
-        halves = exchange(partial.reshape(-1, y_devices * width, nodes), "core").sum(0)
-        return exchange(halves.reshape(y_devices, width, nodes), "y").sum(0) * scale
+    def reduce_cols(partial, rider=None):
+        halves = partial.reshape(-1, y_devices * width, nodes)
+        if rider is not None:
+            halves = jnp.concatenate([halves, rider], axis=1)
+        halves = exchange(halves, "core").sum(0)
+        cut = y_devices * width
+        chunks = halves[:cut].reshape(y_devices, width, nodes)
+        if rider is None:
+            return exchange(chunks, "y").sum(0) * scale
+        rest = jnp.broadcast_to(halves[cut:][None], (y_devices, *rider.shape[1:]))
+        done = exchange(jnp.concatenate([chunks, rest], axis=1), "y").sum(0)
+        return done[:width] * scale, done[width:]
 
     def together(*values):
         return lax.optimization_barrier(values)
@@ -178,16 +188,15 @@
     first = start.T
     scale = jnp.sqrt(16.0 / degrees.astype(jnp.float32))[None, :]
     along_z = gather(first * scale, "z").reshape(-1, nodes)
-    rider = gather(fold(gram(first, first)), COL).sum(0).reshape(lax.axis_size("core"), -1, nodes)
+    gathered, ordered = together(to_all(along_z, "x"), first)
+    (partial,) = call_kernel(tile_kernel, (*tile, gathered), [sums_shape])
+    rider = fold(gram(ordered, ordered)).reshape(lax.axis_size("core"), -1, nodes)
     half_shape = rider.shape[1:]
-    rider = lax.dynamic_index_in_dim(rider, lax.axis_index("core"), keepdims=False)
-    gathered, rider = together(to_all(along_z, "x"), rider)
-    (partial,) = call_kernel(tile_kernel, (*tile_core_first, gathered), [sums_shape])
-    once = reduce_cols(partial)
+    once, rider = reduce_cols(partial, rider)
 
     along_z = gather(jnp.concatenate([once * scale, rider], axis=0), "z")
     along_z = jnp.concatenate([along_z[:, :width].reshape(-1, nodes), along_z[:, width:].sum(0)], axis=0)
-    partial, rider = call_kernel(tile_rider_kernel, (*tile_core_first, to_all(along_z, "x")), [sums_shape, half_shape])
+    partial, rider = call_kernel(tile_rider_kernel, (*tile, to_all(along_z, "x")), [sums_shape, half_shape])
     rider = gather(rider, "core").reshape(-1, nodes)
     (inverse,) = call_kernel(functools.partial(inverse_kernel, nodes_all), (rider,), [(width, width)])
     filtered = matmul(inverse, 2.0 * reduce_cols(partial) - first)

time: 281 us -> 283 us (level)
  waiting for transfers between devices: 8.06 us -> 26.2 us
  blocking collectives: 239 us -> 223 us
    all_gather x6 -> x5, blocking collectives: 137 us -> 112 us  [gather(): return lax.all_gather(value, axes, axis=0, tiled=False)]
    all_to_all x3, waiting for transfers between devices: 8.06 us -> 26.2 us  [exchange(): return lax.all_to_all(chunks, axes, 0, 0, tiled=True)]
    all_to_all x7, blocking collectives: 102 us -> 112 us  [exchange(): return lax.all_to_all(chunks, axes, 0, 0, tiled=True)]
  transfers between devices with their start and end apart: 3 -> 3, of which waited for: 1 -> 2; matrix products, arithmetic and copies ran while one was open for 0% -> 0% of each run, Pallas kernels for 1% -> 1%
where the time goes in v11:
time: 283 us; the launch traced here: 282 us
  blocking collectives  223 us (79%)
  waiting for transfers between devices  26.2 us (9%)
  Pallas kernels  12.8 us (5%)
  starting transfers between devices  12.4 us (4%)
  local copies, waits for them, and re-layouts  3.09 us (1%)
    all_to_all x7, blocking collectives, exchange(): return lax.all_to_all(chunks, axes, 0, 0, tiled=True)  112 us
    all_gather x5, blocking collectives, gather(): return lax.all_gather(value, axes, axis=0, tiled=False)  112 us
    all_to_all x3, waiting for transfers between devices, exchange(): return lax.all_to_all(chunks, axes, 0, 0, tiled=True)  26.2 us
    pallas_call x7, Pallas kernels, call_kernel(): pl.pallas_call(kernel, out_shape=[jax.ShapeDtypeStruct(shape, jnp.float32...  12.8 us
    all_to_all x3, starting transfers between devices, exchange(): return lax.all_to_all(chunks, axes, 0, 0, tiled=True)  12.4 us
  transfers between devices with their start and end apart: 3, of which 2 were waited for; matrix products, arithmetic and copies ran while one was open for 0% of the time, Pallas kernels for 1%

profile of v11, /device:TPU:1, one launch (start us, length us, event | category | flops | bytes accessed | tf_op | source)
XLA Modules:
  0.0 282.5 jit_solution(15089493381030951244)
XLA Ops:
  0.6 0.7 divide_sqrt_fusion
  1.3 0.8 broadcast_multiply_fusion.1
  2.1 39.2 %all-gather = f32[1024,128]{1,0:T(8,128)S(1)} all-gather(f32[64,128]{1,0:T(8,128)S(1)} %broadcast_multiply_fusion.1), channel_id=2, replica_groups=mesh['x'=4,'z'=16,'y'=8,'core'=2] {'z'}, dimensions={0}, use_global_device_ids=true | all-gather | bytes 557056 | tf_op jit(solution)/shard_map/all_gather | solution.py:167
  41.3 1.4 broadcast_in_dim.13
  42.7 0.0 copy-start.3
  42.7 0.0 copy-start
  42.7 0.0 copy-start.1
  42.7 0.0 copy-start.2
  42.7 4.6 %all-to-all-start = ((f32[4,1024,128]{2,1,0:T(8,128)}), f32[4,1024,128]{2,1,0:T(8,128)}, u32[]{:S(2)}, u32[]{:S(2)}) async-start(f32[4,1024,128]{2,1,0:T(8,128)} %broadcast_in_dim.13), calls=%async_computation | async-start | bytes 4194304 | tf_op jit(solution)/shard_map/all_to_all | solution.py:18
  47.9 18.2 %all-to-all-done.gathered_ref = f32[4,1024,128]{2,1,0:T(8,128)} async-done(((f32[4,1024,128]{2,1,0:T(8,128)}), f32[4,1024,128]{2,1,0:T(8,128)}, u32[]{:S(2)}, u32[]{:S(2)}) %all-to-all-start) | async-done | bytes 2097184 | tf_op jit(solution)/shard_map/all_to_all | solution.py:18
  66.1 0.0 copy-done.3
  66.1 0.2 fusion.10
  66.3 0.1 pad_maximum_fusion.4
  66.4 0.0 copy-done
  66.4 0.0 copy-done.1
  66.4 0.0 copy-done.2
  66.4 2.4 shard_map.77
  68.8 12.3 %all_to_all.50 = f32[2,528,128]{2,1,0:T(8,128)S(1)} all-to-all(f32[2,528,128]{2,1,0:T(8,128)S(1)} %pad_maximum_fusion), channel_id=1, replica_groups=mesh['x'=4,'z'=16,'y'=8,'core'=2] {'core'}, dimensions={0} | all-to-all | bytes 1081344 | tf_op jit(solution)/shard_map/all_to_all | solution.py:18
  81.3 19.4 %all_to_all.51 = f32[8,80,128]{2,1,0:T(8,128)S(1)} all-to-all(f32[8,80,128]{2,1,0:T(8,128)S(1)} %pad_maximum_fusion.2), channel_id=1, replica_groups=mesh['x'=4,'z'=16,'y'=8,'core'=2] {'y'}, dimensions={0} | all-to-all | bytes 655360 | tf_op jit(solution)/shard_map/all_to_all | solution.py:18
  100.7 23.0 %all-gather.1 = f32[1280,128]{1,0:T(8,128)S(1)} all-gather(f32[80,128]{1,0:T(8,128)S(1)} %pad_maximum_fusion.3), channel_id=3, replica_groups=mesh['x'=4,'z'=16,'y'=8,'core'=2] {'z'}, dimensions={0}, use_global_device_ids=true | all-gather | bytes 696320 | tf_op jit(solution)/shard_map/all_gather | solution.py:167
  123.9 0.1 broadcast_in_dim.30
  124.0 20.4 %all_to_all.52.gathered_ref = f32[4,1040,128]{2,1,0:T(8,128)S(1)} all-to-all(f32[4,1040,128]{2,1,0:T(8,128)S(1)} %broadcast_in_dim.30), channel_id=1, replica_groups=mesh['x'=4,'z'=16,'y'=8,'core'=2] {'x'}, dimensions={0} | all-to-all | bytes 4259840 | tf_op jit(solution)/shard_map/all_to_all | solution.py:18
  144.4 1.3 shard_map.78
  145.7 13.4 %all_to_all.53 = f32[2,512,128]{2,1,0:T(8,128)S(1)} all-to-all(f32[2,512,128]{2,1,0:T(8,128)S(1)} %bitcast.32), channel_id=1, replica_groups=mesh['x'=4,'z'=16,'y'=8,'core'=2] {'core'}, dimensions={0} | all-to-all | bytes 1048576 | tf_op jit(solution)/shard_map/all_to_all | solution.py:18
  159.2 0.7 reduce_sum.48
  159.9 3.4 %all-to-all-start.5 = ((f32[8,64,128]{2,1,0:T(8,128)}), f32[8,64,128]{2,1,0:T(8,128)S(1)}, u32[]{:S(2)}, u32[]{:S(2)}) async-start(f32[8,64,128]{2,1,0:T(8,128)} %bitcast.10), calls=%async_computation.5 | async-start | bytes 524288 | tf_op jit(solution)/shard_map/all_to_all | solution.py:18
  163.3 1.9 all-gather.2.folded_ref
  165.2 2.3 shard_map.79
  167.5 8.1 %all-to-all-done.5 = f32[8,64,128]{2,1,0:T(8,128)S(1)} async-done(((f32[8,64,128]{2,1,0:T(8,128)}), f32[8,64,128]{2,1,0:T(8,128)S(1)}, u32[]{:S(2)}, u32[]{:S(2)}) %all-to-all-start.5) | async-done | bytes 262176 | tf_op jit(solution)/shard_map/all_to_all | solution.py:18
  175.6 0.2 broadcast_multiply_fusion
  175.8 24.2 %all-gather.3 = f32[1024,128]{1,0:T(8,128)S(1)} all-gather(f32[64,128]{1,0:T(8,128)S(1)} %get-tuple-element.20), channel_id=5, replica_groups=mesh['x'=4,'z'=16,'y'=8,'core'=2] {'z'}, dimensions={0}, use_global_device_ids=true | all-gather | bytes 557056 | tf_op jit(solution)/shard_map/all_gather | solution.py:167
  200.0 1.4 broadcast_in_dim.32
  201.4 4.4 %all-to-all-start.6 = ((f32[4,1024,128]{2,1,0:T(8,128)}), f32[4,1024,128]{2,1,0:T(8,128)}, u32[]{:S(2)}, u32[]{:S(2)}) async-start(f32[4,1024,128]{2,1,0:T(8,128)} %broadcast_in_dim.32), calls=%async_computation.6 | async-start | bytes 4194304 | tf_op jit(solution)/shard_map/all_to_all | solution.py:18
  205.8 0.2 fusion.11.gram_ref
  206.0 23.5 %all-gather.4 = f32[1024,128]{1,0:T(8,128)S(1)} all-gather(f32[64,128]{1,0:T(8,128)S(1)} %get-tuple-element.20), channel_id=6, replica_groups=mesh['x'=4,'z'=16,'y'=8,'core'=2] {'y','core'}, dimensions={0}, use_global_device_ids=true | all-gather | bytes 557056 | tf_op jit(solution)/shard_map/all_gather | solution.py:167
  229.5 0.0 all-to-all-done.6.gathered_ref
  229.5 3.3 %shard_map.80 = f32[64,128]{1,0:T(8,128)S(1)} custom-call(s32[32]{0:T(128)S(1)} %bitcast.37, s32[32]{0:T(128)S(1)} %bitcast.40, s32[1,1]{1,0:T(1,128)S(6)} %copy.8.count_ref, f32[32,128,128]{2,1,0:T(8,128)S(1)} %bitcast.29, f32[4,1024,128]{2,1,0:T(8,128)} %all-to-all-done.6.gathered_ref, f32[16,64,128]{2,1,0:T(8,128)S(1)} %bitcast.30, ...), custom_call_target="tpu_custom_call" | custom-call | tf_op jit(solution)/shard_map/pallas_call | solution.py:126
  232.8 13.6 %all_to_all.54.chunks_ref = f32[16,4,128]{2,1,0:T(4,128)S(1)} all-to-all(f32[16,4,128]{2,1,0:T(4,128)S(1)} %bitcast.33), channel_id=1, replica_groups=mesh['x'=4,'z'=16,'y'=8,'core'=2] {'y','core'}, dimensions={0} | all-to-all | bytes 65536 | tf_op jit(solution)/shard_map/all_to_all | solution.py:18
  246.4 20.5 %all_to_all.55.chunks_ref = f32[64,4,128]{2,1,0:T(4,128)S(1)} all-to-all(f32[64,4,128]{2,1,0:T(4,128)S(1)} %shard_map.81), channel_id=1, replica_groups=mesh['x'=4,'z'=16,'y'=8,'core'=2] {'x','z'}, dimensions={0} | all-to-all | bytes 262144 | tf_op jit(solution)/shard_map/all_to_all | solution.py:18
  266.9 0.1 shard_map.82
  267.0 12.2 %all_to_all.56 = f32[16,4,128]{2,1,0:T(4,128)S(1)} all-to-all(f32[16,4,128]{2,1,0:T(4,128)S(1)} %shard_map.82), channel_id=1, replica_groups=mesh['x'=4,'z'=16,'y'=8,'core'=2] {'y','core'}, dimensions={0} | all-to-all | bytes 65536 | tf_op jit(solution)/shard_map/all_to_all | solution.py:18
  279.2 3.3 %shard_map.83 = (f32[64,128]{1,0:T(8,128)}, f32[64,64]{1,0:T(8,128)}) custom-call(f32[64,128]{1,0:T(8,128)S(1)} %bitcast.34, f32[64,128]{1,0:T(8,128)S(1)} %get-tuple-element.21.filtered_ref), custom_call_target="tpu_custom_call" | custom-call | tf_op jit(solution)/shard_map/pallas_call | solution.py:126
  (16 shorter events, 0.3 us)
Async XLA Ops:
  42.7 23.4 %copy-start.3 = (f32[128,64]{0,1:T(8,128)S(1)}, f32[128,64]{0,1:T(8,128)}, u32[]{:S(2)}) copy-start(f32[128,64]{0,1:T(8,128)} %param.6) | copy-start | bytes 98308
  42.7 23.7 %copy-start = (f32[1,1,32,128,128]{4,3,2,1,0:T(8,128)S(1)}, f32[1,1,32,128,128]{4,3,2,1,0:T(8,128)}, u32[]{:S(2)}) copy-start(f32[1,1,32,128,128]{4,3,2,1,0:T(8,128)} %param.8) | copy-start | bytes 6291460
  42.7 23.7 %copy-start.1 = (s32[1,1,32]{2,1,0:T(1,128)S(1)}, s32[1,1,32]{2,1,0:T(1,128)}, u32[]{:S(2)}) copy-start(s32[1,1,32]{2,1,0:T(1,128)} %param.9) | copy-start | bytes 388
  42.7 23.7 %copy-start.2 = (s32[1,1,32]{2,1,0:T(1,128)S(1)}, s32[1,1,32]{2,1,0:T(1,128)}, u32[]{:S(2)}) copy-start(s32[1,1,32]{2,1,0:T(1,128)} %param.10) | copy-start | bytes 388
  42.7 23.4 %all-to-all-start = ((f32[4,1024,128]{2,1,0:T(8,128)}), f32[4,1024,128]{2,1,0:T(8,128)}, u32[]{:S(2)}, u32[]{:S(2)}) async-start(f32[4,1024,128]{2,1,0:T(8,128)} %broadcast_in_dim.13), calls=%async_computation | async-start | bytes 4194304 | tf_op jit(solution)/shard_map/all_to_all | solution.py:18
  159.9 15.7 %all-to-all-start.5 = ((f32[8,64,128]{2,1,0:T(8,128)}), f32[8,64,128]{2,1,0:T(8,128)S(1)}, u32[]{:S(2)}, u32[]{:S(2)}) async-start(f32[8,64,128]{2,1,0:T(8,128)} %bitcast.10), calls=%async_computation.5 | async-start | bytes 524288 | tf_op jit(solution)/shard_map/all_to_all | solution.py:18
  201.4 28.1 %all-to-all-start.6 = ((f32[4,1024,128]{2,1,0:T(8,128)}), f32[4,1024,128]{2,1,0:T(8,128)}, u32[]{:S(2)}, u32[]{:S(2)}) async-start(f32[4,1024,128]{2,1,0:T(8,128)} %broadcast_in_dim.32), calls=%async_computation.6 | async-start | bytes 4194304 | tf_op jit(solution)/shard_map/all_to_all | solution.py:18

commit v12 on v10

--- a/solution.py
+++ b/solution.py
@@ -105,7 +105,7 @@
 
 def finish_kernel(nodes_all, both_ref, filtered_ref, basis_ref, ritz_ref):
     width = filtered_ref.shape[0]
-    both = both_ref[...] / nodes_all
+    both = jnp.sum(both_ref[...], axis=0) / nodes_all
     inverse = inverse_factor(both[:, width:])
     half = jnp.dot(inverse, both[:, :width], precision=HIGHEST, preferred_element_type=jnp.float32)
     ritz_ref[...] = lax.dot_general(
@@ -201,8 +201,10 @@
         [pltpu.VMEM(sums_shape, jnp.float32)],
     )
     projected = exchange(projected.reshape(col_devices, -1, 2 * width), COL)
-    projected = exchange(sum_to(projected, row_devices), ROW)
-    projected = exchange(sum_to(projected, col_devices), COL).reshape(width, 2 * width)
+    projected = exchange(sum_to(projected, lax.axis_size("z")), "z")
+    everywhere = ("x", "y", "core")
+    projected = exchange(sum_to(projected, lax.axis_size(everywhere)), everywhere)
+    projected = projected.reshape(lax.axis_size("x"), width, 2 * width)
     basis, ritz = call_kernel(
         functools.partial(finish_kernel, nodes_all), (projected, filtered), [(width, nodes), (width, width)]
     )

time: 281 us -> 279 us (level)
  no operation moved by 1% of the time
where the time goes in v12:
time: 279 us
  blocking collectives  238 us (85%)
  Pallas kernels  12.7 us (5%)
  starting transfers between devices  12.4 us (4%)
  waiting for transfers between devices  8.06 us (3%)
  local copies, waits for them, and re-layouts  3.07 us (1%)
    all_gather x6, blocking collectives, gather(): return lax.all_gather(value, axes, axis=0, tiled=False)  137 us
    all_to_all x7, blocking collectives, exchange(): return lax.all_to_all(chunks, axes, 0, 0, tiled=True)  101 us
    pallas_call x7, Pallas kernels, call_kernel(): pl.pallas_call(kernel, out_shape=[jax.ShapeDtypeStruct(shape, jnp.float32...  12.7 us
    all_to_all x3, starting transfers between devices, exchange(): return lax.all_to_all(chunks, axes, 0, 0, tiled=True)  12.4 us
    all_to_all x3, waiting for transfers between devices, exchange(): return lax.all_to_all(chunks, axes, 0, 0, tiled=True)  8.06 us
  transfers between devices with their start and end apart: 3, of which 1 were waited for; matrix products, arithmetic and copies ran while one was open for 0% of the time, Pallas kernels for 1%

profile of v12, /device:TPU:1, one launch (start us, length us, event | category | flops | bytes accessed | tf_op | source)
XLA Modules:
  0.0 278.6 jit_solution(10060688635176986539)
XLA Ops:
  0.6 0.7 divide_sqrt_fusion
  1.3 0.8 bitcast_multiply_fusion
  2.1 39.2 %all-gather = f32[1024,128]{1,0:T(8,128)S(1)} all-gather(f32[64,128]{1,0:T(8,128)S(1)} %bitcast_multiply_fusion), channel_id=2, replica_groups=mesh['x'=4,'z'=16,'y'=8,'core'=2] {'z'}, dimensions={0}, use_global_device_ids=true | all-gather | bytes 557056 | tf_op jit(solution)/shard_map/all_gather | solution.py:166
  41.3 1.4 broadcast_in_dim.22
  42.7 0.0 copy-start.3
  42.7 0.0 copy-start.2
  42.7 0.0 copy-start
  42.7 0.0 copy-start.1
  42.7 4.6 %all-to-all-start = ((f32[4,1024,128]{2,1,0:T(8,128)}), f32[4,1024,128]{2,1,0:T(8,128)}, u32[]{:S(2)}, u32[]{:S(2)}) async-start(f32[4,1024,128]{2,1,0:T(8,128)} %broadcast_in_dim.22), calls=%async_computation | async-start | bytes 4194304 | tf_op jit(solution)/shard_map/all_to_all | solution.py:18
  47.9 0.0 copy-done.3
  48.0 0.2 fusion.9
  48.2 0.1 pad_maximum_fusion.2
  48.2 25.4 %all-gather.1 = f32[512,128]{1,0:T(8,128)S(1)} all-gather(f32[32,128]{1,0:T(8,128)S(1)} %pad_maximum_fusion.2), channel_id=3, replica_groups=mesh['x'=4,'z'=16,'y'=8,'core'=2] {'y','core'}, dimensions={0}, use_global_device_ids=true | all-gather | bytes 278528 | tf_op jit(solution)/shard_map/all_gather | solution.py:166
  73.7 0.0 copy-done.2
  73.7 0.0 all-to-all-done.gathered_ref
  73.7 0.0 copy-done
  73.7 0.0 copy-done.1
  73.8 2.4 shard_map.77
  76.1 4.7 %all_to_all.50 = f32[2,512,128]{2,1,0:T(8,128)S(1)} all-to-all(f32[2,512,128]{2,1,0:T(8,128)S(1)} %bitcast.37), channel_id=1, replica_groups=mesh['x'=4,'z'=16,'y'=8,'core'=2] {'core'}, dimensions={0} | all-to-all | bytes 1048576 | tf_op jit(solution)/shard_map/all_to_all | solution.py:18
  80.8 17.7 %all_to_all.51 = f32[8,64,128]{2,1,0:T(8,128)S(1)} all-to-all(f32[8,64,128]{2,1,0:T(8,128)S(1)} %bitcast.49), channel_id=1, replica_groups=mesh['x'=4,'z'=16,'y'=8,'core'=2] {'y'}, dimensions={0} | all-to-all | bytes 524288 | tf_op jit(solution)/shard_map/all_to_all | solution.py:18
  98.6 23.1 %all-gather.2 = f32[1280,128]{1,0:T(8,128)S(1)} all-gather(f32[80,128]{1,0:T(8,128)S(1)} %pad_maximum_fusion.1), channel_id=4, replica_groups=mesh['x'=4,'z'=16,'y'=8,'core'=2] {'z'}, dimensions={0}, use_global_device_ids=true | all-gather | bytes 696320 | tf_op jit(solution)/shard_map/all_gather | solution.py:166
  121.8 0.1 broadcast_in_dim.23
  121.9 20.3 %all_to_all.52.gathered_ref = f32[4,1040,128]{2,1,0:T(8,128)S(1)} all-to-all(f32[4,1040,128]{2,1,0:T(8,128)S(1)} %broadcast_in_dim.23), channel_id=1, replica_groups=mesh['x'=4,'z'=16,'y'=8,'core'=2] {'x'}, dimensions={0} | all-to-all | bytes 4259840 | tf_op jit(solution)/shard_map/all_to_all | solution.py:18
  142.3 1.3 shard_map.78
  143.6 13.5 %all_to_all.53 = f32[2,512,128]{2,1,0:T(8,128)S(1)} all-to-all(f32[2,512,128]{2,1,0:T(8,128)S(1)} %bitcast.39), channel_id=1, replica_groups=mesh['x'=4,'z'=16,'y'=8,'core'=2] {'core'}, dimensions={0} | all-to-all | bytes 1048576 | tf_op jit(solution)/shard_map/all_to_all | solution.py:18
  157.1 0.7 reduce_sum.58
  157.8 3.4 %all-to-all-start.5 = ((f32[8,64,128]{2,1,0:T(8,128)}), f32[8,64,128]{2,1,0:T(8,128)S(1)}, u32[]{:S(2)}, u32[]{:S(2)}) async-start(f32[8,64,128]{2,1,0:T(8,128)} %bitcast.13), calls=%async_computation.5 | async-start | bytes 524288 | tf_op jit(solution)/shard_map/all_to_all | solution.py:18
  161.2 1.9 all-gather.3.folded_ref
  163.1 2.3 shard_map.79
  165.4 8.1 %all-to-all-done.5 = f32[8,64,128]{2,1,0:T(8,128)S(1)} async-done(((f32[8,64,128]{2,1,0:T(8,128)}), f32[8,64,128]{2,1,0:T(8,128)S(1)}, u32[]{:S(2)}, u32[]{:S(2)}) %all-to-all-start.5) | async-done | bytes 262176 | tf_op jit(solution)/shard_map/all_to_all | solution.py:18
  173.5 0.2 broadcast_multiply_fusion
  173.7 23.8 %all-gather.4 = f32[1024,128]{1,0:T(8,128)S(1)} all-gather(f32[64,128]{1,0:T(8,128)S(1)} %get-tuple-element.20), channel_id=6, replica_groups=mesh['x'=4,'z'=16,'y'=8,'core'=2] {'z'}, dimensions={0}, use_global_device_ids=true | all-gather | bytes 557056 | tf_op jit(solution)/shard_map/all_gather | solution.py:166
  197.5 1.4 broadcast_in_dim.25
  198.9 4.4 %all-to-all-start.6 = ((f32[4,1024,128]{2,1,0:T(8,128)}), f32[4,1024,128]{2,1,0:T(8,128)}, u32[]{:S(2)}, u32[]{:S(2)}) async-start(f32[4,1024,128]{2,1,0:T(8,128)} %broadcast_in_dim.25), calls=%async_computation.6 | async-start | bytes 4194304 | tf_op jit(solution)/shard_map/all_to_all | solution.py:18
  203.3 0.2 fusion.10.gram_ref
  203.5 23.4 %all-gather.5 = f32[1024,128]{1,0:T(8,128)S(1)} all-gather(f32[64,128]{1,0:T(8,128)S(1)} %get-tuple-element.20), channel_id=7, replica_groups=mesh['x'=4,'z'=16,'y'=8,'core'=2] {'y','core'}, dimensions={0}, use_global_device_ids=true | all-gather | bytes 557056 | tf_op jit(solution)/shard_map/all_gather | solution.py:166
  227.0 0.0 all-to-all-done.6.gathered_ref
  227.0 3.3 %shard_map.80 = f32[64,128]{1,0:T(8,128)S(1)} custom-call(s32[32]{0:T(128)S(1)} %bitcast.44, s32[32]{0:T(128)S(1)} %bitcast.43, s32[1]{0:T(128)} %bitcast.32.count_ref, f32[32,128,128]{2,1,0:T(8,128)S(1)} %bitcast.35, f32[4,1024,128]{2,1,0:T(8,128)} %all-to-all-done.6.gathered_ref, f32[16,64,128]{2,1,0:T(8,128)S(1)} %bitcast.36, f32[64,64]{1,0:T(8,128)S(1)} %fusion.10.gram_ref), custom_call_target="tpu_custom_call" | custom-call | tf_op jit(solution)/shard_map/pallas_call | solution.py:122
  230.2 13.6 %all_to_all.54.chunks_ref = f32[16,4,128]{2,1,0:T(4,128)S(1)} all-to-all(f32[16,4,128]{2,1,0:T(4,128)S(1)} %bitcast.40), channel_id=1, replica_groups=mesh['x'=4,'z'=16,'y'=8,'core'=2] {'y','core'}, dimensions={0} | all-to-all | bytes 65536 | tf_op jit(solution)/shard_map/all_to_all | solution.py:18
  243.9 15.9 %all_to_all.55.chunks_ref = f32[16,4,128]{2,1,0:T(4,128)S(1)} all-to-all(f32[16,4,128]{2,1,0:T(4,128)S(1)} %shard_map.81), channel_id=1, replica_groups=mesh['x'=4,'z'=16,'y'=8,'core'=2] {'z'}, dimensions={0} | all-to-all | bytes 65536 | tf_op jit(solution)/shard_map/all_to_all | solution.py:18
  259.8 15.5 %all_to_all.56 = f32[64,4,128]{2,1,0:T(4,128)S(1)} all-to-all(f32[64,4,128]{2,1,0:T(4,128)S(1)} %shard_map.82), channel_id=1, replica_groups=mesh['x'=4,'z'=16,'y'=8,'core'=2] {'x','y','core'}, dimensions={0} | all-to-all | bytes 262144 | tf_op jit(solution)/shard_map/all_to_all | solution.py:18
  275.3 3.3 %shard_map.83 = (f32[64,128]{1,0:T(8,128)}, f32[64,64]{1,0:T(8,128)}) custom-call(f32[4,64,128]{2,1,0:T(8,128)S(1)} %bitcast.38, f32[64,128]{1,0:T(8,128)S(1)} %get-tuple-element.21.filtered_ref), custom_call_target="tpu_custom_call" | custom-call | tf_op jit(solution)/shard_map/pallas_call | solution.py:122
  (14 shorter events, 0.3 us)
Async XLA Ops:
  42.7 5.3 %copy-start.3 = (f32[128,64]{0,1:T(8,128)S(1)}, f32[128,64]{0,1:T(8,128)}, u32[]{:S(2)}) copy-start(f32[128,64]{0,1:T(8,128)} %param.6) | copy-start | bytes 98308
  42.7 31.0 %copy-start.2 = (s32[1,1,32]{2,1,0:T(1,128)S(1)}, s32[1,1,32]{2,1,0:T(1,128)}, u32[]{:S(2)}) copy-start(s32[1,1,32]{2,1,0:T(1,128)} %param.9) | copy-start | bytes 388
  42.7 31.0 %copy-start = (f32[1,1,32,128,128]{4,3,2,1,0:T(8,128)S(1)}, f32[1,1,32,128,128]{4,3,2,1,0:T(8,128)}, u32[]{:S(2)}) copy-start(f32[1,1,32,128,128]{4,3,2,1,0:T(8,128)} %param.8) | copy-start | bytes 6291460
  42.7 31.1 %copy-start.1 = (s32[1,1,32]{2,1,0:T(1,128)S(1)}, s32[1,1,32]{2,1,0:T(1,128)}, u32[]{:S(2)}) copy-start(s32[1,1,32]{2,1,0:T(1,128)} %param.10) | copy-start | bytes 388
  42.7 31.0 %all-to-all-start = ((f32[4,1024,128]{2,1,0:T(8,128)}), f32[4,1024,128]{2,1,0:T(8,128)}, u32[]{:S(2)}, u32[]{:S(2)}) async-start(f32[4,1024,128]{2,1,0:T(8,128)} %broadcast_in_dim.22), calls=%async_computation | async-start | bytes 4194304 | tf_op jit(solution)/shard_map/all_to_all | solution.py:18
  157.8 15.7 %all-to-all-start.5 = ((f32[8,64,128]{2,1,0:T(8,128)}), f32[8,64,128]{2,1,0:T(8,128)S(1)}, u32[]{:S(2)}, u32[]{:S(2)}) async-start(f32[8,64,128]{2,1,0:T(8,128)} %bitcast.13), calls=%async_computation.5 | async-start | bytes 524288 | tf_op jit(solution)/shard_map/all_to_all | solution.py:18
  198.9 28.1 %all-to-all-start.6 = ((f32[4,1024,128]{2,1,0:T(8,128)}), f32[4,1024,128]{2,1,0:T(8,128)}, u32[]{:S(2)}, u32[]{:S(2)}) async-start(f32[4,1024,128]{2,1,0:T(8,128)} %broadcast_in_dim.25), calls=%async_computation.6 | async-start | bytes 4194304 | tf_op jit(solution)/shard_map/all_to_all | solution.py:18

commit v13 on v12

--- a/solution.py
+++ b/solution.py
@@ -74,7 +74,7 @@
     copies_ref[...] = jnp.broadcast_to(jnp.sum(chunks_ref[...], axis=0)[None], copies_ref.shape)
 
 
-def inverse_factor(gram_matrix, pivots=4):
+def inverse_factor(gram_matrix, pivots=8):
     size = gram_matrix.shape[0]
     shape = (size, 2 * size)
     row_of = lax.broadcasted_iota(jnp.int32, shape, 0)

time: 279 us -> 279 us (level)
  no operation moved by 1% of the time
where the time goes in v13:
time: 279 us; the launch traced here: 278 us
  blocking collectives  238 us (85%)
  starting transfers between devices  12.4 us (4%)
  Pallas kernels  11.5 us (4%)
  waiting for transfers between devices  8.64 us (3%)
  local copies, waits for them, and re-layouts  3.07 us (1%)
    all_gather x6, blocking collectives, gather(): return lax.all_gather(value, axes, axis=0, tiled=False)  137 us
    all_to_all x7, blocking collectives, exchange(): return lax.all_to_all(chunks, axes, 0, 0, tiled=True)  101 us
    all_to_all x3, starting transfers between devices, exchange(): return lax.all_to_all(chunks, axes, 0, 0, tiled=True)  12.4 us
    pallas_call x7, Pallas kernels, call_kernel(): pl.pallas_call(kernel, out_shape=[jax.ShapeDtypeStruct(shape, jnp.float32...  11.5 us
    all_to_all x3, waiting for transfers between devices, exchange(): return lax.all_to_all(chunks, axes, 0, 0, tiled=True)  8.64 us
  transfers between devices with their start and end apart: 3, of which 1 were waited for; matrix products, arithmetic and copies ran while one was open for 0% of the time, Pallas kernels for 1%

profile of v13, /device:TPU:1, one launch (start us, length us, event | category | flops | bytes accessed | tf_op | source)
XLA Modules:
  0.0 278.0 jit_solution(4893563955465849044)
XLA Ops:
  0.6 0.7 divide_sqrt_fusion
  1.3 0.8 bitcast_multiply_fusion
  2.1 39.2 %all-gather = f32[1024,128]{1,0:T(8,128)S(1)} all-gather(f32[64,128]{1,0:T(8,128)S(1)} %bitcast_multiply_fusion), channel_id=2, replica_groups=mesh['x'=4,'z'=16,'y'=8,'core'=2] {'z'}, dimensions={0}, use_global_device_ids=true | all-gather | bytes 557056 | tf_op jit(solution)/shard_map/all_gather | solution.py:166
  41.3 1.4 broadcast_in_dim.22
  42.7 0.0 copy-start.3
  42.7 0.0 copy-start.2
  42.7 0.0 copy-start
  42.7 0.0 copy-start.1
  42.7 4.6 %all-to-all-start = ((f32[4,1024,128]{2,1,0:T(8,128)}), f32[4,1024,128]{2,1,0:T(8,128)}, u32[]{:S(2)}, u32[]{:S(2)}) async-start(f32[4,1024,128]{2,1,0:T(8,128)} %broadcast_in_dim.22), calls=%async_computation | async-start | bytes 4194304 | tf_op jit(solution)/shard_map/all_to_all | solution.py:18
  47.9 0.0 copy-done.3
  48.0 0.2 fusion.9
  48.2 0.1 pad_maximum_fusion.2
  48.2 25.4 %all-gather.1 = f32[512,128]{1,0:T(8,128)S(1)} all-gather(f32[32,128]{1,0:T(8,128)S(1)} %pad_maximum_fusion.2), channel_id=3, replica_groups=mesh['x'=4,'z'=16,'y'=8,'core'=2] {'y','core'}, dimensions={0}, use_global_device_ids=true | all-gather | bytes 278528 | tf_op jit(solution)/shard_map/all_gather | solution.py:166
  73.7 0.0 copy-done.2
  73.7 0.0 all-to-all-done.gathered_ref
  73.7 0.0 copy-done
  73.7 0.0 copy-done.1
  73.8 2.4 shard_map.77
  76.1 4.7 %all_to_all.50 = f32[2,512,128]{2,1,0:T(8,128)S(1)} all-to-all(f32[2,512,128]{2,1,0:T(8,128)S(1)} %bitcast.37), channel_id=1, replica_groups=mesh['x'=4,'z'=16,'y'=8,'core'=2] {'core'}, dimensions={0} | all-to-all | bytes 1048576 | tf_op jit(solution)/shard_map/all_to_all | solution.py:18
  80.8 17.7 %all_to_all.51 = f32[8,64,128]{2,1,0:T(8,128)S(1)} all-to-all(f32[8,64,128]{2,1,0:T(8,128)S(1)} %bitcast.49), channel_id=1, replica_groups=mesh['x'=4,'z'=16,'y'=8,'core'=2] {'y'}, dimensions={0} | all-to-all | bytes 524288 | tf_op jit(solution)/shard_map/all_to_all | solution.py:18
  98.6 23.1 %all-gather.2 = f32[1280,128]{1,0:T(8,128)S(1)} all-gather(f32[80,128]{1,0:T(8,128)S(1)} %pad_maximum_fusion.1), channel_id=4, replica_groups=mesh['x'=4,'z'=16,'y'=8,'core'=2] {'z'}, dimensions={0}, use_global_device_ids=true | all-gather | bytes 696320 | tf_op jit(solution)/shard_map/all_gather | solution.py:166
  121.8 0.1 broadcast_in_dim.23
  121.9 20.3 %all_to_all.52.gathered_ref = f32[4,1040,128]{2,1,0:T(8,128)S(1)} all-to-all(f32[4,1040,128]{2,1,0:T(8,128)S(1)} %broadcast_in_dim.23), channel_id=1, replica_groups=mesh['x'=4,'z'=16,'y'=8,'core'=2] {'x'}, dimensions={0} | all-to-all | bytes 4259840 | tf_op jit(solution)/shard_map/all_to_all | solution.py:18
  142.3 1.3 shard_map.78
  143.6 13.5 %all_to_all.53 = f32[2,512,128]{2,1,0:T(8,128)S(1)} all-to-all(f32[2,512,128]{2,1,0:T(8,128)S(1)} %bitcast.39), channel_id=1, replica_groups=mesh['x'=4,'z'=16,'y'=8,'core'=2] {'core'}, dimensions={0} | all-to-all | bytes 1048576 | tf_op jit(solution)/shard_map/all_to_all | solution.py:18
  157.1 0.7 reduce_sum.58
  157.8 3.4 %all-to-all-start.5 = ((f32[8,64,128]{2,1,0:T(8,128)}), f32[8,64,128]{2,1,0:T(8,128)S(1)}, u32[]{:S(2)}, u32[]{:S(2)}) async-start(f32[8,64,128]{2,1,0:T(8,128)} %bitcast.13), calls=%async_computation.5 | async-start | bytes 524288 | tf_op jit(solution)/shard_map/all_to_all | solution.py:18
  161.2 1.9 all-gather.3.folded_ref
  163.1 1.8 shard_map.79
  164.9 8.6 %all-to-all-done.5 = f32[8,64,128]{2,1,0:T(8,128)S(1)} async-done(((f32[8,64,128]{2,1,0:T(8,128)}), f32[8,64,128]{2,1,0:T(8,128)S(1)}, u32[]{:S(2)}, u32[]{:S(2)}) %all-to-all-start.5) | async-done | bytes 262176 | tf_op jit(solution)/shard_map/all_to_all | solution.py:18
  173.5 0.2 broadcast_multiply_fusion
  173.7 23.8 %all-gather.4 = f32[1024,128]{1,0:T(8,128)S(1)} all-gather(f32[64,128]{1,0:T(8,128)S(1)} %get-tuple-element.20), channel_id=6, replica_groups=mesh['x'=4,'z'=16,'y'=8,'core'=2] {'z'}, dimensions={0}, use_global_device_ids=true | all-gather | bytes 557056 | tf_op jit(solution)/shard_map/all_gather | solution.py:166
  197.5 1.4 broadcast_in_dim.25
  198.9 4.4 %all-to-all-start.6 = ((f32[4,1024,128]{2,1,0:T(8,128)}), f32[4,1024,128]{2,1,0:T(8,128)}, u32[]{:S(2)}, u32[]{:S(2)}) async-start(f32[4,1024,128]{2,1,0:T(8,128)} %broadcast_in_dim.25), calls=%async_computation.6 | async-start | bytes 4194304 | tf_op jit(solution)/shard_map/all_to_all | solution.py:18
  203.3 0.2 fusion.10.gram_ref
  203.5 23.4 %all-gather.5 = f32[1024,128]{1,0:T(8,128)S(1)} all-gather(f32[64,128]{1,0:T(8,128)S(1)} %get-tuple-element.20), channel_id=7, replica_groups=mesh['x'=4,'z'=16,'y'=8,'core'=2] {'y','core'}, dimensions={0}, use_global_device_ids=true | all-gather | bytes 557056 | tf_op jit(solution)/shard_map/all_gather | solution.py:166
  227.0 0.0 all-to-all-done.6.gathered_ref
  227.0 3.3 %shard_map.80 = f32[64,128]{1,0:T(8,128)S(1)} custom-call(s32[32]{0:T(128)S(1)} %bitcast.44, s32[32]{0:T(128)S(1)} %bitcast.43, s32[1]{0:T(128)} %bitcast.32.count_ref, f32[32,128,128]{2,1,0:T(8,128)S(1)} %bitcast.35, f32[4,1024,128]{2,1,0:T(8,128)} %all-to-all-done.6.gathered_ref, f32[16,64,128]{2,1,0:T(8,128)S(1)} %bitcast.36, f32[64,64]{1,0:T(8,128)S(1)} %fusion.10.gram_ref), custom_call_target="tpu_custom_call" | custom-call | tf_op jit(solution)/shard_map/pallas_call | solution.py:122
  230.3 13.6 %all_to_all.54.chunks_ref = f32[16,4,128]{2,1,0:T(4,128)S(1)} all-to-all(f32[16,4,128]{2,1,0:T(4,128)S(1)} %bitcast.40), channel_id=1, replica_groups=mesh['x'=4,'z'=16,'y'=8,'core'=2] {'y','core'}, dimensions={0} | all-to-all | bytes 65536 | tf_op jit(solution)/shard_map/all_to_all | solution.py:18
  243.9 15.9 %all_to_all.55.chunks_ref = f32[16,4,128]{2,1,0:T(4,128)S(1)} all-to-all(f32[16,4,128]{2,1,0:T(4,128)S(1)} %shard_map.81), channel_id=1, replica_groups=mesh['x'=4,'z'=16,'y'=8,'core'=2] {'z'}, dimensions={0} | all-to-all | bytes 65536 | tf_op jit(solution)/shard_map/all_to_all | solution.py:18
  259.8 15.5 %all_to_all.56 = f32[64,4,128]{2,1,0:T(4,128)S(1)} all-to-all(f32[64,4,128]{2,1,0:T(4,128)S(1)} %shard_map.82), channel_id=1, replica_groups=mesh['x'=4,'z'=16,'y'=8,'core'=2] {'x','y','core'}, dimensions={0} | all-to-all | bytes 262144 | tf_op jit(solution)/shard_map/all_to_all | solution.py:18
  275.3 2.8 shard_map.83
  (14 shorter events, 0.3 us)
Async XLA Ops:
  42.7 5.3 %copy-start.3 = (f32[128,64]{0,1:T(8,128)S(1)}, f32[128,64]{0,1:T(8,128)}, u32[]{:S(2)}) copy-start(f32[128,64]{0,1:T(8,128)} %param.6) | copy-start | bytes 98308
  42.7 31.0 %copy-start.2 = (s32[1,1,32]{2,1,0:T(1,128)S(1)}, s32[1,1,32]{2,1,0:T(1,128)}, u32[]{:S(2)}) copy-start(s32[1,1,32]{2,1,0:T(1,128)} %param.9) | copy-start | bytes 388
  42.7 31.0 %copy-start = (f32[1,1,32,128,128]{4,3,2,1,0:T(8,128)S(1)}, f32[1,1,32,128,128]{4,3,2,1,0:T(8,128)}, u32[]{:S(2)}) copy-start(f32[1,1,32,128,128]{4,3,2,1,0:T(8,128)} %param.8) | copy-start | bytes 6291460
  42.7 31.1 %copy-start.1 = (s32[1,1,32]{2,1,0:T(1,128)S(1)}, s32[1,1,32]{2,1,0:T(1,128)}, u32[]{:S(2)}) copy-start(s32[1,1,32]{2,1,0:T(1,128)} %param.10) | copy-start | bytes 388
  42.7 31.0 %all-to-all-start = ((f32[4,1024,128]{2,1,0:T(8,128)}), f32[4,1024,128]{2,1,0:T(8,128)}, u32[]{:S(2)}, u32[]{:S(2)}) async-start(f32[4,1024,128]{2,1,0:T(8,128)} %broadcast_in_dim.22), calls=%async_computation | async-start | bytes 4194304 | tf_op jit(solution)/shard_map/all_to_all | solution.py:18
  157.8 15.7 %all-to-all-start.5 = ((f32[8,64,128]{2,1,0:T(8,128)}), f32[8,64,128]{2,1,0:T(8,128)S(1)}, u32[]{:S(2)}, u32[]{:S(2)}) async-start(f32[8,64,128]{2,1,0:T(8,128)} %bitcast.13), calls=%async_computation.5 | async-start | bytes 524288 | tf_op jit(solution)/shard_map/all_to_all | solution.py:18
  198.9 28.1 %all-to-all-start.6 = ((f32[4,1024,128]{2,1,0:T(8,128)}), f32[4,1024,128]{2,1,0:T(8,128)}, u32[]{:S(2)}, u32[]{:S(2)}) async-start(f32[4,1024,128]{2,1,0:T(8,128)} %broadcast_in_dim.25), calls=%async_computation.6 | async-start | bytes 4194304 | tf_op jit(solution)/shard_map/all_to_all | solution.py:18
